TPU v7x, 32 devices: a whole 2x2x4 slice. The times are simulated.
32 devices in a mesh: lx: 2 (over x), ly: 4 (over y, core), col: 4 (over z).
Axes of the slice: x: 2, y: 2, z: 4, core: 2. Of those that a mesh axis runs over, the one named last changes fastest.
Arguments:
- start: float32 [64, 128, 512], P('col', 'lx', 'ly'), may hold values from -360 to 360
- levels: int32 [128, 512], P('lx', 'ly'), may hold values from 0 to 15
Outputs:
- basis: float32 [64, 128, 512], P(None, ('lx', 'col'), 'ly')
All inputs are finite; a program needn't handle non-finite values.
Results may differ from a plain program's by a relative error of at most 0.00014.
Values sent between devices are 32-bit elements; how exact they have to be, the bound alone decides.
No kernel may reach another device: no remote copies, remote signals or barrier semaphores. Data moves between devices by JAX's collectives and lax.ppermute only.
A program may use at most 64 MiB of HBM per device.

v0:
```python
import math

import jax
import jax.numpy as jnp
from jax import lax
from jax.sharding import PartitionSpec as P

center = 2.1
half_width = 3.1
spread_width = 4.0
level_top = 15.0


def with_halo(cells, sides, width):
    for axis, dim in sides:
        count = lax.axis_size(axis)
        head = lax.slice_in_dim(cells, 0, width, axis=dim)
        tail = lax.slice_in_dim(cells, cells.shape[dim] - width, cells.shape[dim], axis=dim)
        cells = jnp.concatenate(
            [
                lax.ppermute(tail, axis, [(i, (i + 1) % count) for i in range(count)]),
                cells,
                lax.ppermute(head, axis, [((i + 1) % count, i) for i in range(count)]),
            ],
            axis=dim,
        )
    return cells


def onsite_of(levels):
    return spread_width * (levels.astype(jnp.float32) / level_top - 0.5)


def hop_padded(padded, onsite, even_sites):
    middle = padded[:, 1:-1, 1:-1]
    above = padded[:, 2:, 1:-1]
    below = padded[:, :-2, 1:-1]
    left_side = padded[:, 1:-1, :-2]
    right_side = padded[:, 1:-1, 2:]
    vertical = jnp.where(even_sites, above, below)
    return ((onsite - center) * middle - (left_side + right_side + vertical)) / half_width


def parity(row_start, col_start, row_count, col_total):
    grid_x = row_start + lax.iota(jnp.int32, row_count)[:, None]
    grid_y = col_start + lax.iota(jnp.int32, col_total)[None, :]
    return (grid_x + grid_y) % 2 == 0


def slab_rim(field):
    return with_halo(field, (("lx", 1), ("ly", 2)), 1)


def shards(start, levels):
    onsite_full = onsite_of(levels)
    block_x, block_y = levels.shape
    even_sites = parity(
        lax.axis_index("lx") * block_x, lax.axis_index("ly") * block_y, block_x, block_y
    )
    first_term = hop_padded(slab_rim(start), onsite_full, even_sites)
    filtered = 2.0 * hop_padded(slab_rim(first_term), onsite_full, even_sites) - start
    relayed = lax.all_to_all(filtered, "col", split_axis=1, concat_axis=0, tiled=True)
    flat_rows = relayed.reshape(relayed.shape[0], -1)
    local_gram = jnp.dot(
        flat_rows, flat_rows.T, precision=lax.Precision.HIGHEST, preferred_element_type=jnp.float32
    )
    total_gram = lax.psum(local_gram, ("lx", "ly", "col"))
    upper_tri = jnp.linalg.cholesky(total_gram).T
    solved = lax.linalg.triangular_solve(upper_tri.T, flat_rows, left_side=True, lower=True)
    norm_scale = math.sqrt(block_x * lax.axis_size("lx") * block_y * lax.axis_size("ly"))
    return (solved * norm_scale).reshape(relayed.shape)


def solution(mesh):
    placed = (P("col", "lx", "ly"), P("lx", "ly"))
    return jax.shard_map(
        shards, mesh=mesh, in_specs=placed, out_specs=P(None, ("lx", "col"), "ly"), check_vma=False
    )
```

profile of v0, /device:TPU:0, one launch (start us, length us, event | category | flops | bytes accessed | tf_op | source)
XLA Modules:
  0.0 111.5 jit_solution(12218081111393330996)
XLA Ops:
  0.0 0.9 fusion.23
  0.9 3.0 %collective-permute-start = (f32[16,1,128]{2,0,1:T(8,128)S(1)}, f32[16,1,128]{2,0,1:T(8,128)S(1)}, u32[]{:S(2)}, u32[]{:S(2)}) collective-permute-start(f32[16,1,128]{2,0,1:T(8,128)S(1)} %bitcast.27), channel_id=1, source_target_pairs={{0,16},{16,0},{1,17},{17,1},{2,18},{18,2},{3,19},{19,3},{4,20},{20... | collective-permute-start | bytes 24584 | tf_op jit(solution)/shard_map/ppermute | solution.py:21
  4.0 1.5 %copy.22 = f32[16,64,128]{1,0,2:T(8,128)S(1)} copy(f32[16,64,128]{2,1,0:T(8,128)} %param.2) | data formatting | bytes 1048576 | tf_op args[0]
  5.6 0.5 copy.25
  6.1 1.4 %collective-permute-done.1 = f32[16,1,128]{2,0,1:T(8,128)S(1)} collective-permute-done((f32[16,1,128]{2,0,1:T(8,128)S(1)}, f32[16,1,128]{2,0,1:T(8,128)S(1)}, u32[]{:S(2)}, u32[]{:S(2)}) %collective-permute-start.1) | collective-permute-done | bytes 8224 | tf_op jit(solution)/shard_map/ppermute | solution.py:23
  7.6 0.5 copy.27
  8.2 0.9 copy-done
  9.1 1.7 %collective-permute-start.3 = (f32[16,66,1]{1,0,2:T(8,128)S(1)}, f32[16,66,1]{1,0,2:T(8,128)S(1)}, u32[]{:S(2)}, u32[]{:S(2)}) collective-permute-start(f32[16,66,1]{1,0,2:T(8,128)S(1)} %get-tuple-element.10), channel_id=1, source_target_pairs={{4,0},{8,4},{12,8},{0,12},{5,1},{9,5},{13,9},{1,13},{6,2},{10,6},{... | collective-permute-start | bytes 12680 | tf_op jit(solution)/shard_map/ppermute | solution.py:23
  11.1 1.1 %collective-permute-done.2 = f32[16,66,1]{1,0,2:T(8,128)S(1)} collective-permute-done((f32[16,66,1]{1,0,2:T(8,128)S(1)}, f32[16,66,1]{1,0,2:T(8,128)S(1)}, u32[]{:S(2)}, u32[]{:S(2)}) %collective-permute-start.2) | collective-permute-done | bytes 4256 | tf_op jit(solution)/shard_map/ppermute | solution.py:21
  12.2 5.1 %broadcast_multiply_fusion = (f32[16,64,128]{1,0,2:T(8,128)S(1)}, f32[16,64,128]{1,0,2:T(8,128)}) fusion(f32[16,64,128]{1,0,2:T(8,128)S(1)} %copy.22, f32[16,1,128]{1,0,2:T(8,128)S(1)} %copy.25, f32[16,1,128]{1,0,2:T(8,128)} %copy-done, pred[64,128]{0,1:T(8,128)(4,1)S(1)} %fusion.16, f32[16,66,1]{1,0,2:T(8,128)S(1)} %collective-permute-done.3, ...), kind=kLoop, calls=%fused_computation.31 | loop fusion | flops 1835008 | bytes 1638656 | tf_op jit(solution)/shard_map/div | solution.py:41
  17.3 1.4 %fusion.22 = (f32[16,1,128]{1,0,2:T(8,128)S(1)}, f32[16,1,128]{1,0,2:T(8,128)}) fusion(f32[16,64,128]{1,0,2:T(8,128)S(1)} %get-tuple-element.5), kind=kLoop, calls=%fused_computation.60 | loop fusion | bytes 32768 | tf_op jit(solution)/shard_map/slice | solution.py:17
  18.7 1.6 %copy.33 = f32[16,1,128]{2,0,1:T(8,128)S(1)} copy(f32[16,1,128]{1,0,2:T(8,128)} %get-tuple-element.12) | data formatting | bytes 16384 | tf_op jit(solution)/shard_map/slice | solution.py:18
  20.3 0.6 collective-permute-start.4
  21.4 1.5 %collective-permute-start.5 = (f32[16,1,128]{2,0,1:T(8,128)S(1)}, f32[16,1,128]{2,0,1:T(8,128)S(1)}, u32[]{:S(2)}, u32[]{:S(2)}) collective-permute-start(f32[16,1,128]{2,0,1:T(8,128)S(1)} %copy.34), channel_id=1, source_target_pairs={{16,0},{0,16},{17,1},{1,17},{18,2},{2,18},{19,3},{3,19},{20,4},{4,... | collective-permute-start | bytes 24584 | tf_op jit(solution)/shard_map/ppermute | solution.py:23
  22.9 1.2 %collective-permute-done.4 = f32[16,1,128]{2,0,1:T(8,128)S(1)} collective-permute-done((f32[16,1,128]{2,0,1:T(8,128)S(1)}, f32[16,1,128]{2,0,1:T(8,128)S(1)}, u32[]{:S(2)}, u32[]{:S(2)}) %collective-permute-start.4) | collective-permute-done | bytes 8224 | tf_op jit(solution)/shard_map/ppermute | solution.py:21
  24.0 0.5 copy.35
  24.6 0.5 collective-permute-done.5
  25.0 1.5 %copy.36 = f32[16,1,128]{1,0,2:T(8,128)} copy(f32[16,1,128]{2,0,1:T(8,128)S(1)} %collective-permute-done.5) | data formatting | bytes 16384 | tf_op jit(solution)/shard_map/ppermute | solution.py:23
  26.5 0.8 pad_maximum_fusion.18
  27.5 1.6 %collective-permute-start.7 = (f32[16,66,1]{1,0,2:T(8,128)S(1)}, f32[16,66,1]{1,0,2:T(8,128)S(1)}, u32[]{:S(2)}, u32[]{:S(2)}) collective-permute-start(f32[16,66,1]{1,0,2:T(8,128)S(1)} %get-tuple-element.8), channel_id=1, source_target_pairs={{4,0},{8,4},{12,8},{0,12},{5,1},{9,5},{13,9},{1,13},{6,2},{10,6},{... | collective-permute-start | bytes 12680 | tf_op jit(solution)/shard_map/ppermute | solution.py:23
  29.1 1.2 %collective-permute-done.6 = f32[16,66,1]{1,0,2:T(8,128)S(1)} collective-permute-done((f32[16,66,1]{1,0,2:T(8,128)S(1)}, f32[16,66,1]{1,0,2:T(8,128)S(1)}, u32[]{:S(2)}, u32[]{:S(2)}) %collective-permute-start.6) | collective-permute-done | bytes 4256 | tf_op jit(solution)/shard_map/ppermute | solution.py:21
  30.4 5.4 %fusion.5 = f32[16,64,128]{1,0,2:T(8,128)} fusion(f32[16,64,128]{1,0,2:T(8,128)S(1)} %copy.22, f32[16,64,128]{1,0,2:T(8,128)S(1)} %get-tuple-element.5, f32[16,1,128]{1,0,2:T(8,128)S(1)} %copy.35, f32[16,1,128]{1,0,2:T(8,128)} %copy.36, f32[16,66,1]{1,0,2:T(8,128)S(1)} %collective-permute-done.7, f32[16,66,1]{1,0,2:T(8,128)S(1)} %collective-permute-done.6, ...), kind=kLoop, calls=%fused_computation.7 | loop fusion | flops 1966080 | bytes 2162944 | tf_op jit(solution)/shard_map/sub | solution.py:61
  35.8 1.7 %copy.40 = f32[16,64,128]{2,0,1:T(8,128)S(1)} copy(f32[16,64,128]{1,0,2:T(8,128)} %fusion.5) | data formatting | bytes 1048576 | tf_op jit(solution)/shard_map/sub | solution.py:61
  37.6 20.3 %all_to_all.15 = f32[16,64,128]{2,0,1:T(8,128)S(1)} all-to-all(f32[16,64,128]{2,0,1:T(8,128)S(1)} %copy.40), channel_id=1, replica_groups=mesh['lx'=2,'ly'=4,'col'=4] {'col'}, dimensions={1} | all-to-all | bytes 1048576 | tf_op jit(solution)/shard_map/all_to_all | solution.py:62
  58.0 0.7 fusion.12
  58.8 38.8 %psum.7 = f32[64,64]{0,1:T(8,128)S(1)} all-reduce(f32[64,64]{0,1:T(8,128)S(1)} %fusion.12), channel_id=1, replica_groups=mesh['lx'=2,'ly'=4,'col'=4] {'lx','ly','col'}, use_global_device_ids=true, to_apply=%region_0.1 | all-reduce | flops 4096 | bytes 32768 | tf_op jit(solution)/shard_map/psum | solution.py:67
  97.7 5.8 %cholesky.16 = f32[64,64]{1,0:T(8,128)S(1)} custom-call(f32[64,64]{1,0:T(8,128)S(1)} %fusion.20), custom_call_target="Cholesky" | custom-call | tf_op jit(solution)/shard_map/jit(cholesky)/cholesky | solution.py:68
  103.6 0.6 compare_reduce_fusion
  104.2 0.7 fusion.18
  104.9 4.9 %custom-call.6 = f32[1,64,64]{1,2,0:T(8,128)S(1)} custom-call(f32[1,64,64]{2,1,0:T(8,128)S(1)} %fusion.18), custom_call_target="InvertDiagBlocksLowerTriangular" | custom-call | tf_op jit(solution)/shard_map/triangular_solve | solution.py:69
  109.8 0.7 fusion
  110.6 0.9 copy.48
  (21 shorter events, 1.4 us)
Async XLA Ops:
  0.0 4.0 %copy-start.1 = (s32[64,128]{1,0:T(8,128)S(1)}, s32[64,128]{1,0:T(8,128)}, u32[]{:S(2)}) copy-start(s32[64,128]{1,0:T(8,128)} %param.3) | copy-start | bytes 98308
  0.9 4.7 %collective-permute-start = (f32[16,1,128]{2,0,1:T(8,128)S(1)}, f32[16,1,128]{2,0,1:T(8,128)S(1)}, u32[]{:S(2)}, u32[]{:S(2)}) collective-permute-start(f32[16,1,128]{2,0,1:T(8,128)S(1)} %bitcast.27), channel_id=1, source_target_pairs={{0,16},{16,0},{1,17},{17,1},{2,18},{18,2},{3,19},{19,3},{4,20},{20... | collective-permute-start | bytes 24584 | tf_op jit(solution)/shard_map/ppermute | solution.py:21
  3.9 3.7 %collective-permute-start.1 = (f32[16,1,128]{2,0,1:T(8,128)S(1)}, f32[16,1,128]{2,0,1:T(8,128)S(1)}, u32[]{:S(2)}, u32[]{:S(2)}) collective-permute-start(f32[16,1,128]{2,0,1:T(8,128)S(1)} %bitcast.26), channel_id=1, source_target_pairs={{16,0},{0,16},{17,1},{1,17},{18,2},{2,18},{19,3},{3,19},{20,4},{4,... | collective-permute-start | bytes 24584 | tf_op jit(solution)/shard_map/ppermute | solution.py:23
  8.1 1.0 copy-start
  9.1 3.1 %collective-permute-start.2 = (f32[16,66,1]{1,0,2:T(8,128)S(1)}, f32[16,66,1]{1,0,2:T(8,128)S(1)}, u32[]{:S(2)}, u32[]{:S(2)}) collective-permute-start(f32[16,66,1]{1,0,2:T(8,128)S(1)} %get-tuple-element.9), channel_id=1, source_target_pairs={{0,4},{4,8},{8,12},{12,0},{1,5},{5,9},{9,13},{13,1},{2,6},{6,10},{... | collective-permute-start | bytes 12680 | tf_op jit(solution)/shard_map/ppermute | solution.py:21
  9.1 3.1 %collective-permute-start.3 = (f32[16,66,1]{1,0,2:T(8,128)S(1)}, f32[16,66,1]{1,0,2:T(8,128)S(1)}, u32[]{:S(2)}, u32[]{:S(2)}) collective-permute-start(f32[16,66,1]{1,0,2:T(8,128)S(1)} %get-tuple-element.10), channel_id=1, source_target_pairs={{4,0},{8,4},{12,8},{0,12},{5,1},{9,5},{13,9},{1,13},{6,2},{10,6},{... | collective-permute-start | bytes 12680 | tf_op jit(solution)/shard_map/ppermute | solution.py:23
  20.3 3.7 %collective-permute-start.4 = (f32[16,1,128]{2,0,1:T(8,128)S(1)}, f32[16,1,128]{2,0,1:T(8,128)S(1)}, u32[]{:S(2)}, u32[]{:S(2)}) collective-permute-start(f32[16,1,128]{2,0,1:T(8,128)S(1)} %copy.33), channel_id=1, source_target_pairs={{0,16},{16,0},{1,17},{17,1},{2,18},{18,2},{3,19},{19,3},{4,20},{20... | collective-permute-start | bytes 24584 | tf_op jit(solution)/shard_map/ppermute | solution.py:21
  21.4 3.7 %collective-permute-start.5 = (f32[16,1,128]{2,0,1:T(8,128)S(1)}, f32[16,1,128]{2,0,1:T(8,128)S(1)}, u32[]{:S(2)}, u32[]{:S(2)}) collective-permute-start(f32[16,1,128]{2,0,1:T(8,128)S(1)} %copy.34), channel_id=1, source_target_pairs={{16,0},{0,16},{17,1},{1,17},{18,2},{2,18},{19,3},{3,19},{20,4},{4,... | collective-permute-start | bytes 24584 | tf_op jit(solution)/shard_map/ppermute | solution.py:23
  27.3 3.1 %collective-permute-start.6 = (f32[16,66,1]{1,0,2:T(8,128)S(1)}, f32[16,66,1]{1,0,2:T(8,128)S(1)}, u32[]{:S(2)}, u32[]{:S(2)}) collective-permute-start(f32[16,66,1]{1,0,2:T(8,128)S(1)} %get-tuple-element.7), channel_id=1, source_target_pairs={{0,4},{4,8},{8,12},{12,0},{1,5},{5,9},{9,13},{13,1},{2,6},{6,10},{... | collective-permute-start | bytes 12680 | tf_op jit(solution)/shard_map/ppermute | solution.py:21
  27.5 2.9 %collective-permute-start.7 = (f32[16,66,1]{1,0,2:T(8,128)S(1)}, f32[16,66,1]{1,0,2:T(8,128)S(1)}, u32[]{:S(2)}, u32[]{:S(2)}) collective-permute-start(f32[16,66,1]{1,0,2:T(8,128)S(1)} %get-tuple-element.8), channel_id=1, source_target_pairs={{4,0},{8,4},{12,8},{0,12},{5,1},{9,5},{13,9},{1,13},{6,2},{10,6},{... | collective-permute-start | bytes 12680 | tf_op jit(solution)/shard_map/ppermute | solution.py:23
where the time goes:
time: 112 us; the launch traced here: 111 us
  blocking collectives  59.1 us (53%)
  other arithmetic  23.6 us (21%)
  local copies, waits for them, and re-layouts  12.9 us (12%)
  starting transfers between devices  8.65 us (8%)
  waiting for transfers between devices  5.52 us (5%)
  matrix products  1.5 us (1%)
    psum x1, blocking collectives, shards(): total_gram = lax.psum(local_gram, ('lx', 'ly', 'col'))  38.8 us
    all_to_all x1, blocking collectives, shards(): lax.all_to_all(filtered, 'col', split_axis=1, concat_axis=0, tiled=True)  20.3 us
    another operation x3, other arithmetic, shards(): upper_tri = jnp.linalg.cholesky(total_gram).T  6.52 us
    another operation x2, other arithmetic, shards(): lax.linalg.triangular_solve(upper_tri.T, flat_rows, left_side=True, lower...  5.55 us
    sub x1, other arithmetic, shards(): 2.0 * hop_padded(slab_rim(first_term), onsite_full, even_sites) - start  5.4 us
    div x1, other arithmetic, hop_padded(): ((onsite - center) * middle - (left_side + right_side + vertical)) / half...  5.11 us
    ppermute x4, starting transfers between devices, with_halo(): lax.ppermute(head, axis, [((i + 1) % count, i) for i in range(count)])  4.9 us
    ppermute x4, starting transfers between devices, with_halo(): lax.ppermute(tail, axis, [(i, (i + 1) % count) for i in range(count)])  3.74 us
  transfers between devices with their start and end apart: 8, of which 5 were waited for; matrix products, arithmetic and copies ran while one was open for 3% of the time, Pallas kernels for 0%

commit v1 on v0

v1 whole, which is shorter than its diff:
```python
import functools
import math

import jax
import jax.numpy as jnp
from jax import lax
from jax.experimental import pallas as pl
from jax.experimental.pallas import tpu as pltpu
from jax.sharding import PartitionSpec as P

center = 2.1
half_width = 3.1
spread_width = 4.0
level_top = 15.0
lanes = 128
tile = 8
per_pack = lanes // 4


def iota(shape, dim):
    return lax.broadcasted_iota(jnp.int32, shape, dim)


def site_factor(levels):
    onsite = spread_width * (levels / level_top - 0.5)
    return (onsite - center) / half_width


def packing(rows, chunks):
    order = [0, rows - 1] + list(range(1, rows - 1))
    return [(row, chunk) for row in order for chunk in range(chunks)]


def pack_kernel(cols, rows, start_ref, levels_ref, edges_ref, outer_ref):
    chunks = cols // tile
    lane = iota((tile, lanes), 1)
    slots = packing(rows, chunks)
    groups = len(slots) // per_pack

    def tile_of(row, chunk):
        return start_ref[pl.ds(chunk * tile * rows + row, tile, stride=rows), :]

    for group in range(groups):
        packed = jnp.zeros((tile, lanes), jnp.float32)
        for k in range(per_pack):
            row, chunk = slots[group * per_pack + k]
            moved = pltpu.roll(tile_of(row, chunk), (4 * k + 2) % lanes, 1)
            packed = jnp.where(lane // 4 == k, moved, packed)
        edges_ref[group] = packed
    packed = jnp.zeros((tile, lanes), jnp.float32)
    for k in range(rows // tile):
        moved = pltpu.roll(levels_ref[k * tile : (k + 1) * tile, :].astype(jnp.float32), 4 * k + 2, 1)
        packed = jnp.where(lane // 4 == k, moved, packed)
    edges_ref[groups] = packed
    for chunk in range(chunks):
        outer_ref[chunk] = tile_of(0, chunk)
        outer_ref[chunks + chunk] = tile_of(rows - 1, chunk)
    first = levels_ref[0:1, :].astype(jnp.float32)
    last = levels_ref[rows - 1 : rows, :].astype(jnp.float32)
    outer_ref[2 * chunks] = jnp.where(iota((tile, lanes), 0) == 0, first, last)


def filter_kernel(
    cols, rows, parts, start_ref, levels_ref, edges_ref, before_ref, after_ref, *rest
):
    out_refs = rest[:parts]
    field, edge, once, once_edge, done, factor, factor_edge = rest[parts:]
    chunks = cols // tile
    slots = packing(rows, chunks)
    groups = len(slots) // per_pack
    lane = iota((cols, lanes), 1)
    first_lane, last_lane = lane == 0, lane == lanes - 1
    even_lane = lane % 2 == 0
    inverse = 1.0 / half_width

    factor[0:rows, :] = site_factor(levels_ref[...].astype(jnp.float32))
    factor[rows : rows + 1, :] = site_factor(before_ref[2 * chunks, 1:2, :])
    factor[rows + 1 : rows + 2, :] = site_factor(after_ref[2 * chunks, 0:1, :])
    packed = edges_ref[groups]
    for k in range(rows // tile):
        factor_edge[k * tile : (k + 1) * tile, :] = site_factor(
            pltpu.roll(packed, lanes - (4 * k + 2), 1)
        )
    for row in range(rows):
        field[row + 1] = start_ref[pl.ds(row, cols, stride=rows), :]
    for chunk in range(chunks):
        part = pl.ds(chunk * tile, tile)
        field[0, part, :] = before_ref[chunks + chunk]
        field[rows + 1, part, :] = after_ref[chunk]
        edge[0, part, :] = pltpu.roll(
            before_ref[2 * chunks + 1], lanes - (4 * (chunks + chunk) + 2), 1
        )
        edge[rows + 1, part, :] = pltpu.roll(
            after_ref[2 * chunks + 1], lanes - (4 * chunk + 2), 1
        )
    for slot, (row, chunk) in enumerate(slots):
        edge[row + 1, pl.ds(chunk * tile, tile), :] = pltpu.roll(
            edges_ref[slot // per_pack], lanes - (4 * (slot % per_pack) + 2), 1
        )

    def sides(main, other):
        return pltpu.roll(jnp.where(last_lane, other, main), 1, 1) + pltpu.roll(
            jnp.where(first_lane, other, main), lanes - 1, 1
        )

    def factor_at(ref, row):
        return jnp.broadcast_to(ref[row : row + 1, :], (cols, lanes))

    for row in range(-1, rows + 1):
        here, beside = field[row + 1], edge[row + 1]
        even = even_lane if row % 2 == 0 else jnp.logical_not(even_lane)
        if row == -1:
            vertical, where = field[1], rows
        elif row == rows:
            vertical, where = field[rows], rows + 1
        else:
            vertical, where = jnp.where(even, field[row + 2], field[row]), row
        once[row + 1] = factor_at(factor, where) * here - inverse * (
            sides(here, beside) + vertical
        )
        if 0 <= row < rows:
            vertical = jnp.where(even, edge[row + 2], edge[row])
            once_edge[row] = factor_at(factor_edge, row) * beside - inverse * (
                sides(beside, here) + vertical
            )
    for row in range(rows):
        here = once[row + 1]
        even = even_lane if row % 2 == 0 else jnp.logical_not(even_lane)
        vertical = jnp.where(even, once[row + 2], once[row])
        twice = factor_at(factor, row) * here - inverse * (
            sides(here, once_edge[row]) + vertical
        )
        done[row] = 2.0 * twice - field[row + 1]
    place = lax.axis_index("col")
    part_rows = rows // parts
    for k in range(parts):
        out_refs[k][...] = done[pl.ds((place ^ k) * part_rows, part_rows)]


def split(values):
    high = values.astype(jnp.bfloat16)
    rest = values - high.astype(jnp.float32)
    middle = rest.astype(jnp.bfloat16)
    low = (rest - middle.astype(jnp.float32)).astype(jnp.bfloat16)
    return high, middle, low


def gram_kernel(cols, parts, *refs):
    piece_refs, (whole_ref, gram_ref) = refs[:parts], refs[parts:]
    part_rows = whole_ref.shape[0]
    total = cols * parts
    place = lax.axis_index("col")
    for k in range(parts):
        whole_ref[:, pl.ds(pl.multiple_of((place ^ k) * cols, tile), cols), :] = piece_refs[k][...]
    products = jnp.zeros((3 * total, 3 * total), jnp.float32)
    for row in range(0, part_rows, 2):
        values = jnp.concatenate([whole_ref[row], whole_ref[row + 1]], axis=1)
        stack = jnp.concatenate(split(values), axis=0)
        products += lax.dot_general(
            stack, stack, (((1,), (1,)), ((), ())), preferred_element_type=jnp.float32
        )
    gram = jnp.zeros((total, total), jnp.float32)
    for i in reversed(range(3)):
        for j in reversed(range(3)):
            gram += products[i * total : (i + 1) * total, j * total : (j + 1) * total]
    half = total // 2
    gram_ref[...] = jnp.concatenate([gram[:half], gram[half:]], axis=1)


def solve_kernel(scale, whole_ref, gram_ref, other_ref, out_ref):
    part_rows, total, _ = whole_ref.shape
    blocks = total // tile
    half = total // 2
    packed = gram_ref[...] + other_ref[...]
    lane = iota((tile, lanes), 1)
    sub = iota((tile, lanes), 0)
    shape = (tile, lanes)
    work = []
    for i in range(blocks):
        at = i * tile % half
        block = packed[at : at + tile, :]
        if i * tile >= half:
            block = pltpu.roll(block, total, 1)
        unit = jnp.where(lane - total == sub + i * tile, 1.0, 0.0)
        work.append(jnp.where(lane < total, block, unit))
    for b in range(blocks):
        column = {
            i: [
                jnp.broadcast_to(work[i][:, b * tile + m : b * tile + m + 1], shape)
                for m in range(tile)
            ]
            for i in range(b, blocks)
        }
        for m in range(tile):
            pivot = jnp.broadcast_to(column[b][m][m : m + 1, :], shape)
            root = lax.rsqrt(pivot)
            root = root * (1.5 - 0.5 * (pivot * root) * root)
            row = jnp.broadcast_to(work[b][m : m + 1, :], shape) * root
            heads = [
                jnp.broadcast_to(column[b][p][m : m + 1, :], shape) * root
                for p in range(m + 1, tile)
            ]
            for i in range(b, blocks):
                ratio = column[i][m] * root
                if i == b:
                    ratio = jnp.where(sub > m, ratio, 0.0)
                    work[i] = jnp.where(sub == m, row, work[i] - ratio * row)
                else:
                    work[i] = work[i] - ratio * row
                for p in range(m + 1, tile):
                    column[i][p] = column[i][p] - ratio * heads[p - m - 1]
    solver = jnp.concatenate(work, axis=0) * scale
    wide = iota((total, lanes), 1)
    high, middle, low = (piece.astype(jnp.float32) for piece in split(solver))

    def pair(left, right):
        return jnp.where(wide < total, pltpu.roll(left, total, 1), right).astype(jnp.bfloat16)

    left_main = jnp.concatenate([pair(high, high), pair(middle, middle)], axis=1)
    left_rest = pair(high, low)
    for row in range(0, part_rows, 2):
        values = jnp.concatenate([whole_ref[row], whole_ref[row + 1]], axis=1)
        f_high, f_middle, f_low = split(values)
        right_main = jnp.concatenate([f_high, f_middle, f_high, f_middle], axis=0)
        right_rest = jnp.concatenate([f_low, f_high], axis=0)
        result = jnp.dot(left_rest, right_rest, preferred_element_type=jnp.float32) + jnp.dot(
            left_main, right_main, preferred_element_type=jnp.float32
        )
        out_ref[pl.ds(row, total, stride=part_rows), :] = result[:, :lanes]
        out_ref[pl.ds(row + 1, total, stride=part_rows), :] = result[:, lanes:]


def call(kernel, outs, *operands, scratch=()):
    return pl.pallas_call(
        kernel,
        out_shape=[jax.ShapeDtypeStruct(shape, jnp.float32) for shape in outs],
        scratch_shapes=[pltpu.VMEM(shape, jnp.float32) for shape in scratch],
        compiler_params=pltpu.CompilerParams(vmem_limit_bytes=32 * 1024 * 1024),
    )(*operands)


def exchange(values, axis, distance):
    count = lax.axis_size(axis)
    return lax.ppermute(values, axis, [(i, i ^ distance) for i in range(count)])


def shards(start, levels):
    cols, rows, _ = start.shape
    parts = lax.axis_size("col")
    chunks = cols // tile
    groups = rows * chunks // per_pack
    total = cols * parts
    part_rows = rows // parts
    flat = start.reshape(cols * rows, lanes)
    edges, outer = call(
        functools.partial(pack_kernel, cols, rows),
        [(groups + 1, tile, lanes), (2 * chunks + 1, tile, lanes)],
        flat,
        levels,
    )
    count = lax.axis_size("ly")
    near = exchange(edges, "ly", 1)
    far_pairs = [(i, (i + 1) % count if i % 2 else (i - 1) % count) for i in range(count)]
    far = lax.ppermute(edges, "ly", far_pairs)
    even_place = lax.axis_index("ly") % 2 == 0
    from_left = lax.broadcasted_iota(jnp.int32, edges.shape, 2) % 4 < 2
    beside = jnp.where(from_left == even_place, far, near)
    outer = jnp.concatenate([outer, beside[:1]], axis=0)
    count = lax.axis_size("lx")
    before = lax.ppermute(outer, "lx", [(i, (i + 1) % count) for i in range(count)])
    after = before
    if count > 2:
        after = lax.ppermute(outer, "lx", [((i + 1) % count, i) for i in range(count)])
    pieces = call(
        functools.partial(filter_kernel, cols, rows, parts),
        [(part_rows, cols, lanes)] * parts,
        flat,
        levels,
        beside,
        before,
        after,
        scratch=[
            (rows + 2, cols, lanes),
            (rows + 2, cols, lanes),
            (rows + 2, cols, lanes),
            (rows, cols, lanes),
            (rows, cols, lanes),
            (rows + tile, lanes),
            (rows, lanes),
        ],
    )
    arrived = {0: pieces[0]}
    for k in sorted(range(1, parts), key=lambda k: -(k & -k) if k != parts - 1 else 0):
        arrived[k] = exchange(pieces[k], "col", k)
    whole, gram = call(
        functools.partial(gram_kernel, cols, parts),
        [(part_rows, total, lanes), (total // 2, 2 * total)],
        *(arrived[k] for k in range(parts)),
    )
    steps = []
    for axis in ("ly", "lx", "col"):
        bit = 1
        while bit < lax.axis_size(axis):
            steps.append((axis, bit))
            bit *= 2
    for axis, bit in steps[:-1]:
        gram = gram + exchange(gram, axis, bit)
    scale = math.sqrt(rows * lax.axis_size("lx") * lanes * lax.axis_size("ly"))
    (basis,) = call(
        functools.partial(solve_kernel, scale),
        [(total * part_rows, lanes)],
        whole,
        gram,
        exchange(gram, *steps[-1]),
    )
    return basis.reshape(total, part_rows, lanes)


def solution(mesh):
    placed = (P("col", "lx", "ly"), P("lx", "ly"))
    return jax.shard_map(
        shards, mesh=mesh, in_specs=placed, out_specs=P(None, ("lx", "col"), "ly"), check_vma=False
    )
```

time: 112 us -> 47.5 us (0.42)
  blocking collectives: 59.1 us -> 0 us
  other arithmetic: 23.6 us -> 0.04 us
  waiting for transfers between devices: 5.52 us -> 22.5 us
  local copies, waits for them, and re-layouts: 12.9 us -> 1.81 us
  starting transfers between devices: 8.65 us -> 17.3 us
  Pallas kernels: 0 us -> 5.58 us
  matrix products: 1.5 us -> 0 us
    psum x1 -> x0, blocking collectives: 38.8 us -> none  [shards(): total_gram = lax.psum(local_gram, ('lx', 'ly', 'col'))]
    all_to_all x1 -> x0, blocking collectives: 20.3 us -> none  [shards(): lax.all_to_all(filtered, 'col', split_axis=1, concat_axis=0, tiled=True)]
    ppermute x8 -> x11, waiting for transfers between devices: 5.52 us -> 22.5 us  [the longest x9 18.9 us: exchange(): return lax.ppermute(values, axis, [(i, i ^ distance) for i in range(count)])]
    another operation x5 -> x0, other arithmetic: 12.1 us -> none  [the longest x3 6.52 us: shards(): upper_tri = jnp.linalg.cholesky(total_gram).T]
    ppermute x8 -> x11, starting transfers between devices: 8.65 us -> 17.3 us  [the longest x9 13 us: exchange(): return lax.ppermute(values, axis, [(i, i ^ distance) for i in range(count)])]
    pallas_call x0 -> x4, Pallas kernels: none -> 5.58 us  [call(): pl.pallas_call(kernel, out_shape=[jax.ShapeDtypeStruct(shape, jnp.float32...]
    sub x1 -> x0, other arithmetic: 5.4 us -> none  [shards(): 2.0 * hop_padded(slab_rim(first_term), onsite_full, even_sites) - start]
    div x2 -> x0, other arithmetic: 5.12 us -> none  [the longest x1 5.11 us: hop_padded(): ((onsite - center) * middle - (left_side + right_side + vertical)) / half...]
  transfers between devices with their start and end apart: 8 -> 11, of which waited for: 5 -> 9; matrix products, arithmetic and copies ran while one was open for 3% -> 0% of each run, Pallas kernels for 0% -> 0%
where the time goes in v1:
time: 47.5 us; the launch traced here: 47.3 us
  waiting for transfers between devices  22.5 us (47%)
  starting transfers between devices  17.3 us (36%)
  Pallas kernels  5.58 us (12%)
  local copies, waits for them, and re-layouts  1.81 us (4%)
    ppermute x9, waiting for transfers between devices, exchange(): return lax.ppermute(values, axis, [(i, i ^ distance) for i in range(count)])  18.9 us
    ppermute x9, starting transfers between devices, exchange(): return lax.ppermute(values, axis, [(i, i ^ distance) for i in range(count)])  13 us
    pallas_call x4, Pallas kernels, call(): pl.pallas_call(kernel, out_shape=[jax.ShapeDtypeStruct(shape, jnp.float32...  5.58 us
    ppermute x1, starting transfers between devices, shards(): far = lax.ppermute(edges, 'ly', far_pairs)  2.64 us
    ppermute x1, waiting for transfers between devices, shards(): lax.ppermute(outer, 'lx', [(i, (i + 1) % count) for i in range(count)])  2.17 us
    unnamed x8, local copies, waits for them, and re-layouts  1.81 us
    ppermute x1, starting transfers between devices, shards(): lax.ppermute(outer, 'lx', [(i, (i + 1) % count) for i in range(count)])  1.72 us
    ppermute x1, waiting for transfers between devices, shards(): far = lax.ppermute(edges, 'ly', far_pairs)  1.47 us
  transfers between devices with their start and end apart: 11, of which 9 were waited for; matrix products, arithmetic and copies ran while one was open for 0% of the time, Pallas kernels for 0%

profile of v1, /device:TPU:0, one launch (start us, length us, event | category | flops | bytes accessed | tf_op | source)
XLA Modules:
  0.0 47.3 jit_solution(7091327374107542380)
XLA Ops:
  0.0 0.0 copy-start
  0.0 1.0 %copy-done = f32[16,64,128]{2,1,0:T(8,128)S(1)} copy-done((f32[16,64,128]{2,1,0:T(8,128)S(1)}, f32[16,64,128]{2,1,0:T(8,128)}, u32[]{:S(2)}) %copy-start) | copy-done | bytes 524312
  1.0 0.0 copy-start.2
  1.0 0.8 %copy-done.2 = s32[64,128]{1,0:T(8,128)S(1)} copy-done((s32[64,128]{1,0:T(8,128)S(1)}, s32[64,128]{1,0:T(8,128)}, u32[]{:S(2)}) %copy-start.2) | copy-done | bytes 32792
  1.8 0.4 shard_map.28
  2.2 0.5 %collective-permute-start.1 = (f32[5,8,128]{2,1,0:T(8,128)S(1)}, f32[5,8,128]{2,1,0:T(8,128)S(1)}, u32[]{:S(2)}, u32[]{:S(2)}) collective-permute-start(f32[5,8,128]{2,1,0:T(8,128)S(1)} %get-tuple-element.13), channel_id=1, source_target_pairs={{0,4},{4,0},{8,12},{12,8},{1,5},{5,1},{9,13},{13,9},{2,6},{6,2},{1... | collective-permute-start | bytes 61448 | tf_op jit(solution)/shard_map/ppermute | solution.py:244
  2.7 2.6 %collective-permute-start = (f32[5,8,128]{2,1,0:T(8,128)S(1)}, f32[5,8,128]{2,1,0:T(8,128)S(1)}, u32[]{:S(2)}, u32[]{:S(2)}) collective-permute-start(f32[5,8,128]{2,1,0:T(8,128)S(1)} %get-tuple-element.13), channel_id=1, source_target_pairs={{0,12},{4,8},{8,4},{12,0},{1,13},{5,9},{9,5},{13,1},{2,14},{6,10},... | collective-permute-start | bytes 61448 | tf_op jit(solution)/shard_map/ppermute | solution.py:264
  5.3 0.0 collective-permute-done.1
  5.3 1.5 %collective-permute-done = f32[5,8,128]{2,1,0:T(8,128)S(1)} collective-permute-done((f32[5,8,128]{2,1,0:T(8,128)S(1)}, f32[5,8,128]{2,1,0:T(8,128)S(1)}, u32[]{:S(2)}, u32[]{:S(2)}) %collective-permute-start) | collective-permute-done | bytes 20512 | tf_op jit(solution)/shard_map/ppermute | solution.py:264
  6.9 1.7 %collective-permute-start.2 = (f32[6,8,128]{2,1,0:T(8,128)S(1)}, f32[6,8,128]{2,1,0:T(8,128)S(1)}, u32[]{:S(2)}, u32[]{:S(2)}) collective-permute-start(f32[6,8,128]{2,1,0:T(8,128)S(1)} %pad_maximum_fusion), channel_id=1, source_target_pairs={{0,16},{16,0},{1,17},{17,1},{2,18},{18,2},{3,19},{19,3},{4,20},{20... | collective-permute-start | bytes 73736 | tf_op jit(solution)/shard_map/ppermute | solution.py:270
  8.6 2.2 %collective-permute-done.2.before_ref.after_ref = f32[6,8,128]{2,1,0:T(8,128)S(1)} collective-permute-done((f32[6,8,128]{2,1,0:T(8,128)S(1)}, f32[6,8,128]{2,1,0:T(8,128)S(1)}, u32[]{:S(2)}, u32[]{:S(2)}) %collective-permute-start.2) | collective-permute-done | bytes 24608 | tf_op jit(solution)/shard_map/ppermute | solution.py:270
  10.7 0.0 copy-done.1
  10.8 0.0 copy-done.3
  10.8 1.1 %shard_map.29 = (f32[16,16,128]{2,1,0:T(8,128)S(1)}, f32[16,16,128]{2,1,0:T(8,128)S(1)}, f32[16,16,128]{2,1,0:T(8,128)S(1)}, f32[16,16,128]{2,1,0:T(8,128)S(1)}) custom-call(f32[1024,128]{1,0:T(8,128)S(1)} %bitcast.3, s32[64,128]{1,0:T(8,128)S(1)} %copy-done.3, f32[5,8,128]{2,1,0:T(8,128)S(1)} %fusion.1.edges_ref, ...), custom_call_target="tpu_custom_call" | custom-call | tf_op jit(solution)/shard_map/pallas_call | solution.py:234
  11.9 1.8 %collective-permute-start.3 = (f32[16,16,128]{2,1,0:T(8,128)S(1)}, f32[16,16,128]{2,1,0:T(8,128)S(1)}, u32[]{:S(2)}, u32[]{:S(2)}) collective-permute-start(f32[16,16,128]{2,1,0:T(8,128)S(1)} %get-tuple-element.16), channel_id=1, source_target_pairs={{0,1},{1,0},{2,3},{3,2},{4,5},{5,4},{6,7},{7,6},{8,9},{9,8},{10,11... | collective-permute-start | bytes 393224 | tf_op jit(solution)/shard_map/ppermute | solution.py:244
  13.7 2.6 %collective-permute-start.4 = (f32[16,16,128]{2,1,0:T(8,128)S(1)}, f32[16,16,128]{2,1,0:T(8,128)S(1)}, u32[]{:S(2)}, u32[]{:S(2)}) collective-permute-start(f32[16,16,128]{2,1,0:T(8,128)S(1)} %get-tuple-element.17), channel_id=1, source_target_pairs={{0,2},{1,3},{2,0},{3,1},{4,6},{5,7},{6,4},{7,5},{8,10},{9,11},{10,... | collective-permute-start | bytes 393224 | tf_op jit(solution)/shard_map/ppermute | solution.py:244
  16.3 0.0 collective-permute-start.5
  16.3 2.0 %collective-permute-done.3.refs_1_ = f32[16,16,128]{2,1,0:T(8,128)S(1)} collective-permute-done((f32[16,16,128]{2,1,0:T(8,128)S(1)}, f32[16,16,128]{2,1,0:T(8,128)S(1)}, u32[]{:S(2)}, u32[]{:S(2)}) %collective-permute-start.3) | collective-permute-done | bytes 131104 | tf_op jit(solution)/shard_map/ppermute | solution.py:244
  18.3 7.7 %collective-permute-done.4.refs_2_ = f32[16,16,128]{2,1,0:T(8,128)S(1)} collective-permute-done((f32[16,16,128]{2,1,0:T(8,128)S(1)}, f32[16,16,128]{2,1,0:T(8,128)S(1)}, u32[]{:S(2)}, u32[]{:S(2)}) %collective-permute-start.4) | collective-permute-done | bytes 131104 | tf_op jit(solution)/shard_map/ppermute | solution.py:244
  26.0 0.0 collective-permute-done.5.refs_3_
  26.0 0.6 %shard_map.30 = (f32[16,64,128]{2,1,0:T(8,128)S(1)}, f32[32,128]{1,0:T(8,128)S(1)}) custom-call(f32[16,16,128]{2,1,0:T(8,128)S(1)} %get-tuple-element.15.refs_0_, f32[16,16,128]{2,1,0:T(8,128)S(1)} %collective-permute-done.3.refs_1_, f32[16,16,128]{2,1,0:T(8,128)S(1)} %collective-permute-done.4.refs_2_, f32[16,16,128]{2,1,0:T(8,128)S(1)} %collective-permute-done.5.refs_3_), custom_call_target="tpu_custom_call" | custom-call | tf_op jit(solution)/shard_map/pallas_call | solution.py:234
  26.6 0.0 collective-permute-start.6
  26.7 1.2 %collective-permute-done.6 = f32[32,128]{1,0:T(8,128)S(1)} collective-permute-done((f32[32,128]{1,0:T(8,128)S(1)}, f32[32,128]{1,0:T(8,128)S(1)}, u32[]{:S(2)}, u32[]{:S(2)}) %collective-permute-start.6) | collective-permute-done | bytes 16416 | tf_op jit(solution)/shard_map/ppermute | solution.py:244
  27.8 1.5 %collective-permute-start.7 = (f32[32,128]{1,0:T(8,128)S(1)}, f32[32,128]{1,0:T(8,128)S(1)}, u32[]{:S(2)}, u32[]{:S(2)}) collective-permute-start(f32[32,128]{1,0:T(8,128)S(1)} %add.25), channel_id=1, source_target_pairs={{0,8},{4,12},{8,0},{12,4},{1,9},{5,13},{9,1},{13,5},{2,10},{6,14},... | collective-permute-start | bytes 49160 | tf_op jit(solution)/shard_map/ppermute | solution.py:244
  29.4 2.2 %collective-permute-done.7 = f32[32,128]{1,0:T(8,128)S(1)} collective-permute-done((f32[32,128]{1,0:T(8,128)S(1)}, f32[32,128]{1,0:T(8,128)S(1)}, u32[]{:S(2)}, u32[]{:S(2)}) %collective-permute-start.7) | collective-permute-done | bytes 16416 | tf_op jit(solution)/shard_map/ppermute | solution.py:244
  31.6 1.5 %collective-permute-start.8 = (f32[32,128]{1,0:T(8,128)S(1)}, f32[32,128]{1,0:T(8,128)S(1)}, u32[]{:S(2)}, u32[]{:S(2)}) collective-permute-start(f32[32,128]{1,0:T(8,128)S(1)} %add.26), channel_id=1, source_target_pairs={{0,16},{16,0},{1,17},{17,1},{2,18},{18,2},{3,19},{19,3},{4,20},{20... | collective-permute-start | bytes 49160 | tf_op jit(solution)/shard_map/ppermute | solution.py:244
  33.1 2.2 %collective-permute-done.8 = f32[32,128]{1,0:T(8,128)S(1)} collective-permute-done((f32[32,128]{1,0:T(8,128)S(1)}, f32[32,128]{1,0:T(8,128)S(1)}, u32[]{:S(2)}, u32[]{:S(2)}) %collective-permute-start.8) | collective-permute-done | bytes 16416 | tf_op jit(solution)/shard_map/ppermute | solution.py:244
  35.3 2.0 %collective-permute-start.9 = (f32[32,128]{1,0:T(8,128)S(1)}, f32[32,128]{1,0:T(8,128)S(1)}, u32[]{:S(2)}, u32[]{:S(2)}) collective-permute-start(f32[32,128]{1,0:T(8,128)S(1)} %add.27), channel_id=1, source_target_pairs={{0,1},{1,0},{2,3},{3,2},{4,5},{5,4},{6,7},{7,6},{8,9},{9,8},{10,11... | collective-permute-start | bytes 49160 | tf_op jit(solution)/shard_map/ppermute | solution.py:244
  37.3 1.8 %collective-permute-done.9 = f32[32,128]{1,0:T(8,128)S(1)} collective-permute-done((f32[32,128]{1,0:T(8,128)S(1)}, f32[32,128]{1,0:T(8,128)S(1)}, u32[]{:S(2)}, u32[]{:S(2)}) %collective-permute-start.9) | collective-permute-done | bytes 16416 | tf_op jit(solution)/shard_map/ppermute | solution.py:244
  39.1 3.0 %collective-permute-start.10 = (f32[32,128]{1,0:T(8,128)S(1)}, f32[32,128]{1,0:T(8,128)S(1)}, u32[]{:S(2)}, u32[]{:S(2)}) collective-permute-start(f32[32,128]{1,0:T(8,128)S(1)} %add.28.gram_ref), channel_id=1, source_target_pairs={{0,2},{1,3},{2,0},{3,1},{4,6},{5,7},{6,4},{7,5},{8,10},{9,11},{10,... | collective-permute-start | bytes 49160 | tf_op jit(solution)/shard_map/ppermute | solution.py:244
  42.0 1.7 %collective-permute-done.10.other_ref = f32[32,128]{1,0:T(8,128)S(1)} collective-permute-done((f32[32,128]{1,0:T(8,128)S(1)}, f32[32,128]{1,0:T(8,128)S(1)}, u32[]{:S(2)}, u32[]{:S(2)}) %collective-permute-start.10) | collective-permute-done | bytes 16416 | tf_op jit(solution)/shard_map/ppermute | solution.py:244
  43.8 3.5 %shard_map.31 = f32[1024,128]{1,0:T(8,128)} custom-call(f32[16,64,128]{2,1,0:T(8,128)S(1)} %get-tuple-element.19.whole_ref, f32[32,128]{1,0:T(8,128)S(1)} %add.28.gram_ref, f32[32,128]{1,0:T(8,128)S(1)} %collective-permute-done.10.other_ref), custom_call_target="tpu_custom_call" | custom-call | tf_op jit(solution)/shard_map/pallas_call | solution.py:234
  (11 shorter events, 0.0 us)
Async XLA Ops:
  0.0 1.0 %copy-start = (f32[16,64,128]{2,1,0:T(8,128)S(1)}, f32[16,64,128]{2,1,0:T(8,128)}, u32[]{:S(2)}) copy-start(f32[16,64,128]{2,1,0:T(8,128)} %param.2) | copy-start | bytes 1572868
  1.0 0.8 %copy-start.2 = (s32[64,128]{1,0:T(8,128)S(1)}, s32[64,128]{1,0:T(8,128)}, u32[]{:S(2)}) copy-start(s32[64,128]{1,0:T(8,128)} %levels_ref.3) | copy-start | bytes 98308
  1.8 8.9 %copy-start.1 = (f32[16,64,128]{2,1,0:T(8,128)S(1)}, f32[16,64,128]{2,1,0:T(8,128)}, u32[]{:S(2)}) copy-start(f32[16,64,128]{2,1,0:T(8,128)} %param.2) | copy-start | bytes 1572868
  2.2 3.2 %collective-permute-start.1 = (f32[5,8,128]{2,1,0:T(8,128)S(1)}, f32[5,8,128]{2,1,0:T(8,128)S(1)}, u32[]{:S(2)}, u32[]{:S(2)}) collective-permute-start(f32[5,8,128]{2,1,0:T(8,128)S(1)} %get-tuple-element.13), channel_id=1, source_target_pairs={{0,4},{4,0},{8,12},{12,8},{1,5},{5,1},{9,13},{13,9},{2,6},{6,2},{1... | collective-permute-start | bytes 61448 | tf_op jit(solution)/shard_map/ppermute | solution.py:244
  2.7 4.1 %collective-permute-start = (f32[5,8,128]{2,1,0:T(8,128)S(1)}, f32[5,8,128]{2,1,0:T(8,128)S(1)}, u32[]{:S(2)}, u32[]{:S(2)}) collective-permute-start(f32[5,8,128]{2,1,0:T(8,128)S(1)} %get-tuple-element.13), channel_id=1, source_target_pairs={{0,12},{4,8},{8,4},{12,0},{1,13},{5,9},{9,5},{13,1},{2,14},{6,10},... | collective-permute-start | bytes 61448 | tf_op jit(solution)/shard_map/ppermute | solution.py:264
  6.8 3.9 %copy-start.3 = (s32[64,128]{1,0:T(8,128)S(1)}, s32[64,128]{1,0:T(8,128)}, u32[]{:S(2)}) copy-start(s32[64,128]{1,0:T(8,128)} %levels_ref.3) | copy-start | bytes 98308
  6.9 3.9 %collective-permute-start.2 = (f32[6,8,128]{2,1,0:T(8,128)S(1)}, f32[6,8,128]{2,1,0:T(8,128)S(1)}, u32[]{:S(2)}, u32[]{:S(2)}) collective-permute-start(f32[6,8,128]{2,1,0:T(8,128)S(1)} %pad_maximum_fusion), channel_id=1, source_target_pairs={{0,16},{16,0},{1,17},{17,1},{2,18},{18,2},{3,19},{19,3},{4,20},{20... | collective-permute-start | bytes 73736 | tf_op jit(solution)/shard_map/ppermute | solution.py:270
  11.9 6.4 %collective-permute-start.3 = (f32[16,16,128]{2,1,0:T(8,128)S(1)}, f32[16,16,128]{2,1,0:T(8,128)S(1)}, u32[]{:S(2)}, u32[]{:S(2)}) collective-permute-start(f32[16,16,128]{2,1,0:T(8,128)S(1)} %get-tuple-element.16), channel_id=1, source_target_pairs={{0,1},{1,0},{2,3},{3,2},{4,5},{5,4},{6,7},{7,6},{8,9},{9,8},{10,11... | collective-permute-start | bytes 393224 | tf_op jit(solution)/shard_map/ppermute | solution.py:244
  13.7 12.4 %collective-permute-start.4 = (f32[16,16,128]{2,1,0:T(8,128)S(1)}, f32[16,16,128]{2,1,0:T(8,128)S(1)}, u32[]{:S(2)}, u32[]{:S(2)}) collective-permute-start(f32[16,16,128]{2,1,0:T(8,128)S(1)} %get-tuple-element.17), channel_id=1, source_target_pairs={{0,2},{1,3},{2,0},{3,1},{4,6},{5,7},{6,4},{7,5},{8,10},{9,11},{10,... | collective-permute-start | bytes 393224 | tf_op jit(solution)/shard_map/ppermute | solution.py:244
  16.3 9.8 %collective-permute-start.5 = (f32[16,16,128]{2,1,0:T(8,128)S(1)}, f32[16,16,128]{2,1,0:T(8,128)S(1)}, u32[]{:S(2)}, u32[]{:S(2)}) collective-permute-start(f32[16,16,128]{2,1,0:T(8,128)S(1)} %get-tuple-element.18), channel_id=1, source_target_pairs={{0,3},{1,2},{2,1},{3,0},{4,7},{5,6},{6,5},{7,4},{8,11},{9,10},{10,... | collective-permute-start | bytes 393224 | tf_op jit(solution)/shard_map/ppermute | solution.py:244
  26.6 1.2 %collective-permute-start.6 = (f32[32,128]{1,0:T(8,128)S(1)}, f32[32,128]{1,0:T(8,128)S(1)}, u32[]{:S(2)}, u32[]{:S(2)}) collective-permute-start(f32[32,128]{1,0:T(8,128)S(1)} %get-tuple-element.20), channel_id=1, source_target_pairs={{0,4},{4,0},{8,12},{12,8},{1,5},{5,1},{9,13},{13,9},{2,6},{6,2},{1... | collective-permute-start | bytes 49160 | tf_op jit(solution)/shard_map/ppermute | solution.py:244
  27.8 3.7 %collective-permute-start.7 = (f32[32,128]{1,0:T(8,128)S(1)}, f32[32,128]{1,0:T(8,128)S(1)}, u32[]{:S(2)}, u32[]{:S(2)}) collective-permute-start(f32[32,128]{1,0:T(8,128)S(1)} %add.25), channel_id=1, source_target_pairs={{0,8},{4,12},{8,0},{12,4},{1,9},{5,13},{9,1},{13,5},{2,10},{6,14},... | collective-permute-start | bytes 49160 | tf_op jit(solution)/shard_map/ppermute | solution.py:244
  31.6 3.7 %collective-permute-start.8 = (f32[32,128]{1,0:T(8,128)S(1)}, f32[32,128]{1,0:T(8,128)S(1)}, u32[]{:S(2)}, u32[]{:S(2)}) collective-permute-start(f32[32,128]{1,0:T(8,128)S(1)} %add.26), channel_id=1, source_target_pairs={{0,16},{16,0},{1,17},{17,1},{2,18},{18,2},{3,19},{19,3},{4,20},{20... | collective-permute-start | bytes 49160 | tf_op jit(solution)/shard_map/ppermute | solution.py:244
  35.3 3.7 %collective-permute-start.9 = (f32[32,128]{1,0:T(8,128)S(1)}, f32[32,128]{1,0:T(8,128)S(1)}, u32[]{:S(2)}, u32[]{:S(2)}) collective-permute-start(f32[32,128]{1,0:T(8,128)S(1)} %add.27), channel_id=1, source_target_pairs={{0,1},{1,0},{2,3},{3,2},{4,5},{5,4},{6,7},{7,6},{8,9},{9,8},{10,11... | collective-permute-start | bytes 49160 | tf_op jit(solution)/shard_map/ppermute | solution.py:244
  39.1 4.7 %collective-permute-start.10 = (f32[32,128]{1,0:T(8,128)S(1)}, f32[32,128]{1,0:T(8,128)S(1)}, u32[]{:S(2)}, u32[]{:S(2)}) collective-permute-start(f32[32,128]{1,0:T(8,128)S(1)} %add.28.gram_ref), channel_id=1, source_target_pairs={{0,2},{1,3},{2,0},{3,1},{4,6},{5,7},{6,4},{7,5},{8,10},{9,11},{10,... | collective-permute-start | bytes 49160 | tf_op jit(solution)/shard_map/ppermute | solution.py:244

commit v2 on v1

v2 whole, which is shorter than its diff:
```python
import functools
import math

import jax
import jax.numpy as jnp
from jax import lax
from jax.experimental import pallas as pl
from jax.experimental.pallas import tpu as pltpu
from jax.sharding import PartitionSpec as P

center = 2.1
half_width = 3.1
spread_width = 4.0
level_top = 15.0
lanes = 128
tile = 8


def iota(shape, dim):
    return lax.broadcasted_iota(jnp.int32, shape, dim)


def site_factor(levels):
    onsite = spread_width * (levels / level_top - 0.5)
    return (onsite - center) / half_width


def tile_at(ref, rows, row, chunk):
    return ref[pl.ds(chunk * tile * rows + row, tile, stride=rows), :]


def pack_edges(tiles):
    lane = iota((tile, lanes), 1)
    packed = jnp.zeros((tile, lanes), jnp.float32)
    for k, values in enumerate(tiles):
        moved = pltpu.roll(values, (4 * k + 2) % lanes, 1)
        packed = jnp.where(lane // 4 == k, moved, packed)
    return packed


def unpack_edges(packed, k):
    return pltpu.roll(packed, lanes - (4 * k + 2), 1)


def pack_kernel(cols, rows, parts, early, start_ref, levels_ref, edges_ref, outer_ref, *piece_refs):
    chunks = cols // tile
    part_rows = rows // parts
    for group in range(parts):
        edges_ref[group] = pack_edges(
            tile_at(start_ref, rows, group * part_rows + row, chunk)
            for row in range(part_rows)
            for chunk in range(chunks)
        )
    edges_ref[parts] = pack_edges(
        levels_ref[k * tile : (k + 1) * tile, :].astype(jnp.float32) for k in range(rows // tile)
    )
    for chunk in range(chunks):
        outer_ref[chunk] = tile_at(start_ref, rows, 0, chunk)
        outer_ref[chunks + chunk] = tile_at(start_ref, rows, rows - 1, chunk)
    first = levels_ref[0:1, :].astype(jnp.float32)
    last = levels_ref[rows - 1 : rows, :].astype(jnp.float32)
    outer_ref[2 * chunks] = jnp.where(iota((tile, lanes), 0) == 0, first, last)
    for k, piece_ref in zip(early, piece_refs):
        copy_piece(cols, rows, parts, k, start_ref, piece_ref)


def copy_piece(cols, rows, parts, k, start_ref, piece_ref):
    chunks = cols // tile
    part_rows = rows // parts
    base = (lax.axis_index("col") ^ k) * part_rows
    for row in range(part_rows):
        for chunk in range(chunks):
            piece_ref[row * chunks + chunk] = tile_at(start_ref, rows, base + row, chunk)


def outer_kernel(cols, rows, parts, early, start_ref, outer_ref, near_ref, far_ref, beside_ref, send_ref, *piece_refs):
    from_left = iota((tile, lanes), 1) % 4 < 2
    even_place = lax.axis_index("ly") % 2 == 0
    for group in range(parts + 1):
        near, far = near_ref[group], far_ref[group]
        beside_ref[group] = jnp.where(
            even_place, jnp.where(from_left, far, near), jnp.where(from_left, near, far)
        )
    count = outer_ref.shape[0]
    send_ref[:count] = outer_ref[...]
    send_ref[count] = beside_ref[0]
    send_ref[count + 1] = beside_ref[parts - 1]
    for k, piece_ref in zip(early, piece_refs):
        copy_piece(cols, rows, parts, k, start_ref, piece_ref)


def rim_kernel(cols, rows, parts, late, start_ref, beside_ref, before_ref, after_ref, *out_refs):
    chunks = cols // tile
    part_rows = rows // parts
    place = lax.axis_index("col")
    for k, out_ref in enumerate(out_refs):
        target = place ^ k
        at = 0
        if k in late:
            at = part_rows * chunks
            copy_piece(cols, rows, parts, k, start_ref, out_ref)
        lowest, highest = target == 0, target == parts - 1
        above = jnp.maximum(target * part_rows - 1, 0)
        below = jnp.minimum((target + 1) * part_rows, rows - 1)
        for chunk in range(chunks):
            out_ref[at + chunk] = jnp.where(
                lowest, before_ref[chunks + chunk], tile_at(start_ref, rows, above, chunk)
            )
            out_ref[at + chunks + chunk] = jnp.where(
                highest, after_ref[chunk], tile_at(start_ref, rows, below, chunk)
            )
        at += 2 * chunks
        out_ref[at] = beside_ref[target]
        out_ref[at + 1] = jnp.where(
            lowest, before_ref[2 * chunks + 2], beside_ref[jnp.maximum(target - 1, 0)]
        )
        out_ref[at + 2] = jnp.where(
            highest, after_ref[2 * chunks + 1], beside_ref[jnp.minimum(target + 1, parts - 1)]
        )


def filter_kernel(cols, rows, parts, late, start_ref, levels_ref, beside_ref, before_ref, after_ref, *refs):
    rim_refs, refs = refs[:parts], refs[parts:]
    piece_refs = dict(zip([k for k in range(1, parts) if k not in late], refs))
    whole_ref, gram_ref, field, edge, once, once_edge, factor, factor_edge = refs[len(piece_refs) :]
    chunks = cols // tile
    part_rows = rows // parts
    total = cols * parts
    place = lax.axis_index("col")
    lane = iota((total, lanes), 1)
    first_lane, last_lane = lane == 0, lane == lanes - 1
    even_lane = lane % 2 == 0
    inverse = 1.0 / half_width

    factor[tile : tile + rows, :] = site_factor(levels_ref[...].astype(jnp.float32))
    factor[tile - 1 : tile, :] = site_factor(before_ref[2 * chunks, 1:2, :])
    factor[tile + rows : tile + rows + 1, :] = site_factor(after_ref[2 * chunks, 0:1, :])
    packed = beside_ref[parts]
    for k in range(rows // tile):
        factor_edge[k * tile : (k + 1) * tile, :] = site_factor(unpack_edges(packed, k))
    for k in range(parts):
        base = (place ^ k) * cols
        at = part_rows * chunks if k in late else 0
        rim_ref = rim_refs[k]
        for chunk in range(chunks):
            part = pl.ds(pl.multiple_of(base + chunk * tile, tile), tile)
            for row in range(part_rows):
                if k == 0:
                    values = tile_at(start_ref, rows, place * part_rows + row, chunk)
                else:
                    values = (rim_ref if k in late else piece_refs[k])[row * chunks + chunk]
                field[row + 1, part, :] = values
                edge[row + 1, part, :] = unpack_edges(
                    rim_ref[at + 2 * chunks], row * chunks + chunk
                )
            field[0, part, :] = rim_ref[at + chunk]
            field[part_rows + 1, part, :] = rim_ref[at + chunks + chunk]
            edge[0, part, :] = unpack_edges(
                rim_ref[at + 2 * chunks + 1], (part_rows - 1) * chunks + chunk
            )
            edge[part_rows + 1, part, :] = unpack_edges(rim_ref[at + 2 * chunks + 2], chunk)

    def sides(main, other):
        return pltpu.roll(jnp.where(last_lane, other, main), 1, 1) + pltpu.roll(
            jnp.where(first_lane, other, main), lanes - 1, 1
        )

    def factor_at(ref, row):
        return jnp.broadcast_to(ref[pl.ds(row, 1), :], (total, lanes))

    base = place * part_rows
    for row in range(-1, part_rows + 1):
        here, beside = field[row + 1], edge[row + 1]
        even = even_lane if row % 2 == 0 else jnp.logical_not(even_lane)
        if row == -1:
            vertical = field[1]
        elif row == part_rows:
            vertical = field[part_rows]
        else:
            vertical = jnp.where(even, field[row + 2], field[row])
        once[row + 1] = factor_at(factor, tile + base + row) * here - inverse * (
            sides(here, beside) + vertical
        )
        if 0 <= row < part_rows:
            vertical = jnp.where(even, edge[row + 2], edge[row])
            once_edge[row] = factor_at(factor_edge, base + row) * beside - inverse * (
                sides(beside, here) + vertical
            )
    products = jnp.zeros((3 * total, 3 * total), jnp.float32)
    for row in range(part_rows):
        here = once[row + 1]
        even = even_lane if row % 2 == 0 else jnp.logical_not(even_lane)
        vertical = jnp.where(even, once[row + 2], once[row])
        twice = factor_at(factor, tile + base + row) * here - inverse * (
            sides(here, once_edge[row]) + vertical
        )
        whole_ref[row] = 2.0 * twice - field[row + 1]
        if row % 2:
            values = jnp.concatenate([whole_ref[row - 1], whole_ref[row]], axis=1)
            stack = jnp.concatenate(split(values), axis=0)
            products += lax.dot_general(
                stack, stack, (((1,), (1,)), ((), ())), preferred_element_type=jnp.float32
            )
    gram = jnp.zeros((total, total), jnp.float32)
    for i in reversed(range(3)):
        for j in reversed(range(3)):
            gram += products[i * total : (i + 1) * total, j * total : (j + 1) * total]
    half = total // 2
    gram_ref[...] = jnp.concatenate([gram[:half], gram[half:]], axis=1)


def split(values):
    high = values.astype(jnp.bfloat16)
    rest = values - high.astype(jnp.float32)
    middle = rest.astype(jnp.bfloat16)
    low = (rest - middle.astype(jnp.float32)).astype(jnp.bfloat16)
    return high, middle, low


def solve_kernel(scale, whole_ref, gram_ref, other_ref, out_ref):
    part_rows, total, _ = whole_ref.shape
    blocks = total // tile
    half = total // 2
    packed = gram_ref[...] + other_ref[...]
    lane = iota((tile, lanes), 1)
    sub = iota((tile, lanes), 0)
    shape = (tile, lanes)
    work = []
    for i in range(blocks):
        at = i * tile % half
        block = packed[at : at + tile, :]
        if i * tile >= half:
            block = pltpu.roll(block, total, 1)
        unit = jnp.where(lane - total == sub + i * tile, 1.0, 0.0)
        work.append(jnp.where(lane < total, block, unit))
    for b in range(blocks):
        column = {
            i: [
                jnp.broadcast_to(work[i][:, b * tile + m : b * tile + m + 1], shape)
                for m in range(tile)
            ]
            for i in range(b, blocks)
        }
        for m in range(tile):
            pivot = jnp.broadcast_to(column[b][m][m : m + 1, :], shape)
            root = lax.rsqrt(pivot)
            root = root * (1.5 - 0.5 * (pivot * root) * root)
            row = jnp.broadcast_to(work[b][m : m + 1, :], shape) * root
            heads = [
                jnp.broadcast_to(column[b][p][m : m + 1, :], shape) * root
                for p in range(m + 1, tile)
            ]
            for i in range(b, blocks):
                ratio = column[i][m] * root
                if i == b:
                    ratio = jnp.where(sub > m, ratio, 0.0)
                    work[i] = jnp.where(sub == m, row, work[i] - ratio * row)
                else:
                    work[i] = work[i] - ratio * row
                for p in range(m + 1, tile):
                    column[i][p] = column[i][p] - ratio * heads[p - m - 1]
    solver = jnp.concatenate(work, axis=0) * scale
    wide = iota((total, lanes), 1)
    high, middle, low = (piece.astype(jnp.float32) for piece in split(solver))

    def pair(left, right):
        return jnp.where(wide < total, pltpu.roll(left, total, 1), right).astype(jnp.bfloat16)

    left_main = jnp.concatenate([pair(high, high), pair(middle, middle)], axis=1)
    left_rest = pair(high, low)
    for row in range(0, part_rows, 2):
        values = jnp.concatenate([whole_ref[row], whole_ref[row + 1]], axis=1)
        f_high, f_middle, f_low = split(values)
        right_main = jnp.concatenate([f_high, f_middle, f_high, f_middle], axis=0)
        right_rest = jnp.concatenate([f_low, f_high], axis=0)
        result = jnp.dot(left_rest, right_rest, preferred_element_type=jnp.float32) + jnp.dot(
            left_main, right_main, preferred_element_type=jnp.float32
        )
        out_ref[pl.ds(row, total, stride=part_rows), :] = result[:, :lanes]
        out_ref[pl.ds(row + 1, total, stride=part_rows), :] = result[:, lanes:]


def call(kernel, outs, *operands, scratch=()):
    return pl.pallas_call(
        kernel,
        out_shape=[jax.ShapeDtypeStruct(shape, jnp.float32) for shape in outs],
        scratch_shapes=[pltpu.VMEM(shape, jnp.float32) for shape in scratch],
        compiler_params=pltpu.CompilerParams(vmem_limit_bytes=32 * 1024 * 1024),
    )(*operands)


def exchange(values, axis, distance):
    count = lax.axis_size(axis)
    return lax.ppermute(values, axis, [(i, i ^ distance) for i in range(count)])


def sending_order(parts):
    if parts == 4:
        return (2,), (3,), (1,)
    far = tuple(k for k in range(parts // 2, parts))
    return far, tuple(k for k in range(2, parts // 2)), (1,)


def shards(start, levels):
    cols, rows, _ = start.shape
    parts = lax.axis_size("col")
    chunks = cols // tile
    total = cols * parts
    part_rows = rows // parts
    sizes = (cols, rows, parts)
    first, second, late = sending_order(parts)
    flat = start.reshape(cols * rows, lanes)
    piece = (part_rows * chunks, tile, lanes)
    edges, outer, *firsts = call(
        functools.partial(pack_kernel, *sizes, first),
        [(parts + 1, tile, lanes), (2 * chunks + 1, tile, lanes)] + [piece] * len(first),
        flat,
        levels,
    )
    arrived = {}
    count = lax.axis_size("ly")
    near = exchange(edges, "ly", 1)
    far_pairs = [(i, (i + 1) % count if i % 2 else (i - 1) % count) for i in range(count)]
    far = lax.ppermute(edges, "ly", far_pairs)
    for k, values in zip(first, firsts):
        arrived[k] = exchange(values, "col", k)
    beside, outer, *seconds = call(
        functools.partial(outer_kernel, *sizes, second),
        [(parts + 1, tile, lanes), (2 * chunks + 3, tile, lanes)] + [piece] * len(second),
        flat,
        outer,
        near,
        far,
    )
    count = lax.axis_size("lx")
    before = lax.ppermute(outer, "lx", [(i, (i + 1) % count) for i in range(count)])
    after = before
    if count > 2:
        after = lax.ppermute(outer, "lx", [((i + 1) % count, i) for i in range(count)])
    for k, values in zip(second, seconds):
        arrived[k] = exchange(values, "col", k)
    rims = call(
        functools.partial(rim_kernel, *sizes, late),
        [
            (2 * chunks + 3 + (part_rows * chunks if k in late else 0), tile, lanes)
            for k in range(parts)
        ],
        flat,
        beside,
        before,
        after,
    )
    rims = [exchange(values, "col", k) if k else values for k, values in enumerate(rims)]
    whole, gram = call(
        functools.partial(filter_kernel, *sizes, late),
        [(part_rows, total, lanes), (total // 2, 2 * total)],
        flat,
        levels,
        beside,
        before,
        after,
        *rims,
        *(arrived[k] for k in sorted(arrived)),
        scratch=[
            (part_rows + 2, total, lanes),
            (part_rows + 2, total, lanes),
            (part_rows + 2, total, lanes),
            (part_rows, total, lanes),
            (rows + 2 * tile, lanes),
            (rows, lanes),
        ],
    )
    steps = []
    for axis in ("ly", "lx", "col"):
        bit = 1
        while bit < lax.axis_size(axis):
            steps.append((axis, bit))
            bit *= 2
    for axis, bit in steps[:-1]:
        gram = gram + exchange(gram, axis, bit)
    scale = math.sqrt(rows * lax.axis_size("lx") * lanes * lax.axis_size("ly"))
    (basis,) = call(
        functools.partial(solve_kernel, scale),
        [(total * part_rows, lanes)],
        whole,
        gram,
        exchange(gram, *steps[-1]),
    )
    return basis.reshape(total, part_rows, lanes)


def solution(mesh):
    placed = (P("col", "lx", "ly"), P("lx", "ly"))
    return jax.shard_map(
        shards, mesh=mesh, in_specs=placed, out_specs=P(None, ("lx", "col"), "ly"), check_vma=False
    )
```

time: 47.5 us -> 51.1 us (1.076)
  starting transfers between devices: 17.3 us -> 20 us
  waiting for transfers between devices: 22.5 us -> 23.1 us
    ppermute x9 -> x11, starting transfers between devices: 13 us -> 15.1 us  [exchange(): return lax.ppermute(values, axis, [(i, i ^ distance) for i in range(count)])]
    ppermute x9 -> x11, waiting for transfers between devices: 18.9 us -> 20.4 us  [exchange(): return lax.ppermute(values, axis, [(i, i ^ distance) for i in range(count)])]
    ppermute x1, starting transfers between devices: 1.72 us -> 2.43 us  [shards(): lax.ppermute(outer, 'lx', [(i, (i + 1) % count) for i in range(count)])]
    ppermute x1, waiting for transfers between devices: 1.47 us -> 0.84 us  [shards(): far = lax.ppermute(edges, 'ly', far_pairs)]
    pallas_call x4 -> x5, Pallas kernels: 5.58 us -> 5.86 us  [call(): pl.pallas_call(kernel, out_shape=[jax.ShapeDtypeStruct(shape, jnp.float32...]
    unnamed x8 -> x6, local copies, waits for them, and re-layouts: 1.81 us -> 1.8 us
  transfers between devices with their start and end apart: 11 -> 13, of which waited for: 9 -> 8; matrix products, arithmetic and copies ran while one was open for 0% -> 0% of each run, Pallas kernels for 0% -> 0%
where the time goes in v2:
time: 51.1 us; the launch traced here: 50.8 us
  waiting for transfers between devices  23.1 us (45%)
  starting transfers between devices  20 us (39%)
  Pallas kernels  5.86 us (11%)
  local copies, waits for them, and re-layouts  1.8 us (4%)
    ppermute x11, waiting for transfers between devices, exchange(): return lax.ppermute(values, axis, [(i, i ^ distance) for i in range(count)])  20.4 us
    ppermute x11, starting transfers between devices, exchange(): return lax.ppermute(values, axis, [(i, i ^ distance) for i in range(count)])  15.1 us
    pallas_call x5, Pallas kernels, call(): pl.pallas_call(kernel, out_shape=[jax.ShapeDtypeStruct(shape, jnp.float32...  5.86 us
    ppermute x1, starting transfers between devices, shards(): far = lax.ppermute(edges, 'ly', far_pairs)  2.47 us
    ppermute x1, starting transfers between devices, shards(): lax.ppermute(outer, 'lx', [(i, (i + 1) % count) for i in range(count)])  2.43 us
    ppermute x1, waiting for transfers between devices, shards(): lax.ppermute(outer, 'lx', [(i, (i + 1) % count) for i in range(count)])  1.85 us
    unnamed x6, local copies, waits for them, and re-layouts  1.8 us
  transfers between devices with their start and end apart: 13, of which 8 were waited for; matrix products, arithmetic and copies ran while one was open for 0% of the time, Pallas kernels for 0%

profile of v2, /device:TPU:0, one launch (start us, length us, event | category | flops | bytes accessed | tf_op | source)
XLA Modules:
  0.0 50.8 jit_solution(9945896616956065551)
XLA Ops:
  0.0 1.0 %copy-done = f32[16,64,128]{2,1,0:T(8,128)S(1)} copy-done((f32[16,64,128]{2,1,0:T(8,128)S(1)}, f32[16,64,128]{2,1,0:T(8,128)}, u32[]{:S(2)}) %copy-start) | copy-done | bytes 524312
  1.0 0.8 %copy-done.1 = s32[64,128]{1,0:T(8,128)S(1)} copy-done((s32[64,128]{1,0:T(8,128)S(1)}, s32[64,128]{1,0:T(8,128)}, u32[]{:S(2)}) %copy-start.1) | copy-done | bytes 32792
  1.8 0.4 shard_map.28
  2.2 2.5 %collective-permute-start.1 = (f32[5,8,128]{2,1,0:T(8,128)S(1)}, f32[5,8,128]{2,1,0:T(8,128)S(1)}, u32[]{:S(2)}, u32[]{:S(2)}) collective-permute-start(f32[5,8,128]{2,1,0:T(8,128)S(1)} %get-tuple-element.18), channel_id=1, source_target_pairs={{0,12},{4,8},{8,4},{12,0},{1,13},{5,9},{9,5},{13,1},{2,14},{6,10},... | collective-permute-start | bytes 61448 | tf_op jit(solution)/shard_map/ppermute | solution.py:324
  4.7 0.7 %collective-permute-start = (f32[5,8,128]{2,1,0:T(8,128)S(1)}, f32[5,8,128]{2,1,0:T(8,128)S(1)}, u32[]{:S(2)}, u32[]{:S(2)}) collective-permute-start(f32[5,8,128]{2,1,0:T(8,128)S(1)} %get-tuple-element.18), channel_id=1, source_target_pairs={{0,4},{4,0},{8,12},{12,8},{1,5},{5,1},{9,13},{13,9},{2,6},{6,2},{1... | collective-permute-start | bytes 61448 | tf_op jit(solution)/shard_map/ppermute | solution.py:294
  5.3 0.8 %collective-permute-done.1.far_ref = f32[5,8,128]{2,1,0:T(8,128)S(1)} collective-permute-done((f32[5,8,128]{2,1,0:T(8,128)S(1)}, f32[5,8,128]{2,1,0:T(8,128)S(1)}, u32[]{:S(2)}, u32[]{:S(2)}) %collective-permute-start.1) | collective-permute-done | bytes 20512 | tf_op jit(solution)/shard_map/ppermute | solution.py:324
  6.2 0.0 collective-permute-done.near_ref
  6.2 0.1 shard_map.29
  6.3 2.4 %collective-permute-start.2 = (f32[7,8,128]{2,1,0:T(8,128)S(1)}, f32[7,8,128]{2,1,0:T(8,128)S(1)}, u32[]{:S(2)}, u32[]{:S(2)}) collective-permute-start(f32[7,8,128]{2,1,0:T(8,128)S(1)} %get-tuple-element.20), channel_id=1, source_target_pairs={{0,16},{16,0},{1,17},{17,1},{2,18},{18,2},{3,19},{19,3},{4,20},{20... | collective-permute-start | bytes 86024 | tf_op jit(solution)/shard_map/ppermute | solution.py:336
  8.7 1.9 %collective-permute-done.2.before_ref.after_ref = f32[7,8,128]{2,1,0:T(8,128)S(1)} collective-permute-done((f32[7,8,128]{2,1,0:T(8,128)S(1)}, f32[7,8,128]{2,1,0:T(8,128)S(1)}, u32[]{:S(2)}, u32[]{:S(2)}) %collective-permute-start.2) | collective-permute-done | bytes 28704 | tf_op jit(solution)/shard_map/ppermute | solution.py:336
  10.5 0.1 shard_map.30
  10.7 2.2 %collective-permute-start.3 = (f32[39,8,128]{2,1,0:T(8,128)S(1)}, f32[39,8,128]{2,1,0:T(8,128)S(1)}, u32[]{:S(2)}, u32[]{:S(2)}) collective-permute-start(f32[39,8,128]{2,1,0:T(8,128)S(1)} %get-tuple-element.22), channel_id=1, source_target_pairs={{0,1},{1,0},{2,3},{3,2},{4,5},{5,4},{6,7},{7,6},{8,9},{9,8},{10,11... | collective-permute-start | bytes 479240 | tf_op jit(solution)/shard_map/ppermute | solution.py:294
  12.9 2.6 %collective-permute-start.6 = (f32[32,8,128]{2,1,0:T(8,128)S(1)}, f32[32,8,128]{2,1,0:T(8,128)S(1)}, u32[]{:S(2)}, u32[]{:S(2)}) collective-permute-start(f32[32,8,128]{2,1,0:T(8,128)S(1)} %get-tuple-element.25), channel_id=1, source_target_pairs={{0,2},{1,3},{2,0},{3,1},{4,6},{5,7},{6,4},{7,5},{8,10},{9,11},{10,... | collective-permute-start | bytes 393224 | tf_op jit(solution)/shard_map/ppermute | solution.py:294
  15.5 0.0 collective-permute-start.7
  15.5 1.9 %collective-permute-start.4 = (f32[7,8,128]{2,1,0:T(8,128)S(1)}, f32[7,8,128]{2,1,0:T(8,128)S(1)}, u32[]{:S(2)}, u32[]{:S(2)}) collective-permute-start(f32[7,8,128]{2,1,0:T(8,128)S(1)} %get-tuple-element.23), channel_id=1, source_target_pairs={{0,2},{1,3},{2,0},{3,1},{4,6},{5,7},{6,4},{7,5},{8,10},{9,11},{10,... | collective-permute-start | bytes 86024 | tf_op jit(solution)/shard_map/ppermute | solution.py:294
  17.4 1.9 %collective-permute-start.5 = (f32[7,8,128]{2,1,0:T(8,128)S(1)}, f32[7,8,128]{2,1,0:T(8,128)S(1)}, u32[]{:S(2)}, u32[]{:S(2)}) collective-permute-start(f32[7,8,128]{2,1,0:T(8,128)S(1)} %get-tuple-element.24), channel_id=1, source_target_pairs={{0,3},{1,2},{2,1},{3,0},{4,7},{5,6},{6,5},{7,4},{8,11},{9,10},{10,... | collective-permute-start | bytes 86024 | tf_op jit(solution)/shard_map/ppermute | solution.py:294
  19.3 9.2 %collective-permute-done.4.refs_2_ = f32[7,8,128]{2,1,0:T(8,128)S(1)} collective-permute-done((f32[7,8,128]{2,1,0:T(8,128)S(1)}, f32[7,8,128]{2,1,0:T(8,128)S(1)}, u32[]{:S(2)}, u32[]{:S(2)}) %collective-permute-start.4) | collective-permute-done | bytes 28704 | tf_op jit(solution)/shard_map/ppermute | solution.py:294
  28.5 0.0 collective-permute-done.5.refs_3_
  28.5 0.0 collective-permute-done.6.refs_4_
  28.5 0.0 collective-permute-done.7.refs_5_
  28.5 1.7 %shard_map.31 = (f32[16,64,128]{2,1,0:T(8,128)S(1)}, f32[32,128]{1,0:T(8,128)S(1)}) custom-call(f32[1024,128]{1,0:T(8,128)S(1)} %bitcast.5, s32[64,128]{1,0:T(8,128)S(1)} %copy-done.2, f32[5,8,128]{2,1,0:T(8,128)S(1)} %get-tuple-element.19.beside_ref, f32[7,8,128]{2,1,0:T(8,128)S(1)} %collective-permute-done.2.before_ref.after_ref, ...), custom_call_target="tpu_custom_call" | custom-call | tf_op jit(solution)/shard_map/pallas_call | solution.py:284
  30.2 0.0 collective-permute-start.8
  30.2 1.2 %collective-permute-done.8 = f32[32,128]{1,0:T(8,128)S(1)} collective-permute-done((f32[32,128]{1,0:T(8,128)S(1)}, f32[32,128]{1,0:T(8,128)S(1)}, u32[]{:S(2)}, u32[]{:S(2)}) %collective-permute-start.8) | collective-permute-done | bytes 16416 | tf_op jit(solution)/shard_map/ppermute | solution.py:294
  31.4 1.6 %collective-permute-start.9 = (f32[32,128]{1,0:T(8,128)S(1)}, f32[32,128]{1,0:T(8,128)S(1)}, u32[]{:S(2)}, u32[]{:S(2)}) collective-permute-start(f32[32,128]{1,0:T(8,128)S(1)} %add.12), channel_id=1, source_target_pairs={{0,8},{4,12},{8,0},{12,4},{1,9},{5,13},{9,1},{13,5},{2,10},{6,14},... | collective-permute-start | bytes 49160 | tf_op jit(solution)/shard_map/ppermute | solution.py:294
  33.0 2.2 %collective-permute-done.9 = f32[32,128]{1,0:T(8,128)S(1)} collective-permute-done((f32[32,128]{1,0:T(8,128)S(1)}, f32[32,128]{1,0:T(8,128)S(1)}, u32[]{:S(2)}, u32[]{:S(2)}) %collective-permute-start.9) | collective-permute-done | bytes 16416 | tf_op jit(solution)/shard_map/ppermute | solution.py:294
  35.2 1.5 %collective-permute-start.10 = (f32[32,128]{1,0:T(8,128)S(1)}, f32[32,128]{1,0:T(8,128)S(1)}, u32[]{:S(2)}, u32[]{:S(2)}) collective-permute-start(f32[32,128]{1,0:T(8,128)S(1)} %add.13), channel_id=1, source_target_pairs={{0,16},{16,0},{1,17},{17,1},{2,18},{18,2},{3,19},{19,3},{4,20},{20... | collective-permute-start | bytes 49160 | tf_op jit(solution)/shard_map/ppermute | solution.py:294
  36.7 2.2 %collective-permute-done.10 = f32[32,128]{1,0:T(8,128)S(1)} collective-permute-done((f32[32,128]{1,0:T(8,128)S(1)}, f32[32,128]{1,0:T(8,128)S(1)}, u32[]{:S(2)}, u32[]{:S(2)}) %collective-permute-start.10) | collective-permute-done | bytes 16416 | tf_op jit(solution)/shard_map/ppermute | solution.py:294
  38.9 0.9 %collective-permute-start.11 = (f32[32,128]{1,0:T(8,128)S(1)}, f32[32,128]{1,0:T(8,128)S(1)}, u32[]{:S(2)}, u32[]{:S(2)}) collective-permute-start(f32[32,128]{1,0:T(8,128)S(1)} %add.14), channel_id=1, source_target_pairs={{0,1},{1,0},{2,3},{3,2},{4,5},{5,4},{6,7},{7,6},{8,9},{9,8},{10,11... | collective-permute-start | bytes 49160 | tf_op jit(solution)/shard_map/ppermute | solution.py:294
  39.8 2.9 %collective-permute-done.11 = f32[32,128]{1,0:T(8,128)S(1)} collective-permute-done((f32[32,128]{1,0:T(8,128)S(1)}, f32[32,128]{1,0:T(8,128)S(1)}, u32[]{:S(2)}, u32[]{:S(2)}) %collective-permute-start.11) | collective-permute-done | bytes 16416 | tf_op jit(solution)/shard_map/ppermute | solution.py:294
  42.7 1.9 %collective-permute-start.12 = (f32[32,128]{1,0:T(8,128)S(1)}, f32[32,128]{1,0:T(8,128)S(1)}, u32[]{:S(2)}, u32[]{:S(2)}) collective-permute-start(f32[32,128]{1,0:T(8,128)S(1)} %add.15.gram_ref), channel_id=1, source_target_pairs={{0,2},{1,3},{2,0},{3,1},{4,6},{5,7},{6,4},{7,5},{8,10},{9,11},{10,... | collective-permute-start | bytes 49160 | tf_op jit(solution)/shard_map/ppermute | solution.py:294
  44.5 2.8 %collective-permute-done.12.other_ref = f32[32,128]{1,0:T(8,128)S(1)} collective-permute-done((f32[32,128]{1,0:T(8,128)S(1)}, f32[32,128]{1,0:T(8,128)S(1)}, u32[]{:S(2)}, u32[]{:S(2)}) %collective-permute-start.12) | collective-permute-done | bytes 16416 | tf_op jit(solution)/shard_map/ppermute | solution.py:294
  47.3 3.5 %shard_map.32 = f32[1024,128]{1,0:T(8,128)} custom-call(f32[16,64,128]{2,1,0:T(8,128)S(1)} %get-tuple-element.27.whole_ref, f32[32,128]{1,0:T(8,128)S(1)} %add.15.gram_ref, f32[32,128]{1,0:T(8,128)S(1)} %collective-permute-done.12.other_ref), custom_call_target="tpu_custom_call" | custom-call | tf_op jit(solution)/shard_map/pallas_call | solution.py:284
  (9 shorter events, 0.0 us)
Async XLA Ops:
  0.0 1.0 %copy-start = (f32[16,64,128]{2,1,0:T(8,128)S(1)}, f32[16,64,128]{2,1,0:T(8,128)}, u32[]{:S(2)}) copy-start(f32[16,64,128]{2,1,0:T(8,128)} %param.2) | copy-start | bytes 1572868
  1.0 0.8 %copy-start.1 = (s32[64,128]{1,0:T(8,128)S(1)}, s32[64,128]{1,0:T(8,128)}, u32[]{:S(2)}) copy-start(s32[64,128]{1,0:T(8,128)} %levels_ref.3) | copy-start | bytes 98308
  2.2 4.0 %collective-permute-start.1 = (f32[5,8,128]{2,1,0:T(8,128)S(1)}, f32[5,8,128]{2,1,0:T(8,128)S(1)}, u32[]{:S(2)}, u32[]{:S(2)}) collective-permute-start(f32[5,8,128]{2,1,0:T(8,128)S(1)} %get-tuple-element.18), channel_id=1, source_target_pairs={{0,12},{4,8},{8,4},{12,0},{1,13},{5,9},{9,5},{13,1},{2,14},{6,10},... | collective-permute-start | bytes 61448 | tf_op jit(solution)/shard_map/ppermute | solution.py:324
  4.7 1.5 %collective-permute-start = (f32[5,8,128]{2,1,0:T(8,128)S(1)}, f32[5,8,128]{2,1,0:T(8,128)S(1)}, u32[]{:S(2)}, u32[]{:S(2)}) collective-permute-start(f32[5,8,128]{2,1,0:T(8,128)S(1)} %get-tuple-element.18), channel_id=1, source_target_pairs={{0,4},{4,0},{8,12},{12,8},{1,5},{5,1},{9,13},{13,9},{2,6},{6,2},{1... | collective-permute-start | bytes 61448 | tf_op jit(solution)/shard_map/ppermute | solution.py:294
  6.3 4.3 %collective-permute-start.2 = (f32[7,8,128]{2,1,0:T(8,128)S(1)}, f32[7,8,128]{2,1,0:T(8,128)S(1)}, u32[]{:S(2)}, u32[]{:S(2)}) collective-permute-start(f32[7,8,128]{2,1,0:T(8,128)S(1)} %get-tuple-element.20), channel_id=1, source_target_pairs={{0,16},{16,0},{1,17},{17,1},{2,18},{18,2},{3,19},{19,3},{4,20},{20... | collective-permute-start | bytes 86024 | tf_op jit(solution)/shard_map/ppermute | solution.py:336
  10.5 18.0 %copy-start.2 = (s32[64,128]{1,0:T(8,128)S(1)}, s32[64,128]{1,0:T(8,128)}, u32[]{:S(2)}) copy-start(s32[64,128]{1,0:T(8,128)} %levels_ref.3) | copy-start | bytes 98308
  10.7 17.8 %collective-permute-start.3 = (f32[39,8,128]{2,1,0:T(8,128)S(1)}, f32[39,8,128]{2,1,0:T(8,128)S(1)}, u32[]{:S(2)}, u32[]{:S(2)}) collective-permute-start(f32[39,8,128]{2,1,0:T(8,128)S(1)} %get-tuple-element.22), channel_id=1, source_target_pairs={{0,1},{1,0},{2,3},{3,2},{4,5},{5,4},{6,7},{7,6},{8,9},{9,8},{10,11... | collective-permute-start | bytes 479240 | tf_op jit(solution)/shard_map/ppermute | solution.py:294
  12.9 15.6 %collective-permute-start.6 = (f32[32,8,128]{2,1,0:T(8,128)S(1)}, f32[32,8,128]{2,1,0:T(8,128)S(1)}, u32[]{:S(2)}, u32[]{:S(2)}) collective-permute-start(f32[32,8,128]{2,1,0:T(8,128)S(1)} %get-tuple-element.25), channel_id=1, source_target_pairs={{0,2},{1,3},{2,0},{3,1},{4,6},{5,7},{6,4},{7,5},{8,10},{9,11},{10,... | collective-permute-start | bytes 393224 | tf_op jit(solution)/shard_map/ppermute | solution.py:294
  15.5 13.0 %collective-permute-start.7 = (f32[32,8,128]{2,1,0:T(8,128)S(1)}, f32[32,8,128]{2,1,0:T(8,128)S(1)}, u32[]{:S(2)}, u32[]{:S(2)}) collective-permute-start(f32[32,8,128]{2,1,0:T(8,128)S(1)} %get-tuple-element.26), channel_id=1, source_target_pairs={{0,3},{1,2},{2,1},{3,0},{4,7},{5,6},{6,5},{7,4},{8,11},{9,10},{10,... | collective-permute-start | bytes 393224 | tf_op jit(solution)/shard_map/ppermute | solution.py:294
  15.5 13.0 %collective-permute-start.4 = (f32[7,8,128]{2,1,0:T(8,128)S(1)}, f32[7,8,128]{2,1,0:T(8,128)S(1)}, u32[]{:S(2)}, u32[]{:S(2)}) collective-permute-start(f32[7,8,128]{2,1,0:T(8,128)S(1)} %get-tuple-element.23), channel_id=1, source_target_pairs={{0,2},{1,3},{2,0},{3,1},{4,6},{5,7},{6,4},{7,5},{8,10},{9,11},{10,... | collective-permute-start | bytes 86024 | tf_op jit(solution)/shard_map/ppermute | solution.py:294
  17.4 11.1 %collective-permute-start.5 = (f32[7,8,128]{2,1,0:T(8,128)S(1)}, f32[7,8,128]{2,1,0:T(8,128)S(1)}, u32[]{:S(2)}, u32[]{:S(2)}) collective-permute-start(f32[7,8,128]{2,1,0:T(8,128)S(1)} %get-tuple-element.24), channel_id=1, source_target_pairs={{0,3},{1,2},{2,1},{3,0},{4,7},{5,6},{6,5},{7,4},{8,11},{9,10},{10,... | collective-permute-start | bytes 86024 | tf_op jit(solution)/shard_map/ppermute | solution.py:294
  30.2 1.2 %collective-permute-start.8 = (f32[32,128]{1,0:T(8,128)S(1)}, f32[32,128]{1,0:T(8,128)S(1)}, u32[]{:S(2)}, u32[]{:S(2)}) collective-permute-start(f32[32,128]{1,0:T(8,128)S(1)} %get-tuple-element.28), channel_id=1, source_target_pairs={{0,4},{4,0},{8,12},{12,8},{1,5},{5,1},{9,13},{13,9},{2,6},{6,2},{1... | collective-permute-start | bytes 49160 | tf_op jit(solution)/shard_map/ppermute | solution.py:294
  31.4 3.7 %collective-permute-start.9 = (f32[32,128]{1,0:T(8,128)S(1)}, f32[32,128]{1,0:T(8,128)S(1)}, u32[]{:S(2)}, u32[]{:S(2)}) collective-permute-start(f32[32,128]{1,0:T(8,128)S(1)} %add.12), channel_id=1, source_target_pairs={{0,8},{4,12},{8,0},{12,4},{1,9},{5,13},{9,1},{13,5},{2,10},{6,14},... | collective-permute-start | bytes 49160 | tf_op jit(solution)/shard_map/ppermute | solution.py:294
  35.2 3.7 %collective-permute-start.10 = (f32[32,128]{1,0:T(8,128)S(1)}, f32[32,128]{1,0:T(8,128)S(1)}, u32[]{:S(2)}, u32[]{:S(2)}) collective-permute-start(f32[32,128]{1,0:T(8,128)S(1)} %add.13), channel_id=1, source_target_pairs={{0,16},{16,0},{1,17},{17,1},{2,18},{18,2},{3,19},{19,3},{4,20},{20... | collective-permute-start | bytes 49160 | tf_op jit(solution)/shard_map/ppermute | solution.py:294
  38.9 3.7 %collective-permute-start.11 = (f32[32,128]{1,0:T(8,128)S(1)}, f32[32,128]{1,0:T(8,128)S(1)}, u32[]{:S(2)}, u32[]{:S(2)}) collective-permute-start(f32[32,128]{1,0:T(8,128)S(1)} %add.14), channel_id=1, source_target_pairs={{0,1},{1,0},{2,3},{3,2},{4,5},{5,4},{6,7},{7,6},{8,9},{9,8},{10,11... | collective-permute-start | bytes 49160 | tf_op jit(solution)/shard_map/ppermute | solution.py:294
  42.7 4.6 %collective-permute-start.12 = (f32[32,128]{1,0:T(8,128)S(1)}, f32[32,128]{1,0:T(8,128)S(1)}, u32[]{:S(2)}, u32[]{:S(2)}) collective-permute-start(f32[32,128]{1,0:T(8,128)S(1)} %add.15.gram_ref), channel_id=1, source_target_pairs={{0,2},{1,3},{2,0},{3,1},{4,6},{5,7},{6,4},{7,5},{8,10},{9,11},{10,... | collective-permute-start | bytes 49160 | tf_op jit(solution)/shard_map/ppermute | solution.py:294

commit v3 on v1

v3 whole, which is shorter than its diff:
```python
import functools
import math

import jax
import jax.numpy as jnp
from jax import lax
from jax.experimental import pallas as pl
from jax.experimental.pallas import tpu as pltpu
from jax.sharding import PartitionSpec as P

center = 2.1
half_width = 3.1
spread_width = 4.0
level_top = 15.0
lanes = 128
tile = 8


def iota(shape, dim):
    return lax.broadcasted_iota(jnp.int32, shape, dim)


def site_factor(levels):
    onsite = spread_width * (levels / level_top - 0.5)
    return (onsite - center) / half_width


def tile_at(ref, rows, row, chunk):
    return ref[pl.ds(chunk * tile * rows + row, tile, stride=rows), :]


def pack_edges(tiles):
    lane = iota((tile, lanes), 1)
    packed = jnp.zeros((tile, lanes), jnp.float32)
    for k, values in enumerate(tiles):
        moved = pltpu.roll(values, (4 * k + 2) % lanes, 1)
        packed = jnp.where(lane // 4 == k, moved, packed)
    return packed


def unpack_edges(packed, k):
    return pltpu.roll(packed, lanes - (4 * k + 2), 1)


def pack_kernel(cols, rows, parts, early, start_ref, levels_ref, edges_ref, outer_ref, *piece_refs):
    chunks = cols // tile
    part_rows = rows // parts
    for group in range(parts):
        edges_ref[group] = pack_edges(
            tile_at(start_ref, rows, group * part_rows + row, chunk)
            for row in range(part_rows)
            for chunk in range(chunks)
        )
    edges_ref[parts] = pack_edges(
        levels_ref[k * tile : (k + 1) * tile, :].astype(jnp.float32) for k in range(rows // tile)
    )
    for chunk in range(chunks):
        outer_ref[chunk] = tile_at(start_ref, rows, 0, chunk)
        outer_ref[chunks + chunk] = tile_at(start_ref, rows, rows - 1, chunk)
    first = levels_ref[0:1, :].astype(jnp.float32)
    last = levels_ref[rows - 1 : rows, :].astype(jnp.float32)
    outer_ref[2 * chunks] = jnp.where(iota((tile, lanes), 0) == 0, first, last)
    for k, piece_ref in zip(early, piece_refs):
        copy_piece(cols, rows, parts, k, start_ref, piece_ref)


def copy_piece(cols, rows, parts, k, start_ref, piece_ref):
    chunks = cols // tile
    part_rows = rows // parts
    base = (lax.axis_index("col") ^ k) * part_rows
    for row in range(part_rows):
        for chunk in range(chunks):
            piece_ref[row, chunk * tile : (chunk + 1) * tile, :] = tile_at(
                start_ref, rows, base + row, chunk
            )


def outer_kernel(parts, outer_ref, near_ref, far_ref, beside_ref, send_ref):
    from_left = iota((tile, lanes), 1) % 4 < 2
    even_place = lax.axis_index("ly") % 2 == 0
    for group in range(parts + 1):
        near, far = near_ref[group], far_ref[group]
        beside_ref[group] = jnp.where(
            even_place, jnp.where(from_left, far, near), jnp.where(from_left, near, far)
        )
    count = outer_ref.shape[0]
    send_ref[:count] = outer_ref[...]
    send_ref[count] = beside_ref[0]
    send_ref[count + 1] = beside_ref[parts - 1]


inverse = 1.0 / half_width


def sides(main, other):
    lane = iota(main.shape, 1)
    return pltpu.roll(jnp.where(lane == lanes - 1, other, main), 1, 1) + pltpu.roll(
        jnp.where(lane == 0, other, main), lanes - 1, 1
    )


def upward(row, above, below):
    even = iota(above.shape, 1) % 2 == row % 2
    return jnp.where(even, above, below)


def factor_at(ref, row, height):
    return jnp.broadcast_to(ref[pl.ds(row, 1), :], (height, lanes))


def filter_kernel(
    cols, rows, parts, early, start_ref, levels_ref, beside_ref, before_ref, after_ref, *refs
):
    out_refs, (field, edge, once, once_edge, done, factor, factor_edge) = refs[:parts], refs[parts:]
    chunks = cols // tile
    part_rows = rows // parts
    factor[0:rows, :] = site_factor(levels_ref[...].astype(jnp.float32))
    factor[rows : rows + 1, :] = site_factor(before_ref[2 * chunks, 1:2, :])
    factor[rows + 1 : rows + 2, :] = site_factor(after_ref[2 * chunks, 0:1, :])
    for k in range(rows // tile):
        factor_edge[k * tile : (k + 1) * tile, :] = site_factor(unpack_edges(beside_ref[parts], k))
    for chunk in range(chunks):
        part = pl.ds(chunk * tile, tile)
        for row in range(rows):
            field[row + 1, part, :] = tile_at(start_ref, rows, row, chunk)
            edge[row + 1, part, :] = unpack_edges(
                beside_ref[row // part_rows], row % part_rows * chunks + chunk
            )
        field[0, part, :] = before_ref[chunks + chunk]
        field[rows + 1, part, :] = after_ref[chunk]
        edge[0, part, :] = unpack_edges(
            before_ref[2 * chunks + 2], (part_rows - 1) * chunks + chunk
        )
        edge[rows + 1, part, :] = unpack_edges(after_ref[2 * chunks + 1], chunk)
    for row in range(-1, rows + 1):
        here, beside = field[row + 1], edge[row + 1]
        if row == -1:
            vertical, where = field[1], rows
        elif row == rows:
            vertical, where = field[rows], rows + 1
        else:
            vertical, where = upward(row, field[row + 2], field[row]), row
        once[row + 1] = factor_at(factor, where, cols) * here - inverse * (
            sides(here, beside) + vertical
        )
        if 0 <= row < rows:
            vertical = upward(row, edge[row + 2], edge[row])
            once_edge[row] = factor_at(factor_edge, row, cols) * beside - inverse * (
                sides(beside, here) + vertical
            )
    for row in range(rows):
        here = once[row + 1]
        twice = factor_at(factor, row, cols) * here - inverse * (
            sides(here, once_edge[row]) + upward(row, once[row + 2], once[row])
        )
        done[row] = 2.0 * twice - field[row + 1]
    for k, out_ref in enumerate(out_refs):
        base = (lax.axis_index("col") ^ k) * part_rows
        if k not in early:
            out_ref[...] = done[pl.ds(base, part_rows)]
            continue
        for chunk in range(chunks):
            part = pl.ds(chunk * tile, tile)
            out_ref[chunk] = done[base, part, :]
            out_ref[chunks + chunk] = done[base + part_rows - 1, part, :]
        out_ref[2 * chunks] = pack_edges(
            done[base + row, chunk * tile : (chunk + 1) * tile, :]
            for row in range(part_rows)
            for chunk in range(chunks)
        )


def gram_kernel(cols, parts, early, levels_ref, *refs):
    late_refs, refs = refs[:parts], refs[parts:]
    raw_refs = dict(zip(early, refs))
    whole_ref, gram_ref, once, factor = refs[len(early) :]
    chunks = cols // tile
    part_rows = whole_ref.shape[0]
    total = cols * parts
    place = lax.axis_index("col")
    factor[...] = site_factor(levels_ref[...].astype(jnp.float32))
    lane = iota((cols, lanes), 1)
    outer_lanes = (lane < 2) | (lane >= lanes - 2)
    for k in range(parts):
        part = pl.ds(pl.multiple_of((place ^ k) * cols, tile), cols)
        late_ref = late_refs[k]
        if k not in early:
            whole_ref[:, part, :] = late_ref[...]
            continue
        raw_ref = raw_refs[k]
        base = place * part_rows
        for row in range(part_rows):
            above, below = raw_ref[min(row + 1, part_rows - 1)], raw_ref[max(row - 1, 0)]
            here = raw_ref[row]
            once[row] = factor_at(factor, base + row, cols) * here - inverse * (
                sides(here, here) + upward(row, above, below)
            )
        packed = late_ref[2 * chunks]
        for row in range(part_rows):
            if row in (0, part_rows - 1):
                at = 0 if row == 0 else chunks
                whole_ref[row, part, :] = jnp.concatenate(
                    [late_ref[at + chunk] for chunk in range(chunks)], axis=0
                )
                continue
            here = once[row]
            twice = factor_at(factor, base + row, cols) * here - inverse * (
                sides(here, here) + upward(row, once[row + 1], once[row - 1])
            )
            sent = jnp.concatenate(
                [unpack_edges(packed, row * chunks + chunk) for chunk in range(chunks)], axis=0
            )
            whole_ref[row, part, :] = jnp.where(outer_lanes, sent, 2.0 * twice - raw_ref[row])
    products = jnp.zeros((3 * total, 3 * total), jnp.float32)
    for row in range(0, part_rows, 2):
        values = jnp.concatenate([whole_ref[row], whole_ref[row + 1]], axis=1)
        stack = jnp.concatenate(split(values), axis=0)
        products += lax.dot_general(
            stack, stack, (((1,), (1,)), ((), ())), preferred_element_type=jnp.float32
        )
    gram = jnp.zeros((total, total), jnp.float32)
    for i in reversed(range(3)):
        for j in reversed(range(3)):
            gram += products[i * total : (i + 1) * total, j * total : (j + 1) * total]
    half = total // 2
    gram_ref[...] = jnp.concatenate([gram[:half], gram[half:]], axis=1)


def split(values):
    high = values.astype(jnp.bfloat16)
    rest = values - high.astype(jnp.float32)
    middle = rest.astype(jnp.bfloat16)
    low = (rest - middle.astype(jnp.float32)).astype(jnp.bfloat16)
    return high, middle, low


def solve_kernel(scale, whole_ref, gram_ref, other_ref, out_ref):
    part_rows, total, _ = whole_ref.shape
    blocks = total // tile
    half = total // 2
    packed = gram_ref[...] + other_ref[...]
    lane = iota((tile, lanes), 1)
    sub = iota((tile, lanes), 0)
    shape = (tile, lanes)
    work = []
    for i in range(blocks):
        at = i * tile % half
        block = packed[at : at + tile, :]
        if i * tile >= half:
            block = pltpu.roll(block, total, 1)
        unit = jnp.where(lane - total == sub + i * tile, 1.0, 0.0)
        work.append(jnp.where(lane < total, block, unit))
    for b in range(blocks):
        column = {
            i: [
                jnp.broadcast_to(work[i][:, b * tile + m : b * tile + m + 1], shape)
                for m in range(tile)
            ]
            for i in range(b, blocks)
        }
        for m in range(tile):
            pivot = jnp.broadcast_to(column[b][m][m : m + 1, :], shape)
            root = lax.rsqrt(pivot)
            root = root * (1.5 - 0.5 * (pivot * root) * root)
            row = jnp.broadcast_to(work[b][m : m + 1, :], shape) * root
            heads = [
                jnp.broadcast_to(column[b][p][m : m + 1, :], shape) * root
                for p in range(m + 1, tile)
            ]
            for i in range(b, blocks):
                ratio = column[i][m] * root
                if i == b:
                    ratio = jnp.where(sub > m, ratio, 0.0)
                    work[i] = jnp.where(sub == m, row, work[i] - ratio * row)
                else:
                    work[i] = work[i] - ratio * row
                for p in range(m + 1, tile):
                    column[i][p] = column[i][p] - ratio * heads[p - m - 1]
    solver = jnp.concatenate(work, axis=0) * scale
    wide = iota((total, lanes), 1)
    high, middle, low = (piece.astype(jnp.float32) for piece in split(solver))

    def pair(left, right):
        return jnp.where(wide < total, pltpu.roll(left, total, 1), right).astype(jnp.bfloat16)

    left_main = jnp.concatenate([pair(high, high), pair(middle, middle)], axis=1)
    left_rest = pair(high, low)
    for row in range(0, part_rows, 2):
        values = jnp.concatenate([whole_ref[row], whole_ref[row + 1]], axis=1)
        f_high, f_middle, f_low = split(values)
        right_main = jnp.concatenate([f_high, f_middle, f_high, f_middle], axis=0)
        right_rest = jnp.concatenate([f_low, f_high], axis=0)
        result = jnp.dot(left_rest, right_rest, preferred_element_type=jnp.float32) + jnp.dot(
            left_main, right_main, preferred_element_type=jnp.float32
        )
        out_ref[pl.ds(row, total, stride=part_rows), :] = result[:, :lanes]
        out_ref[pl.ds(row + 1, total, stride=part_rows), :] = result[:, lanes:]


def call(kernel, outs, *operands, scratch=()):
    return pl.pallas_call(
        kernel,
        out_shape=[jax.ShapeDtypeStruct(shape, jnp.float32) for shape in outs],
        scratch_shapes=[pltpu.VMEM(shape, jnp.float32) for shape in scratch],
        compiler_params=pltpu.CompilerParams(vmem_limit_bytes=32 * 1024 * 1024),
    )(*operands)


def exchange(values, axis, distance):
    count = lax.axis_size(axis)
    return lax.ppermute(values, axis, [(i, i ^ distance) for i in range(count)])


def shards(start, levels):
    cols, rows, _ = start.shape
    parts = lax.axis_size("col")
    chunks = cols // tile
    total = cols * parts
    part_rows = rows // parts
    sizes = (cols, rows, parts)
    early = (parts // 2,)
    flat = start.reshape(cols * rows, lanes)
    piece = (part_rows, cols, lanes)
    edges, outer, *raws = call(
        functools.partial(pack_kernel, *sizes, early),
        [(parts + 1, tile, lanes), (2 * chunks + 1, tile, lanes)] + [piece] * len(early),
        flat,
        levels,
    )
    count = lax.axis_size("ly")
    near = exchange(edges, "ly", 1)
    far_pairs = [(i, (i + 1) % count if i % 2 else (i - 1) % count) for i in range(count)]
    far = lax.ppermute(edges, "ly", far_pairs)
    raws = [exchange(values, "col", k) for k, values in zip(early, raws)]
    beside, outer = call(
        functools.partial(outer_kernel, parts),
        [(parts + 1, tile, lanes), (2 * chunks + 3, tile, lanes)],
        outer,
        near,
        far,
    )
    count = lax.axis_size("lx")
    before = lax.ppermute(outer, "lx", [(i, (i + 1) % count) for i in range(count)])
    after = before
    if count > 2:
        after = lax.ppermute(outer, "lx", [((i + 1) % count, i) for i in range(count)])
    lates = call(
        functools.partial(filter_kernel, *sizes, early),
        [(2 * chunks + 1, tile, lanes) if k in early else piece for k in range(parts)],
        flat,
        levels,
        beside,
        before,
        after,
        scratch=[
            (rows + 2, cols, lanes),
            (rows + 2, cols, lanes),
            (rows + 2, cols, lanes),
            (rows, cols, lanes),
            (rows, cols, lanes),
            (rows + tile, lanes),
            (rows, lanes),
        ],
    )
    lates = [exchange(values, "col", k) if k else values for k, values in enumerate(lates)]
    whole, gram = call(
        functools.partial(gram_kernel, cols, parts, early),
        [(part_rows, total, lanes), (total // 2, 2 * total)],
        levels,
        *lates,
        *raws,
        scratch=[piece, (rows, lanes)],
    )
    steps = []
    for axis in ("ly", "lx", "col"):
        bit = 1
        while bit < lax.axis_size(axis):
            steps.append((axis, bit))
            bit *= 2
    for axis, bit in steps[:-1]:
        gram = gram + exchange(gram, axis, bit)
    scale = math.sqrt(rows * lax.axis_size("lx") * lanes * lax.axis_size("ly"))
    (basis,) = call(
        functools.partial(solve_kernel, scale),
        [(total * part_rows, lanes)],
        whole,
        gram,
        exchange(gram, *steps[-1]),
    )
    return basis.reshape(total, part_rows, lanes)


def solution(mesh):
    placed = (P("col", "lx", "ly"), P("lx", "ly"))
    return jax.shard_map(
        shards, mesh=mesh, in_specs=placed, out_specs=P(None, ("lx", "col"), "ly"), check_vma=False
    )
```

time: 47.5 us -> 45.7 us (0.962)
  waiting for transfers between devices: 22.5 us -> 20.3 us
    ppermute x1, waiting for transfers between devices: 2.17 us -> 0.01 us  [shards(): lax.ppermute(outer, 'lx', [(i, (i + 1) % count) for i in range(count)])]
    ppermute x1, starting transfers between devices: 1.72 us -> 2.43 us  [shards(): lax.ppermute(outer, 'lx', [(i, (i + 1) % count) for i in range(count)])]
    ppermute x1, waiting for transfers between devices: 1.47 us -> 0.84 us  [shards(): far = lax.ppermute(edges, 'ly', far_pairs)]
    ppermute x9 -> x10, waiting for transfers between devices: 18.9 us -> 19.5 us  [exchange(): return lax.ppermute(values, axis, [(i, i ^ distance) for i in range(count)])]
    ppermute x9 -> x10, starting transfers between devices: 13 us -> 12.4 us  [exchange(): return lax.ppermute(values, axis, [(i, i ^ distance) for i in range(count)])]
    pallas_call x4 -> x5, Pallas kernels: 5.58 us -> 5.99 us  [call(): pl.pallas_call(kernel, out_shape=[jax.ShapeDtypeStruct(shape, jnp.float32...]
  transfers between devices with their start and end apart: 11 -> 12, of which waited for: 9 -> 7; matrix products, arithmetic and copies ran while one was open for 0% -> 0% of each run, Pallas kernels for 0% -> 3%
where the time goes in v3:
time: 45.7 us; the launch traced here: 45.5 us
  waiting for transfers between devices  20.3 us (44%)
  starting transfers between devices  17.3 us (38%)
  Pallas kernels  5.99 us (13%)
  local copies, waits for them, and re-layouts  1.81 us (4%)
    ppermute x10, waiting for transfers between devices, exchange(): return lax.ppermute(values, axis, [(i, i ^ distance) for i in range(count)])  19.5 us
    ppermute x10, starting transfers between devices, exchange(): return lax.ppermute(values, axis, [(i, i ^ distance) for i in range(count)])  12.4 us
    pallas_call x5, Pallas kernels, call(): pl.pallas_call(kernel, out_shape=[jax.ShapeDtypeStruct(shape, jnp.float32...  5.99 us
    ppermute x1, starting transfers between devices, shards(): far = lax.ppermute(edges, 'ly', far_pairs)  2.47 us
    ppermute x1, starting transfers between devices, shards(): lax.ppermute(outer, 'lx', [(i, (i + 1) % count) for i in range(count)])  2.43 us
    unnamed x8, local copies, waits for them, and re-layouts  1.81 us
  transfers between devices with their start and end apart: 12, of which 7 were waited for; matrix products, arithmetic and copies ran while one was open for 0% of the time, Pallas kernels for 3%

profile of v3, /device:TPU:0, one launch (start us, length us, event | category | flops | bytes accessed | tf_op | source)
XLA Modules:
  0.0 45.5 jit_solution(4400426841801012953)
XLA Ops:
  0.0 1.0 %copy-done = f32[16,64,128]{2,1,0:T(8,128)S(1)} copy-done((f32[16,64,128]{2,1,0:T(8,128)S(1)}, f32[16,64,128]{2,1,0:T(8,128)}, u32[]{:S(2)}) %copy-start) | copy-done | bytes 524312
  1.0 0.8 %copy-done.2 = s32[64,128]{1,0:T(8,128)S(1)} copy-done((s32[64,128]{1,0:T(8,128)S(1)}, s32[64,128]{1,0:T(8,128)}, u32[]{:S(2)}) %copy-start.2) | copy-done | bytes 32792
  1.8 0.4 shard_map.28
  2.2 2.5 %collective-permute-start.1 = (f32[5,8,128]{2,1,0:T(8,128)S(1)}, f32[5,8,128]{2,1,0:T(8,128)S(1)}, u32[]{:S(2)}, u32[]{:S(2)}) collective-permute-start(f32[5,8,128]{2,1,0:T(8,128)S(1)} %get-tuple-element.17), channel_id=1, source_target_pairs={{0,12},{4,8},{8,4},{12,0},{1,13},{5,9},{9,5},{13,1},{2,14},{6,10},... | collective-permute-start | bytes 61448 | tf_op jit(solution)/shard_map/ppermute | solution.py:333
  4.7 0.7 %collective-permute-start = (f32[5,8,128]{2,1,0:T(8,128)S(1)}, f32[5,8,128]{2,1,0:T(8,128)S(1)}, u32[]{:S(2)}, u32[]{:S(2)}) collective-permute-start(f32[5,8,128]{2,1,0:T(8,128)S(1)} %get-tuple-element.17), channel_id=1, source_target_pairs={{0,4},{4,0},{8,12},{12,8},{1,5},{5,1},{9,13},{13,9},{2,6},{6,2},{1... | collective-permute-start | bytes 61448 | tf_op jit(solution)/shard_map/ppermute | solution.py:311
  5.3 0.8 %collective-permute-done.1.far_ref = f32[5,8,128]{2,1,0:T(8,128)S(1)} collective-permute-done((f32[5,8,128]{2,1,0:T(8,128)S(1)}, f32[5,8,128]{2,1,0:T(8,128)S(1)}, u32[]{:S(2)}, u32[]{:S(2)}) %collective-permute-start.1) | collective-permute-done | bytes 20512 | tf_op jit(solution)/shard_map/ppermute | solution.py:333
  6.2 0.0 collective-permute-done.near_ref
  6.2 2.4 %collective-permute-start.2 = (f32[7,8,128]{2,1,0:T(8,128)S(1)}, f32[7,8,128]{2,1,0:T(8,128)S(1)}, u32[]{:S(2)}, u32[]{:S(2)}) collective-permute-start(f32[7,8,128]{2,1,0:T(8,128)S(1)} %get-tuple-element.19), channel_id=1, source_target_pairs={{0,16},{16,0},{1,17},{17,1},{2,18},{18,2},{3,19},{19,3},{4,20},{20... | collective-permute-start | bytes 86024 | tf_op jit(solution)/shard_map/ppermute | solution.py:343
  8.6 2.6 %collective-permute-start.6 = (f32[16,16,128]{2,1,0:T(8,128)S(1)}, f32[16,16,128]{2,1,0:T(8,128)S(1)}, u32[]{:S(2)}, u32[]{:S(2)}) collective-permute-start(f32[16,16,128]{2,1,0:T(8,128)S(1)} %get-tuple-element.24), channel_id=1, source_target_pairs={{0,2},{1,3},{2,0},{3,1},{4,6},{5,7},{6,4},{7,5},{8,10},{9,11},{10,... | collective-permute-start | bytes 393224 | tf_op jit(solution)/shard_map/ppermute | solution.py:311
  11.2 0.0 collective-permute-done.2.before_ref.after_ref
  11.2 0.0 copy-done.1
  11.2 1.3 %shard_map.30 = (f32[16,16,128]{2,1,0:T(8,128)S(1)}, f32[16,16,128]{2,1,0:T(8,128)S(1)}, f32[5,8,128]{2,1,0:T(8,128)S(1)}, f32[16,16,128]{2,1,0:T(8,128)S(1)}) custom-call(f32[1024,128]{1,0:T(8,128)S(1)} %bitcast.3, s32[64,128]{1,0:T(8,128)S(1)} %copy-done.2, f32[5,8,128]{2,1,0:T(8,128)S(1)} %get-tuple-element.18.beside_ref, ...), custom_call_target="tpu_custom_call" | custom-call | tf_op jit(solution)/shard_map/pallas_call | solution.py:301
  12.5 1.6 %collective-permute-start.3 = (f32[16,16,128]{2,1,0:T(8,128)S(1)}, f32[16,16,128]{2,1,0:T(8,128)S(1)}, u32[]{:S(2)}, u32[]{:S(2)}) collective-permute-start(f32[16,16,128]{2,1,0:T(8,128)S(1)} %get-tuple-element.21), channel_id=1, source_target_pairs={{0,1},{1,0},{2,3},{3,2},{4,5},{5,4},{6,7},{7,6},{8,9},{9,8},{10,11... | collective-permute-start | bytes 393224 | tf_op jit(solution)/shard_map/ppermute | solution.py:311
  14.1 2.3 %collective-permute-start.5 = (f32[16,16,128]{2,1,0:T(8,128)S(1)}, f32[16,16,128]{2,1,0:T(8,128)S(1)}, u32[]{:S(2)}, u32[]{:S(2)}) collective-permute-start(f32[16,16,128]{2,1,0:T(8,128)S(1)} %get-tuple-element.23), channel_id=1, source_target_pairs={{0,3},{1,2},{2,1},{3,0},{4,7},{5,6},{6,5},{7,4},{8,11},{9,10},{10,... | collective-permute-start | bytes 393224 | tf_op jit(solution)/shard_map/ppermute | solution.py:311
  16.4 0.1 collective-permute-start.4
  16.6 7.5 %collective-permute-done.4.refs_2_ = f32[5,8,128]{2,1,0:T(8,128)S(1)} collective-permute-done((f32[5,8,128]{2,1,0:T(8,128)S(1)}, f32[5,8,128]{2,1,0:T(8,128)S(1)}, u32[]{:S(2)}, u32[]{:S(2)}) %collective-permute-start.4) | collective-permute-done | bytes 20512 | tf_op jit(solution)/shard_map/ppermute | solution.py:311
  24.1 0.0 collective-permute-done.6.refs_4_
  24.1 0.0 collective-permute-done.3.refs_1_
  24.1 0.0 collective-permute-done.5.refs_3_
  24.1 0.0 copy-done.3
  24.1 0.8 %shard_map.31 = (f32[16,64,128]{2,1,0:T(8,128)S(1)}, f32[32,128]{1,0:T(8,128)S(1)}) custom-call(s32[64,128]{1,0:T(8,128)S(1)} %copy-done.3, f32[16,16,128]{2,1,0:T(8,128)S(1)} %get-tuple-element.20.refs_0_, f32[16,16,128]{2,1,0:T(8,128)S(1)} %collective-permute-done.3.refs_1_, f32[5,8,128]{2,1,0:T(8,128)S(1)} %collective-permute-done.4.refs_2_, ...), custom_call_target="tpu_custom_call" | custom-call | tf_op jit(solution)/shard_map/pallas_call | solution.py:301
  24.9 0.0 collective-permute-start.7
  24.9 1.2 %collective-permute-done.7 = f32[32,128]{1,0:T(8,128)S(1)} collective-permute-done((f32[32,128]{1,0:T(8,128)S(1)}, f32[32,128]{1,0:T(8,128)S(1)}, u32[]{:S(2)}, u32[]{:S(2)}) %collective-permute-start.7) | collective-permute-done | bytes 16416 | tf_op jit(solution)/shard_map/ppermute | solution.py:311
  26.1 1.6 %collective-permute-start.8 = (f32[32,128]{1,0:T(8,128)S(1)}, f32[32,128]{1,0:T(8,128)S(1)}, u32[]{:S(2)}, u32[]{:S(2)}) collective-permute-start(f32[32,128]{1,0:T(8,128)S(1)} %add.12), channel_id=1, source_target_pairs={{0,8},{4,12},{8,0},{12,4},{1,9},{5,13},{9,1},{13,5},{2,10},{6,14},... | collective-permute-start | bytes 49160 | tf_op jit(solution)/shard_map/ppermute | solution.py:311
  27.7 2.2 %collective-permute-done.8 = f32[32,128]{1,0:T(8,128)S(1)} collective-permute-done((f32[32,128]{1,0:T(8,128)S(1)}, f32[32,128]{1,0:T(8,128)S(1)}, u32[]{:S(2)}, u32[]{:S(2)}) %collective-permute-start.8) | collective-permute-done | bytes 16416 | tf_op jit(solution)/shard_map/ppermute | solution.py:311
  29.8 0.5 %collective-permute-start.9 = (f32[32,128]{1,0:T(8,128)S(1)}, f32[32,128]{1,0:T(8,128)S(1)}, u32[]{:S(2)}, u32[]{:S(2)}) collective-permute-start(f32[32,128]{1,0:T(8,128)S(1)} %add.13), channel_id=1, source_target_pairs={{0,16},{16,0},{1,17},{17,1},{2,18},{18,2},{3,19},{19,3},{4,20},{20... | collective-permute-start | bytes 49160 | tf_op jit(solution)/shard_map/ppermute | solution.py:311
  30.4 3.2 %collective-permute-done.9 = f32[32,128]{1,0:T(8,128)S(1)} collective-permute-done((f32[32,128]{1,0:T(8,128)S(1)}, f32[32,128]{1,0:T(8,128)S(1)}, u32[]{:S(2)}, u32[]{:S(2)}) %collective-permute-start.9) | collective-permute-done | bytes 16416 | tf_op jit(solution)/shard_map/ppermute | solution.py:311
  33.6 0.7 %collective-permute-start.10 = (f32[32,128]{1,0:T(8,128)S(1)}, f32[32,128]{1,0:T(8,128)S(1)}, u32[]{:S(2)}, u32[]{:S(2)}) collective-permute-start(f32[32,128]{1,0:T(8,128)S(1)} %add.14), channel_id=1, source_target_pairs={{0,1},{1,0},{2,3},{3,2},{4,5},{5,4},{6,7},{7,6},{8,9},{9,8},{10,11... | collective-permute-start | bytes 49160 | tf_op jit(solution)/shard_map/ppermute | solution.py:311
  34.3 3.0 %collective-permute-done.10 = f32[32,128]{1,0:T(8,128)S(1)} collective-permute-done((f32[32,128]{1,0:T(8,128)S(1)}, f32[32,128]{1,0:T(8,128)S(1)}, u32[]{:S(2)}, u32[]{:S(2)}) %collective-permute-start.10) | collective-permute-done | bytes 16416 | tf_op jit(solution)/shard_map/ppermute | solution.py:311
  37.3 2.3 %collective-permute-start.11 = (f32[32,128]{1,0:T(8,128)S(1)}, f32[32,128]{1,0:T(8,128)S(1)}, u32[]{:S(2)}, u32[]{:S(2)}) collective-permute-start(f32[32,128]{1,0:T(8,128)S(1)} %add.15.gram_ref), channel_id=1, source_target_pairs={{0,2},{1,3},{2,0},{3,1},{4,6},{5,7},{6,4},{7,5},{8,10},{9,11},{10,... | collective-permute-start | bytes 49160 | tf_op jit(solution)/shard_map/ppermute | solution.py:311
  39.6 2.4 %collective-permute-done.11.other_ref = f32[32,128]{1,0:T(8,128)S(1)} collective-permute-done((f32[32,128]{1,0:T(8,128)S(1)}, f32[32,128]{1,0:T(8,128)S(1)}, u32[]{:S(2)}, u32[]{:S(2)}) %collective-permute-start.11) | collective-permute-done | bytes 16416 | tf_op jit(solution)/shard_map/ppermute | solution.py:311
  42.0 3.6 %shard_map.32 = f32[1024,128]{1,0:T(8,128)} custom-call(f32[16,64,128]{2,1,0:T(8,128)S(1)} %get-tuple-element.25.whole_ref, f32[32,128]{1,0:T(8,128)S(1)} %add.15.gram_ref, f32[32,128]{1,0:T(8,128)S(1)} %collective-permute-done.11.other_ref), custom_call_target="tpu_custom_call" | custom-call | tf_op jit(solution)/shard_map/pallas_call | solution.py:301
  (9 shorter events, 0.0 us)
Async XLA Ops:
  0.0 1.0 %copy-start = (f32[16,64,128]{2,1,0:T(8,128)S(1)}, f32[16,64,128]{2,1,0:T(8,128)}, u32[]{:S(2)}) copy-start(f32[16,64,128]{2,1,0:T(8,128)} %param.2) | copy-start | bytes 1572868
  1.0 0.8 %copy-start.2 = (s32[64,128]{1,0:T(8,128)S(1)}, s32[64,128]{1,0:T(8,128)}, u32[]{:S(2)}) copy-start(s32[64,128]{1,0:T(8,128)} %levels_ref.5) | copy-start | bytes 98308
  1.8 9.4 %copy-start.1 = (f32[16,64,128]{2,1,0:T(8,128)S(1)}, f32[16,64,128]{2,1,0:T(8,128)}, u32[]{:S(2)}) copy-start(f32[16,64,128]{2,1,0:T(8,128)} %param.2) | copy-start | bytes 1572868
  2.2 4.0 %collective-permute-start.1 = (f32[5,8,128]{2,1,0:T(8,128)S(1)}, f32[5,8,128]{2,1,0:T(8,128)S(1)}, u32[]{:S(2)}, u32[]{:S(2)}) collective-permute-start(f32[5,8,128]{2,1,0:T(8,128)S(1)} %get-tuple-element.17), channel_id=1, source_target_pairs={{0,12},{4,8},{8,4},{12,0},{1,13},{5,9},{9,5},{13,1},{2,14},{6,10},... | collective-permute-start | bytes 61448 | tf_op jit(solution)/shard_map/ppermute | solution.py:333
  4.7 1.5 %collective-permute-start = (f32[5,8,128]{2,1,0:T(8,128)S(1)}, f32[5,8,128]{2,1,0:T(8,128)S(1)}, u32[]{:S(2)}, u32[]{:S(2)}) collective-permute-start(f32[5,8,128]{2,1,0:T(8,128)S(1)} %get-tuple-element.17), channel_id=1, source_target_pairs={{0,4},{4,0},{8,12},{12,8},{1,5},{5,1},{9,13},{13,9},{2,6},{6,2},{1... | collective-permute-start | bytes 61448 | tf_op jit(solution)/shard_map/ppermute | solution.py:311
  6.2 5.0 %collective-permute-start.2 = (f32[7,8,128]{2,1,0:T(8,128)S(1)}, f32[7,8,128]{2,1,0:T(8,128)S(1)}, u32[]{:S(2)}, u32[]{:S(2)}) collective-permute-start(f32[7,8,128]{2,1,0:T(8,128)S(1)} %get-tuple-element.19), channel_id=1, source_target_pairs={{0,16},{16,0},{1,17},{17,1},{2,18},{18,2},{3,19},{19,3},{4,20},{20... | collective-permute-start | bytes 86024 | tf_op jit(solution)/shard_map/ppermute | solution.py:343
  8.6 15.4 %collective-permute-start.6 = (f32[16,16,128]{2,1,0:T(8,128)S(1)}, f32[16,16,128]{2,1,0:T(8,128)S(1)}, u32[]{:S(2)}, u32[]{:S(2)}) collective-permute-start(f32[16,16,128]{2,1,0:T(8,128)S(1)} %get-tuple-element.24), channel_id=1, source_target_pairs={{0,2},{1,3},{2,0},{3,1},{4,6},{5,7},{6,4},{7,5},{8,10},{9,11},{10,... | collective-permute-start | bytes 393224 | tf_op jit(solution)/shard_map/ppermute | solution.py:311
  11.2 12.9 %copy-start.3 = (s32[64,128]{1,0:T(8,128)S(1)}, s32[64,128]{1,0:T(8,128)}, u32[]{:S(2)}) copy-start(s32[64,128]{1,0:T(8,128)} %levels_ref.5) | copy-start | bytes 98308
  12.5 11.6 %collective-permute-start.3 = (f32[16,16,128]{2,1,0:T(8,128)S(1)}, f32[16,16,128]{2,1,0:T(8,128)S(1)}, u32[]{:S(2)}, u32[]{:S(2)}) collective-permute-start(f32[16,16,128]{2,1,0:T(8,128)S(1)} %get-tuple-element.21), channel_id=1, source_target_pairs={{0,1},{1,0},{2,3},{3,2},{4,5},{5,4},{6,7},{7,6},{8,9},{9,8},{10,11... | collective-permute-start | bytes 393224 | tf_op jit(solution)/shard_map/ppermute | solution.py:311
  14.1 9.9 %collective-permute-start.5 = (f32[16,16,128]{2,1,0:T(8,128)S(1)}, f32[16,16,128]{2,1,0:T(8,128)S(1)}, u32[]{:S(2)}, u32[]{:S(2)}) collective-permute-start(f32[16,16,128]{2,1,0:T(8,128)S(1)} %get-tuple-element.23), channel_id=1, source_target_pairs={{0,3},{1,2},{2,1},{3,0},{4,7},{5,6},{6,5},{7,4},{8,11},{9,10},{10,... | collective-permute-start | bytes 393224 | tf_op jit(solution)/shard_map/ppermute | solution.py:311
  16.4 7.7 %collective-permute-start.4 = (f32[5,8,128]{2,1,0:T(8,128)S(1)}, f32[5,8,128]{2,1,0:T(8,128)S(1)}, u32[]{:S(2)}, u32[]{:S(2)}) collective-permute-start(f32[5,8,128]{2,1,0:T(8,128)S(1)} %get-tuple-element.22), channel_id=1, source_target_pairs={{0,2},{1,3},{2,0},{3,1},{4,6},{5,7},{6,4},{7,5},{8,10},{9,11},{10,... | collective-permute-start | bytes 61448 | tf_op jit(solution)/shard_map/ppermute | solution.py:311
  24.9 1.2 %collective-permute-start.7 = (f32[32,128]{1,0:T(8,128)S(1)}, f32[32,128]{1,0:T(8,128)S(1)}, u32[]{:S(2)}, u32[]{:S(2)}) collective-permute-start(f32[32,128]{1,0:T(8,128)S(1)} %get-tuple-element.26), channel_id=1, source_target_pairs={{0,4},{4,0},{8,12},{12,8},{1,5},{5,1},{9,13},{13,9},{2,6},{6,2},{1... | collective-permute-start | bytes 49160 | tf_op jit(solution)/shard_map/ppermute | solution.py:311
  26.1 3.7 %collective-permute-start.8 = (f32[32,128]{1,0:T(8,128)S(1)}, f32[32,128]{1,0:T(8,128)S(1)}, u32[]{:S(2)}, u32[]{:S(2)}) collective-permute-start(f32[32,128]{1,0:T(8,128)S(1)} %add.12), channel_id=1, source_target_pairs={{0,8},{4,12},{8,0},{12,4},{1,9},{5,13},{9,1},{13,5},{2,10},{6,14},... | collective-permute-start | bytes 49160 | tf_op jit(solution)/shard_map/ppermute | solution.py:311
  29.8 3.7 %collective-permute-start.9 = (f32[32,128]{1,0:T(8,128)S(1)}, f32[32,128]{1,0:T(8,128)S(1)}, u32[]{:S(2)}, u32[]{:S(2)}) collective-permute-start(f32[32,128]{1,0:T(8,128)S(1)} %add.13), channel_id=1, source_target_pairs={{0,16},{16,0},{1,17},{17,1},{2,18},{18,2},{3,19},{19,3},{4,20},{20... | collective-permute-start | bytes 49160 | tf_op jit(solution)/shard_map/ppermute | solution.py:311
  33.6 3.7 %collective-permute-start.10 = (f32[32,128]{1,0:T(8,128)S(1)}, f32[32,128]{1,0:T(8,128)S(1)}, u32[]{:S(2)}, u32[]{:S(2)}) collective-permute-start(f32[32,128]{1,0:T(8,128)S(1)} %add.14), channel_id=1, source_target_pairs={{0,1},{1,0},{2,3},{3,2},{4,5},{5,4},{6,7},{7,6},{8,9},{9,8},{10,11... | collective-permute-start | bytes 49160 | tf_op jit(solution)/shard_map/ppermute | solution.py:311
  37.3 4.6 %collective-permute-start.11 = (f32[32,128]{1,0:T(8,128)S(1)}, f32[32,128]{1,0:T(8,128)S(1)}, u32[]{:S(2)}, u32[]{:S(2)}) collective-permute-start(f32[32,128]{1,0:T(8,128)S(1)} %add.15.gram_ref), channel_id=1, source_target_pairs={{0,2},{1,3},{2,0},{3,1},{4,6},{5,7},{6,4},{7,5},{8,10},{9,11},{10,... | collective-permute-start | bytes 49160 | tf_op jit(solution)/shard_map/ppermute | solution.py:311

commit v4 on v3

--- a/solution.py
+++ b/solution.py
@@ -42,9 +42,18 @@
     return pltpu.roll(packed, lanes - (4 * k + 2), 1)
 
 
-def pack_kernel(cols, rows, parts, early, start_ref, levels_ref, edges_ref, outer_ref, *piece_refs):
-    chunks = cols // tile
-    part_rows = rows // parts
+def pack_kernel(cols, rows, parts, early, start_hbm, levels_hbm, edges_ref, outer_ref, *refs):
+    piece_refs, (start_ref, levels_ref, arrived) = refs[: len(early)], refs[len(early) :]
+    chunks = cols // tile
+    part_rows = rows // parts
+    copies = [
+        pltpu.make_async_copy(start_hbm, start_ref, arrived.at[0]),
+        pltpu.make_async_copy(levels_hbm, levels_ref, arrived.at[1]),
+    ]
+    for copy in copies:
+        copy.start()
+    for copy in copies:
+        copy.wait()
     for group in range(parts):
         edges_ref[group] = pack_edges(
             tile_at(start_ref, rows, group * part_rows + row, chunk)
@@ -108,66 +117,141 @@
     return jnp.broadcast_to(ref[pl.ds(row, 1), :], (height, lanes))
 
 
-def filter_kernel(
-    cols, rows, parts, early, start_ref, levels_ref, beside_ref, before_ref, after_ref, *refs
+def inner_kernel(
+    cols, rows, parts, early, start_ref, levels_ref, beside_ref, done_ref, next_ref, packed_ref, *refs
 ):
-    out_refs, (field, edge, once, once_edge, done, factor, factor_edge) = refs[:parts], refs[parts:]
-    chunks = cols // tile
-    part_rows = rows // parts
-    factor[0:rows, :] = site_factor(levels_ref[...].astype(jnp.float32))
-    factor[rows : rows + 1, :] = site_factor(before_ref[2 * chunks, 1:2, :])
-    factor[rows + 1 : rows + 2, :] = site_factor(after_ref[2 * chunks, 0:1, :])
+    field, edge, once, once_edge, factor, factor_edge = refs
+    chunks = cols // tile
+    part_rows = rows // parts
+    factor[...] = site_factor(levels_ref[...].astype(jnp.float32))
     for k in range(rows // tile):
         factor_edge[k * tile : (k + 1) * tile, :] = site_factor(unpack_edges(beside_ref[parts], k))
-    for chunk in range(chunks):
-        part = pl.ds(chunk * tile, tile)
-        for row in range(rows):
-            field[row + 1, part, :] = tile_at(start_ref, rows, row, chunk)
-            edge[row + 1, part, :] = unpack_edges(
+    for row in range(rows):
+        for chunk in range(chunks):
+            part = pl.ds(chunk * tile, tile)
+            field[row, part, :] = tile_at(start_ref, rows, row, chunk)
+            edge[row, part, :] = unpack_edges(
                 beside_ref[row // part_rows], row % part_rows * chunks + chunk
             )
-        field[0, part, :] = before_ref[chunks + chunk]
-        field[rows + 1, part, :] = after_ref[chunk]
-        edge[0, part, :] = unpack_edges(
-            before_ref[2 * chunks + 2], (part_rows - 1) * chunks + chunk
-        )
-        edge[rows + 1, part, :] = unpack_edges(after_ref[2 * chunks + 1], chunk)
-    for row in range(-1, rows + 1):
-        here, beside = field[row + 1], edge[row + 1]
-        if row == -1:
-            vertical, where = field[1], rows
-        elif row == rows:
-            vertical, where = field[rows], rows + 1
+    for row in range(rows):
+        here, beside = field[row], edge[row]
+        up, down = min(row + 1, rows - 1), max(row - 1, 0)
+        once[row] = factor_at(factor, row, cols) * here - inverse * (
+            sides(here, beside) + upward(row, field[up], field[down])
+        )
+        once_edge[row] = factor_at(factor_edge, row, cols) * beside - inverse * (
+            sides(beside, here) + upward(row, edge[up], edge[down])
+        )
+    for row in range(1, rows - 1):
+        here = once[row]
+        twice = factor_at(factor, row, cols) * here - inverse * (
+            sides(here, once_edge[row]) + upward(row, once[row + 1], once[row - 1])
+        )
+        done_ref[row] = 2.0 * twice - field[row]
+    done_ref[0] = once[0]
+    done_ref[rows - 1] = once[rows - 1]
+    next_ref[0] = once[1]
+    next_ref[1] = once[rows - 2]
+    for at, k in enumerate(early):
+        base = (lax.axis_index("col") ^ k) * part_rows
+        packed_ref[at] = pack_edges(
+            done_ref[base + row, chunk * tile : (chunk + 1) * tile, :]
+            for row in range(part_rows)
+            for chunk in range(chunks)
+        )
+
+
+def outer_rows(cols, rows, start_ref, levels_ref, beside_ref, parts, before_ref, after_ref, next_ref):
+    chunks = cols // tile
+    part_rows = rows // parts
+
+    def joined(tiles):
+        return jnp.concatenate(list(tiles), axis=0)
+
+    def field(row):
+        return joined(tile_at(start_ref, rows, row, chunk) for chunk in range(chunks))
+
+    def edge(row):
+        return joined(
+            unpack_edges(beside_ref[row // part_rows], row % part_rows * chunks + chunk)
+            for chunk in range(chunks)
+        )
+
+    def factor(values):
+        return jnp.broadcast_to(site_factor(values), (cols, lanes))
+
+    for outer in (0, 1):
+        if outer == 0:
+            row, inside = 0, 1
+            field_out = joined(before_ref[chunks + chunk] for chunk in range(chunks))
+            edge_out = joined(
+                unpack_edges(before_ref[2 * chunks + 2], (part_rows - 1) * chunks + chunk)
+                for chunk in range(chunks)
+            )
+            factor_out = factor(before_ref[2 * chunks, 1:2, :])
         else:
-            vertical, where = upward(row, field[row + 2], field[row]), row
-        once[row + 1] = factor_at(factor, where, cols) * here - inverse * (
-            sides(here, beside) + vertical
-        )
-        if 0 <= row < rows:
-            vertical = upward(row, edge[row + 2], edge[row])
-            once_edge[row] = factor_at(factor_edge, row, cols) * beside - inverse * (
-                sides(beside, here) + vertical
-            )
-    for row in range(rows):
-        here = once[row + 1]
-        twice = factor_at(factor, row, cols) * here - inverse * (
-            sides(here, once_edge[row]) + upward(row, once[row + 2], once[row])
-        )
-        done[row] = 2.0 * twice - field[row + 1]
+            row, inside = rows - 1, rows - 2
+            field_out = joined(after_ref[chunk] for chunk in range(chunks))
+            edge_out = joined(
+                unpack_edges(after_ref[2 * chunks + 1], chunk) for chunk in range(chunks)
+            )
+            factor_out = factor(after_ref[2 * chunks, 0:1, :])
+
+        def vertical(within, without):
+            return upward(row, *((within, without) if outer == 0 else (without, within)))
+
+        here, beside = field(row), edge(row)
+        here_factor = factor(levels_ref[row : row + 1, :].astype(jnp.float32))
+        levels_edge = unpack_edges(beside_ref[parts], row // tile)
+        edge_factor = factor(levels_edge[row % tile : row % tile + 1, :])
+        once = here_factor * here - inverse * (
+            sides(here, beside) + vertical(field(inside), field_out)
+        )
+        once_edge = edge_factor * beside - inverse * (
+            sides(beside, here) + vertical(edge(inside), edge_out)
+        )
+        once_out = factor_out * field_out - inverse * (sides(field_out, edge_out) + here)
+        twice = here_factor * once - inverse * (
+            sides(once, once_edge) + vertical(next_ref[outer], once_out)
+        )
+        yield 2.0 * twice - here
+
+
+def late_kernel(
+    cols,
+    rows,
+    parts,
+    early,
+    start_ref,
+    levels_ref,
+    beside_ref,
+    done_ref,
+    next_ref,
+    packed_ref,
+    before_ref,
+    after_ref,
+    *out_refs,
+):
+    chunks = cols // tile
+    part_rows = rows // parts
+    first, last = outer_rows(
+        cols, rows, start_ref, levels_ref, beside_ref, parts, before_ref, after_ref, next_ref
+    )
     for k, out_ref in enumerate(out_refs):
-        base = (lax.axis_index("col") ^ k) * part_rows
+        target = lax.axis_index("col") ^ k
+        base = target * part_rows
+        top = jnp.where(target == 0, first, done_ref[base])
+        bottom = jnp.where(target == parts - 1, last, done_ref[base + part_rows - 1])
         if k not in early:
-            out_ref[...] = done[pl.ds(base, part_rows)]
+            out_ref[0] = top
+            out_ref[1 : part_rows - 1] = done_ref[pl.ds(base + 1, part_rows - 2)]
+            out_ref[part_rows - 1] = bottom
             continue
         for chunk in range(chunks):
-            part = pl.ds(chunk * tile, tile)
-            out_ref[chunk] = done[base, part, :]
-            out_ref[chunks + chunk] = done[base + part_rows - 1, part, :]
-        out_ref[2 * chunks] = pack_edges(
-            done[base + row, chunk * tile : (chunk + 1) * tile, :]
-            for row in range(part_rows)
-            for chunk in range(chunks)
-        )
+            part = slice(chunk * tile, (chunk + 1) * tile)
+            out_ref[chunk] = top[part]
+            out_ref[chunks + chunk] = bottom[part]
+        out_ref[2 * chunks] = packed_ref[early.index(k)]
 
 
 def gram_kernel(cols, parts, early, levels_ref, *refs):
@@ -261,7 +345,6 @@
         for m in range(tile):
             pivot = jnp.broadcast_to(column[b][m][m : m + 1, :], shape)
             root = lax.rsqrt(pivot)
-            root = root * (1.5 - 0.5 * (pivot * root) * root)
             row = jnp.broadcast_to(work[b][m : m + 1, :], shape) * root
             heads = [
                 jnp.broadcast_to(column[b][p][m : m + 1, :], shape) * root
@@ -297,12 +380,16 @@
         out_ref[pl.ds(row + 1, total, stride=part_rows), :] = result[:, lanes:]
 
 
-def call(kernel, outs, *operands, scratch=()):
+def call(kernel, outs, *operands, scratch=(), limit=32, **specs):
     return pl.pallas_call(
         kernel,
         out_shape=[jax.ShapeDtypeStruct(shape, jnp.float32) for shape in outs],
-        scratch_shapes=[pltpu.VMEM(shape, jnp.float32) for shape in scratch],
-        compiler_params=pltpu.CompilerParams(vmem_limit_bytes=32 * 1024 * 1024),
+        scratch_shapes=[
+            pltpu.VMEM(shape, jnp.float32) if isinstance(shape, tuple) else shape
+            for shape in scratch
+        ],
+        compiler_params=pltpu.CompilerParams(vmem_limit_bytes=limit * 1024 * 1024),
+        **specs,
     )(*operands)
 
 
@@ -324,8 +411,15 @@
     edges, outer, *raws = call(
         functools.partial(pack_kernel, *sizes, early),
         [(parts + 1, tile, lanes), (2 * chunks + 1, tile, lanes)] + [piece] * len(early),
-        flat,
-        levels,
+        pltpu.with_memory_space_constraint(flat, pltpu.HBM),
+        pltpu.with_memory_space_constraint(levels, pltpu.HBM),
+        scratch=[
+            flat.shape,
+            pltpu.VMEM(levels.shape, levels.dtype),
+            pltpu.SemaphoreType.DMA((2,)),
+        ],
+        limit=32,
+        in_specs=[pl.BlockSpec(memory_space=pl.ANY)] * 2,
     )
     count = lax.axis_size("ly")
     near = exchange(edges, "ly", 1)
@@ -344,23 +438,24 @@
     after = before
     if count > 2:
         after = lax.ppermute(outer, "lx", [((i + 1) % count, i) for i in range(count)])
+    inner = call(
+        functools.partial(inner_kernel, *sizes, early),
+        [(rows, cols, lanes), (2, cols, lanes), (len(early), tile, lanes)],
+        flat,
+        levels,
+        beside,
+        scratch=[(rows, cols, lanes)] * 4 + [(rows, lanes)] * 2,
+        cost_estimate=pl.CostEstimate(flops=10**11, bytes_accessed=10**9, transcendentals=0),
+    )
     lates = call(
-        functools.partial(filter_kernel, *sizes, early),
+        functools.partial(late_kernel, *sizes, early),
         [(2 * chunks + 1, tile, lanes) if k in early else piece for k in range(parts)],
         flat,
         levels,
         beside,
+        *inner,
         before,
         after,
-        scratch=[
-            (rows + 2, cols, lanes),
-            (rows + 2, cols, lanes),
-            (rows + 2, cols, lanes),
-            (rows, cols, lanes),
-            (rows, cols, lanes),
-            (rows + tile, lanes),
-            (rows, lanes),
-        ],
     )
     lates = [exchange(values, "col", k) if k else values for k, values in enumerate(lates)]
     whole, gram = call(

time: 45.7 us -> 42.5 us (0.930)
  starting transfers between devices: 17.3 us -> 15.4 us
  local copies, waits for them, and re-layouts: 1.81 us -> 0.01 us
  Pallas kernels: 5.99 us -> 6.82 us
    unnamed x8 -> x4, local copies, waits for them, and re-layouts: 1.81 us -> 0.01 us
    ppermute x1, waiting for transfers between devices: 0.01 us -> 1.19 us  [shards(): lax.ppermute(outer, 'lx', [(i, (i + 1) % count) for i in range(count)])]
    ppermute x10, starting transfers between devices: 12.4 us -> 11.3 us  [exchange(): return lax.ppermute(values, axis, [(i, i ^ distance) for i in range(count)])]
    ppermute x1, starting transfers between devices: 2.43 us -> 1.56 us  [shards(): lax.ppermute(outer, 'lx', [(i, (i + 1) % count) for i in range(count)])]
    ppermute x1, waiting for transfers between devices: 0.84 us -> 0.01 us  [shards(): far = lax.ppermute(edges, 'ly', far_pairs)]
    pallas_call x5 -> x6, Pallas kernels: 5.99 us -> 6.82 us  [call(): pl.pallas_call(kernel, out_shape=[jax.ShapeDtypeStruct(shape, jnp.float32...]
    ppermute x10, waiting for transfers between devices: 19.5 us -> 18.8 us  [exchange(): return lax.ppermute(values, axis, [(i, i ^ distance) for i in range(count)])]
where the time goes in v4:
time: 42.5 us; the launch traced here: 42.3 us
  waiting for transfers between devices  20 us (47%)
  starting transfers between devices  15.4 us (36%)
  Pallas kernels  6.82 us (16%)
    ppermute x10, waiting for transfers between devices, exchange(): return lax.ppermute(values, axis, [(i, i ^ distance) for i in range(count)])  18.8 us
    ppermute x10, starting transfers between devices, exchange(): return lax.ppermute(values, axis, [(i, i ^ distance) for i in range(count)])  11.3 us
    pallas_call x6, Pallas kernels, call(): pl.pallas_call(kernel, out_shape=[jax.ShapeDtypeStruct(shape, jnp.float32...  6.82 us
    ppermute x1, starting transfers between devices, shards(): far = lax.ppermute(edges, 'ly', far_pairs)  2.47 us
    ppermute x1, starting transfers between devices, shards(): lax.ppermute(outer, 'lx', [(i, (i + 1) % count) for i in range(count)])  1.56 us
    ppermute x1, waiting for transfers between devices, shards(): lax.ppermute(outer, 'lx', [(i, (i + 1) % count) for i in range(count)])  1.19 us
  transfers between devices with their start and end apart: 12, of which 7 were waited for; matrix products, arithmetic and copies ran while one was open for 0% of the time, Pallas kernels for 3%

profile of v4, /device:TPU:0, one launch (start us, length us, event | category | flops | bytes accessed | tf_op | source)
XLA Modules:
  0.0 42.3 jit_solution(14124092869987351420)
XLA Ops:
  0.0 0.0 copy-start
  0.0 1.6 %shard_map.28 = (f32[5,8,128]{2,1,0:T(8,128)S(1)}, f32[5,8,128]{2,1,0:T(8,128)S(1)}, f32[16,16,128]{2,1,0:T(8,128)S(1)}) custom-call(f32[1024,128]{1,0:T(8,128)} %bitcast.2, s32[64,128]{1,0:T(8,128)} %levels_ref.5), custom_call_target="tpu_custom_call" | custom-call | tf_op jit(solution)/shard_map/pallas_call | solution.py:384
  1.6 2.5 %collective-permute-start.1 = (f32[5,8,128]{2,1,0:T(8,128)S(1)}, f32[5,8,128]{2,1,0:T(8,128)S(1)}, u32[]{:S(2)}, u32[]{:S(2)}) collective-permute-start(f32[5,8,128]{2,1,0:T(8,128)S(1)} %get-tuple-element.20), channel_id=1, source_target_pairs={{0,12},{4,8},{8,4},{12,0},{1,13},{5,9},{9,5},{13,1},{2,14},{6,10},... | collective-permute-start | bytes 61448 | tf_op jit(solution)/shard_map/ppermute | solution.py:427
  4.1 0.7 %collective-permute-start = (f32[5,8,128]{2,1,0:T(8,128)S(1)}, f32[5,8,128]{2,1,0:T(8,128)S(1)}, u32[]{:S(2)}, u32[]{:S(2)}) collective-permute-start(f32[5,8,128]{2,1,0:T(8,128)S(1)} %get-tuple-element.20), channel_id=1, source_target_pairs={{0,4},{4,0},{8,12},{12,8},{1,5},{5,1},{9,13},{13,9},{2,6},{6,2},{1... | collective-permute-start | bytes 61448 | tf_op jit(solution)/shard_map/ppermute | solution.py:398
  4.7 2.6 %collective-permute-start.6 = (f32[16,16,128]{2,1,0:T(8,128)S(1)}, f32[16,16,128]{2,1,0:T(8,128)S(1)}, u32[]{:S(2)}, u32[]{:S(2)}) collective-permute-start(f32[16,16,128]{2,1,0:T(8,128)S(1)} %get-tuple-element.30), channel_id=1, source_target_pairs={{0,2},{1,3},{2,0},{3,1},{4,6},{5,7},{6,4},{7,5},{8,10},{9,11},{10,... | collective-permute-start | bytes 393224 | tf_op jit(solution)/shard_map/ppermute | solution.py:398
  7.3 0.0 collective-permute-done.1.far_ref
  7.3 0.0 collective-permute-done.near_ref
  7.4 1.6 %collective-permute-start.2 = (f32[7,8,128]{2,1,0:T(8,128)S(1)}, f32[7,8,128]{2,1,0:T(8,128)S(1)}, u32[]{:S(2)}, u32[]{:S(2)}) collective-permute-start(f32[7,8,128]{2,1,0:T(8,128)S(1)} %get-tuple-element.25), channel_id=1, source_target_pairs={{0,16},{16,0},{1,17},{17,1},{2,18},{18,2},{3,19},{19,3},{4,20},{20... | collective-permute-start | bytes 86024 | tf_op jit(solution)/shard_map/ppermute | solution.py:437
  8.9 0.0 copy-done
  8.9 0.0 copy-done.1
  8.9 1.2 %shard_map.30 = (f32[64,16,128]{2,1,0:T(8,128)S(1)}, f32[2,16,128]{2,1,0:T(8,128)S(1)}, f32[1,8,128]{2,1,0:T(8,128)S(1)}) custom-call(f32[1024,128]{1,0:T(8,128)S(1)} %bitcast.3, s32[64,128]{1,0:T(8,128)S(1)} %copy-done.1, f32[5,8,128]{2,1,0:T(8,128)S(1)} %get-tuple-element.21.beside_ref), custom_call_target="tpu_custom_call" | custom-call | flops 99999997952 | bytes 1000000000 | tf_op jit(solution)/shard_map/pallas_call | solution.py:384
  10.1 1.2 %collective-permute-done.2.before_ref.after_ref = f32[7,8,128]{2,1,0:T(8,128)S(1)} collective-permute-done((f32[7,8,128]{2,1,0:T(8,128)S(1)}, f32[7,8,128]{2,1,0:T(8,128)S(1)}, u32[]{:S(2)}, u32[]{:S(2)}) %collective-permute-start.2) | collective-permute-done | bytes 28704 | tf_op jit(solution)/shard_map/ppermute | solution.py:437
  11.3 0.2 shard_map.31
  11.5 1.6 %collective-permute-start.3 = (f32[16,16,128]{2,1,0:T(8,128)S(1)}, f32[16,16,128]{2,1,0:T(8,128)S(1)}, u32[]{:S(2)}, u32[]{:S(2)}) collective-permute-start(f32[16,16,128]{2,1,0:T(8,128)S(1)} %get-tuple-element.27), channel_id=1, source_target_pairs={{0,1},{1,0},{2,3},{3,2},{4,5},{5,4},{6,7},{7,6},{8,9},{9,8},{10,11... | collective-permute-start | bytes 393224 | tf_op jit(solution)/shard_map/ppermute | solution.py:398
  13.2 1.6 %collective-permute-start.5 = (f32[16,16,128]{2,1,0:T(8,128)S(1)}, f32[16,16,128]{2,1,0:T(8,128)S(1)}, u32[]{:S(2)}, u32[]{:S(2)}) collective-permute-start(f32[16,16,128]{2,1,0:T(8,128)S(1)} %get-tuple-element.29), channel_id=1, source_target_pairs={{0,3},{1,2},{2,1},{3,0},{4,7},{5,6},{6,5},{7,4},{8,11},{9,10},{10,... | collective-permute-start | bytes 393224 | tf_op jit(solution)/shard_map/ppermute | solution.py:398
  14.8 0.3 collective-permute-start.4
  15.1 6.3 %collective-permute-done.4.refs_2_ = f32[5,8,128]{2,1,0:T(8,128)S(1)} collective-permute-done((f32[5,8,128]{2,1,0:T(8,128)S(1)}, f32[5,8,128]{2,1,0:T(8,128)S(1)}, u32[]{:S(2)}, u32[]{:S(2)}) %collective-permute-start.4) | collective-permute-done | bytes 20512 | tf_op jit(solution)/shard_map/ppermute | solution.py:398
  21.4 0.0 collective-permute-done.6.refs_4_
  21.4 0.0 collective-permute-done.3.refs_1_
  21.4 0.0 collective-permute-done.5.refs_3_
  21.4 0.8 %shard_map.32 = (f32[16,64,128]{2,1,0:T(8,128)S(1)}, f32[32,128]{1,0:T(8,128)S(1)}) custom-call(s32[64,128]{1,0:T(8,128)S(1)} %copy-done.1, f32[16,16,128]{2,1,0:T(8,128)S(1)} %get-tuple-element.26.refs_0_, f32[16,16,128]{2,1,0:T(8,128)S(1)} %collective-permute-done.3.refs_1_, f32[5,8,128]{2,1,0:T(8,128)S(1)} %collective-permute-done.4.refs_2_, ...), custom_call_target="tpu_custom_call" | custom-call | tf_op jit(solution)/shard_map/pallas_call | solution.py:384
  22.2 0.0 collective-permute-start.7
  22.2 1.2 %collective-permute-done.7 = f32[32,128]{1,0:T(8,128)S(1)} collective-permute-done((f32[32,128]{1,0:T(8,128)S(1)}, f32[32,128]{1,0:T(8,128)S(1)}, u32[]{:S(2)}, u32[]{:S(2)}) %collective-permute-start.7) | collective-permute-done | bytes 16416 | tf_op jit(solution)/shard_map/ppermute | solution.py:398
  23.4 1.4 %collective-permute-start.8 = (f32[32,128]{1,0:T(8,128)S(1)}, f32[32,128]{1,0:T(8,128)S(1)}, u32[]{:S(2)}, u32[]{:S(2)}) collective-permute-start(f32[32,128]{1,0:T(8,128)S(1)} %add.12), channel_id=1, source_target_pairs={{0,8},{4,12},{8,0},{12,4},{1,9},{5,13},{9,1},{13,5},{2,10},{6,14},... | collective-permute-start | bytes 49160 | tf_op jit(solution)/shard_map/ppermute | solution.py:398
  24.8 2.4 %collective-permute-done.8 = f32[32,128]{1,0:T(8,128)S(1)} collective-permute-done((f32[32,128]{1,0:T(8,128)S(1)}, f32[32,128]{1,0:T(8,128)S(1)}, u32[]{:S(2)}, u32[]{:S(2)}) %collective-permute-start.8) | collective-permute-done | bytes 16416 | tf_op jit(solution)/shard_map/ppermute | solution.py:398
  27.2 1.5 %collective-permute-start.9 = (f32[32,128]{1,0:T(8,128)S(1)}, f32[32,128]{1,0:T(8,128)S(1)}, u32[]{:S(2)}, u32[]{:S(2)}) collective-permute-start(f32[32,128]{1,0:T(8,128)S(1)} %add.13), channel_id=1, source_target_pairs={{0,16},{16,0},{1,17},{17,1},{2,18},{18,2},{3,19},{19,3},{4,20},{20... | collective-permute-start | bytes 49160 | tf_op jit(solution)/shard_map/ppermute | solution.py:398
  28.6 2.2 %collective-permute-done.9 = f32[32,128]{1,0:T(8,128)S(1)} collective-permute-done((f32[32,128]{1,0:T(8,128)S(1)}, f32[32,128]{1,0:T(8,128)S(1)}, u32[]{:S(2)}, u32[]{:S(2)}) %collective-permute-start.9) | collective-permute-done | bytes 16416 | tf_op jit(solution)/shard_map/ppermute | solution.py:398
  30.9 0.3 collective-permute-start.10
  31.2 3.4 %collective-permute-done.10 = f32[32,128]{1,0:T(8,128)S(1)} collective-permute-done((f32[32,128]{1,0:T(8,128)S(1)}, f32[32,128]{1,0:T(8,128)S(1)}, u32[]{:S(2)}, u32[]{:S(2)}) %collective-permute-start.10) | collective-permute-done | bytes 16416 | tf_op jit(solution)/shard_map/ppermute | solution.py:398
  34.6 1.3 %collective-permute-start.11 = (f32[32,128]{1,0:T(8,128)S(1)}, f32[32,128]{1,0:T(8,128)S(1)}, u32[]{:S(2)}, u32[]{:S(2)}) collective-permute-start(f32[32,128]{1,0:T(8,128)S(1)} %add.15.gram_ref), channel_id=1, source_target_pairs={{0,2},{1,3},{2,0},{3,1},{4,6},{5,7},{6,4},{7,5},{8,10},{9,11},{10,... | collective-permute-start | bytes 49160 | tf_op jit(solution)/shard_map/ppermute | solution.py:398
  36.0 3.3 %collective-permute-done.11.other_ref = f32[32,128]{1,0:T(8,128)S(1)} collective-permute-done((f32[32,128]{1,0:T(8,128)S(1)}, f32[32,128]{1,0:T(8,128)S(1)}, u32[]{:S(2)}, u32[]{:S(2)}) %collective-permute-start.11) | collective-permute-done | bytes 16416 | tf_op jit(solution)/shard_map/ppermute | solution.py:398
  39.3 3.0 %shard_map.33 = f32[1024,128]{1,0:T(8,128)} custom-call(f32[16,64,128]{2,1,0:T(8,128)S(1)} %get-tuple-element.31.whole_ref, f32[32,128]{1,0:T(8,128)S(1)} %add.15.gram_ref, f32[32,128]{1,0:T(8,128)S(1)} %collective-permute-done.11.other_ref), custom_call_target="tpu_custom_call" | custom-call | tf_op jit(solution)/shard_map/pallas_call | solution.py:384
  (6 shorter events, 0.0 us)
Async XLA Ops:
  0.0 8.9 %copy-start = (f32[16,64,128]{2,1,0:T(8,128)S(1)}, f32[16,64,128]{2,1,0:T(8,128)}, u32[]{:S(2)}) copy-start(f32[16,64,128]{2,1,0:T(8,128)} %param.2) | copy-start | bytes 1572868
  1.6 5.7 %collective-permute-start.1 = (f32[5,8,128]{2,1,0:T(8,128)S(1)}, f32[5,8,128]{2,1,0:T(8,128)S(1)}, u32[]{:S(2)}, u32[]{:S(2)}) collective-permute-start(f32[5,8,128]{2,1,0:T(8,128)S(1)} %get-tuple-element.20), channel_id=1, source_target_pairs={{0,12},{4,8},{8,4},{12,0},{1,13},{5,9},{9,5},{13,1},{2,14},{6,10},... | collective-permute-start | bytes 61448 | tf_op jit(solution)/shard_map/ppermute | solution.py:427
  4.1 3.3 %collective-permute-start = (f32[5,8,128]{2,1,0:T(8,128)S(1)}, f32[5,8,128]{2,1,0:T(8,128)S(1)}, u32[]{:S(2)}, u32[]{:S(2)}) collective-permute-start(f32[5,8,128]{2,1,0:T(8,128)S(1)} %get-tuple-element.20), channel_id=1, source_target_pairs={{0,4},{4,0},{8,12},{12,8},{1,5},{5,1},{9,13},{13,9},{2,6},{6,2},{1... | collective-permute-start | bytes 61448 | tf_op jit(solution)/shard_map/ppermute | solution.py:398
  4.7 16.7 %collective-permute-start.6 = (f32[16,16,128]{2,1,0:T(8,128)S(1)}, f32[16,16,128]{2,1,0:T(8,128)S(1)}, u32[]{:S(2)}, u32[]{:S(2)}) collective-permute-start(f32[16,16,128]{2,1,0:T(8,128)S(1)} %get-tuple-element.30), channel_id=1, source_target_pairs={{0,2},{1,3},{2,0},{3,1},{4,6},{5,7},{6,4},{7,5},{8,10},{9,11},{10,... | collective-permute-start | bytes 393224 | tf_op jit(solution)/shard_map/ppermute | solution.py:398
  7.3 1.6 %copy-start.1 = (s32[64,128]{1,0:T(8,128)S(1)}, s32[64,128]{1,0:T(8,128)}, u32[]{:S(2)}) copy-start(s32[64,128]{1,0:T(8,128)} %levels_ref.5) | copy-start | bytes 98308
  7.4 3.9 %collective-permute-start.2 = (f32[7,8,128]{2,1,0:T(8,128)S(1)}, f32[7,8,128]{2,1,0:T(8,128)S(1)}, u32[]{:S(2)}, u32[]{:S(2)}) collective-permute-start(f32[7,8,128]{2,1,0:T(8,128)S(1)} %get-tuple-element.25), channel_id=1, source_target_pairs={{0,16},{16,0},{1,17},{17,1},{2,18},{18,2},{3,19},{19,3},{4,20},{20... | collective-permute-start | bytes 86024 | tf_op jit(solution)/shard_map/ppermute | solution.py:437
  11.5 9.9 %collective-permute-start.3 = (f32[16,16,128]{2,1,0:T(8,128)S(1)}, f32[16,16,128]{2,1,0:T(8,128)S(1)}, u32[]{:S(2)}, u32[]{:S(2)}) collective-permute-start(f32[16,16,128]{2,1,0:T(8,128)S(1)} %get-tuple-element.27), channel_id=1, source_target_pairs={{0,1},{1,0},{2,3},{3,2},{4,5},{5,4},{6,7},{7,6},{8,9},{9,8},{10,11... | collective-permute-start | bytes 393224 | tf_op jit(solution)/shard_map/ppermute | solution.py:398
  13.2 8.2 %collective-permute-start.5 = (f32[16,16,128]{2,1,0:T(8,128)S(1)}, f32[16,16,128]{2,1,0:T(8,128)S(1)}, u32[]{:S(2)}, u32[]{:S(2)}) collective-permute-start(f32[16,16,128]{2,1,0:T(8,128)S(1)} %get-tuple-element.29), channel_id=1, source_target_pairs={{0,3},{1,2},{2,1},{3,0},{4,7},{5,6},{6,5},{7,4},{8,11},{9,10},{10,... | collective-permute-start | bytes 393224 | tf_op jit(solution)/shard_map/ppermute | solution.py:398
  14.8 6.6 %collective-permute-start.4 = (f32[5,8,128]{2,1,0:T(8,128)S(1)}, f32[5,8,128]{2,1,0:T(8,128)S(1)}, u32[]{:S(2)}, u32[]{:S(2)}) collective-permute-start(f32[5,8,128]{2,1,0:T(8,128)S(1)} %get-tuple-element.28), channel_id=1, source_target_pairs={{0,2},{1,3},{2,0},{3,1},{4,6},{5,7},{6,4},{7,5},{8,10},{9,11},{10,... | collective-permute-start | bytes 61448 | tf_op jit(solution)/shard_map/ppermute | solution.py:398
  22.2 1.2 %collective-permute-start.7 = (f32[32,128]{1,0:T(8,128)S(1)}, f32[32,128]{1,0:T(8,128)S(1)}, u32[]{:S(2)}, u32[]{:S(2)}) collective-permute-start(f32[32,128]{1,0:T(8,128)S(1)} %get-tuple-element.32), channel_id=1, source_target_pairs={{0,4},{4,0},{8,12},{12,8},{1,5},{5,1},{9,13},{13,9},{2,6},{6,2},{1... | collective-permute-start | bytes 49160 | tf_op jit(solution)/shard_map/ppermute | solution.py:398
  23.4 3.7 %collective-permute-start.8 = (f32[32,128]{1,0:T(8,128)S(1)}, f32[32,128]{1,0:T(8,128)S(1)}, u32[]{:S(2)}, u32[]{:S(2)}) collective-permute-start(f32[32,128]{1,0:T(8,128)S(1)} %add.12), channel_id=1, source_target_pairs={{0,8},{4,12},{8,0},{12,4},{1,9},{5,13},{9,1},{13,5},{2,10},{6,14},... | collective-permute-start | bytes 49160 | tf_op jit(solution)/shard_map/ppermute | solution.py:398
  27.2 3.7 %collective-permute-start.9 = (f32[32,128]{1,0:T(8,128)S(1)}, f32[32,128]{1,0:T(8,128)S(1)}, u32[]{:S(2)}, u32[]{:S(2)}) collective-permute-start(f32[32,128]{1,0:T(8,128)S(1)} %add.13), channel_id=1, source_target_pairs={{0,16},{16,0},{1,17},{17,1},{2,18},{18,2},{3,19},{19,3},{4,20},{20... | collective-permute-start | bytes 49160 | tf_op jit(solution)/shard_map/ppermute | solution.py:398
  30.9 3.7 %collective-permute-start.10 = (f32[32,128]{1,0:T(8,128)S(1)}, f32[32,128]{1,0:T(8,128)S(1)}, u32[]{:S(2)}, u32[]{:S(2)}) collective-permute-start(f32[32,128]{1,0:T(8,128)S(1)} %add.14), channel_id=1, source_target_pairs={{0,1},{1,0},{2,3},{3,2},{4,5},{5,4},{6,7},{7,6},{8,9},{9,8},{10,11... | collective-permute-start | bytes 49160 | tf_op jit(solution)/shard_map/ppermute | solution.py:398
  34.6 4.6 %collective-permute-start.11 = (f32[32,128]{1,0:T(8,128)S(1)}, f32[32,128]{1,0:T(8,128)S(1)}, u32[]{:S(2)}, u32[]{:S(2)}) collective-permute-start(f32[32,128]{1,0:T(8,128)S(1)} %add.15.gram_ref), channel_id=1, source_target_pairs={{0,2},{1,3},{2,0},{3,1},{4,6},{5,7},{6,4},{7,5},{8,10},{9,11},{10,... | collective-permute-start | bytes 49160 | tf_op jit(solution)/shard_map/ppermute | solution.py:398

commit v5 on v4

--- a/solution.py
+++ b/solution.py
@@ -1,4 +1,5 @@
 import functools
+import itertools
 import math
 
 import jax
@@ -222,6 +223,7 @@
     rows,
     parts,
     early,
+    order,
     start_ref,
     levels_ref,
     beside_ref,
@@ -237,7 +239,7 @@
     first, last = outer_rows(
         cols, rows, start_ref, levels_ref, beside_ref, parts, before_ref, after_ref, next_ref
     )
-    for k, out_ref in enumerate(out_refs):
+    for k, out_ref in zip(order, out_refs):
         target = lax.axis_index("col") ^ k
         base = target * part_rows
         top = jnp.where(target == 0, first, done_ref[base])
@@ -254,8 +256,8 @@
         out_ref[2 * chunks] = packed_ref[early.index(k)]
 
 
-def gram_kernel(cols, parts, early, levels_ref, *refs):
-    late_refs, refs = refs[:parts], refs[parts:]
+def gram_kernel(cols, parts, early, order, levels_ref, *refs):
+    late_refs, refs = dict(zip(order, refs)), refs[parts:]
     raw_refs = dict(zip(early, refs))
     whole_ref, gram_ref, once, factor = refs[len(early) :]
     chunks = cols // tile
@@ -318,11 +320,12 @@
     return high, middle, low
 
 
-def solve_kernel(scale, whole_ref, gram_ref, other_ref, out_ref):
+def solve_kernel(scale, holder, whole_ref, gram_ref, other_ref, out_ref):
     part_rows, total, _ = whole_ref.shape
     blocks = total // tile
     half = total // 2
-    packed = gram_ref[...] + other_ref[...]
+    holds = lax.axis_index("ly") % 2 == holder
+    packed = jnp.where(holds, gram_ref[...], other_ref[...])
     lane = iota((tile, lanes), 1)
     sub = iota((tile, lanes), 0)
     shape = (tile, lanes)
@@ -398,6 +401,30 @@
     return lax.ppermute(values, axis, [(i, i ^ distance) for i in range(count)])
 
 
+axes = ("lx", "ly", "col")
+
+
+def pair_steps():
+    steps = []
+    for axis in ("ly", "lx", "col"):
+        bit = 2 if axis == "ly" else 1
+        while bit < lax.axis_size(axis):
+            steps.append((axis, bit))
+            bit *= 2
+    return steps
+
+
+def handover(holder, axis, bit):
+    sizes = [lax.axis_size(name) for name in axes]
+    pairs = []
+    for at, (x, y, z) in enumerate(itertools.product(*map(range, sizes))):
+        to = {"lx": x, "ly": y ^ 1, "col": z}
+        if y % 2 == holder:
+            to[axis] ^= bit
+        pairs.append((at, (to["lx"] * sizes[1] + to["ly"]) * sizes[2] + to["col"]))
+    return pairs
+
+
 def shards(start, levels):
     cols, rows, _ = start.shape
     parts = lax.axis_size("col")
@@ -406,6 +433,7 @@
     part_rows = rows // parts
     sizes = (cols, rows, parts)
     early = (parts // 2,)
+    order = (*sorted(range(1, parts), key=lambda k: (k in early, -k)), 0)
     flat = start.reshape(cols * rows, lanes)
     piece = (part_rows, cols, lanes)
     edges, outer, *raws = call(
@@ -448,8 +476,8 @@
         cost_estimate=pl.CostEstimate(flops=10**11, bytes_accessed=10**9, transcendentals=0),
     )
     lates = call(
-        functools.partial(late_kernel, *sizes, early),
-        [(2 * chunks + 1, tile, lanes) if k in early else piece for k in range(parts)],
+        functools.partial(late_kernel, *sizes, early, order),
+        [(2 * chunks + 1, tile, lanes) if k in early else piece for k in order],
         flat,
         levels,
         beside,
@@ -457,30 +485,28 @@
         before,
         after,
     )
-    lates = [exchange(values, "col", k) if k else values for k, values in enumerate(lates)]
+    lates = [exchange(values, "col", k) if k else values for k, values in zip(order, lates)]
     whole, gram = call(
-        functools.partial(gram_kernel, cols, parts, early),
+        functools.partial(gram_kernel, cols, parts, early, order),
         [(part_rows, total, lanes), (total // 2, 2 * total)],
         levels,
         *lates,
         *raws,
         scratch=[piece, (rows, lanes)],
     )
-    steps = []
-    for axis in ("ly", "lx", "col"):
-        bit = 1
-        while bit < lax.axis_size(axis):
-            steps.append((axis, bit))
-            bit *= 2
-    for axis, bit in steps[:-1]:
-        gram = gram + exchange(gram, axis, bit)
+    gram = gram + exchange(gram, "ly", 1)
+    holder = 0
+    for axis, bit in pair_steps():
+        near = exchange(gram, "ly", 1)
+        gram = near + lax.ppermute(gram, axes, handover(holder, axis, bit))
+        holder = 1 - holder
     scale = math.sqrt(rows * lax.axis_size("lx") * lanes * lax.axis_size("ly"))
     (basis,) = call(
-        functools.partial(solve_kernel, scale),
+        functools.partial(solve_kernel, scale, holder),
         [(total * part_rows, lanes)],
         whole,
         gram,
-        exchange(gram, *steps[-1]),
+        exchange(gram, "ly", 1),
     )
     return basis.reshape(total, part_rows, lanes)
 

time: 42.5 us -> 39.5 us (0.929)
  waiting for transfers between devices: 20 us -> 15.4 us
  starting transfers between devices: 15.4 us -> 17 us
    ppermute x10 -> x11, waiting for transfers between devices: 18.8 us -> 7.38 us  [exchange(): return lax.ppermute(values, axis, [(i, i ^ distance) for i in range(count)])]
    ppermute x0 -> x4, waiting for transfers between devices: none -> 6.82 us  [shards(): gram = near + lax.ppermute(gram, axes, handover(holder, axis, bit))]
    ppermute x0 -> x4, starting transfers between devices: none -> 3.23 us  [shards(): gram = near + lax.ppermute(gram, axes, handover(holder, axis, bit))]
    ppermute x10 -> x11, starting transfers between devices: 11.3 us -> 9.76 us  [exchange(): return lax.ppermute(values, axis, [(i, i ^ distance) for i in range(count)])]
  transfers between devices with their start and end apart: 12 -> 17, of which waited for: 7 -> 9; matrix products, arithmetic and copies ran while one was open for 0% -> 0% of each run, Pallas kernels for 3% -> 4%
where the time goes in v5:
time: 39.5 us; the launch traced here: 39.3 us
  starting transfers between devices  17 us (43%)
  waiting for transfers between devices  15.4 us (39%)
  Pallas kernels  6.82 us (17%)
    ppermute x11, starting transfers between devices, exchange(): return lax.ppermute(values, axis, [(i, i ^ distance) for i in range(count)])  9.76 us
    ppermute x11, waiting for transfers between devices, exchange(): return lax.ppermute(values, axis, [(i, i ^ distance) for i in range(count)])  7.38 us
    ppermute x4, waiting for transfers between devices, shards(): gram = near + lax.ppermute(gram, axes, handover(holder, axis, bit))  6.82 us
    pallas_call x6, Pallas kernels, call(): pl.pallas_call(kernel, out_shape=[jax.ShapeDtypeStruct(shape, jnp.float32...  6.82 us
    ppermute x4, starting transfers between devices, shards(): gram = near + lax.ppermute(gram, axes, handover(holder, axis, bit))  3.23 us
    ppermute x1, starting transfers between devices, shards(): far = lax.ppermute(edges, 'ly', far_pairs)  2.47 us
    ppermute x1, starting transfers between devices, shards(): lax.ppermute(outer, 'lx', [(i, (i + 1) % count) for i in range(count)])  1.56 us
    ppermute x1, waiting for transfers between devices, shards(): lax.ppermute(outer, 'lx', [(i, (i + 1) % count) for i in range(count)])  1.19 us
  transfers between devices with their start and end apart: 17, of which 9 were waited for; matrix products, arithmetic and copies ran while one was open for 0% of the time, Pallas kernels for 4%

profile of v5, /device:TPU:0, one launch (start us, length us, event | category | flops | bytes accessed | tf_op | source)
XLA Modules:
  0.0 39.3 jit_solution(14653245630110790317)
XLA Ops:
  0.0 1.6 %shard_map.28 = (f32[5,8,128]{2,1,0:T(8,128)S(1)}, f32[5,8,128]{2,1,0:T(8,128)S(1)}, f32[16,16,128]{2,1,0:T(8,128)S(1)}) custom-call(f32[1024,128]{1,0:T(8,128)} %bitcast.2, s32[64,128]{1,0:T(8,128)} %levels_ref.5), custom_call_target="tpu_custom_call" | custom-call | tf_op jit(solution)/shard_map/pallas_call | solution.py:387
  1.6 2.5 %collective-permute-start.1 = (f32[5,8,128]{2,1,0:T(8,128)S(1)}, f32[5,8,128]{2,1,0:T(8,128)S(1)}, u32[]{:S(2)}, u32[]{:S(2)}) collective-permute-start(f32[5,8,128]{2,1,0:T(8,128)S(1)} %get-tuple-element.20), channel_id=1, source_target_pairs={{0,12},{4,8},{8,4},{12,0},{1,13},{5,9},{9,5},{13,1},{2,14},{6,10},... | collective-permute-start | bytes 61448 | tf_op jit(solution)/shard_map/ppermute | solution.py:455
  4.1 0.7 %collective-permute-start = (f32[5,8,128]{2,1,0:T(8,128)S(1)}, f32[5,8,128]{2,1,0:T(8,128)S(1)}, u32[]{:S(2)}, u32[]{:S(2)}) collective-permute-start(f32[5,8,128]{2,1,0:T(8,128)S(1)} %get-tuple-element.20), channel_id=1, source_target_pairs={{0,4},{4,0},{8,12},{12,8},{1,5},{5,1},{9,13},{13,9},{2,6},{6,2},{1... | collective-permute-start | bytes 61448 | tf_op jit(solution)/shard_map/ppermute | solution.py:401
  4.7 2.6 %collective-permute-start.6 = (f32[16,16,128]{2,1,0:T(8,128)S(1)}, f32[16,16,128]{2,1,0:T(8,128)S(1)}, u32[]{:S(2)}, u32[]{:S(2)}) collective-permute-start(f32[16,16,128]{2,1,0:T(8,128)S(1)} %get-tuple-element.30), channel_id=1, source_target_pairs={{0,2},{1,3},{2,0},{3,1},{4,6},{5,7},{6,4},{7,5},{8,10},{9,11},{10,... | collective-permute-start | bytes 393224 | tf_op jit(solution)/shard_map/ppermute | solution.py:401
  7.3 0.0 collective-permute-done.1.far_ref
  7.4 1.6 %collective-permute-start.2 = (f32[7,8,128]{2,1,0:T(8,128)S(1)}, f32[7,8,128]{2,1,0:T(8,128)S(1)}, u32[]{:S(2)}, u32[]{:S(2)}) collective-permute-start(f32[7,8,128]{2,1,0:T(8,128)S(1)} %get-tuple-element.25), channel_id=1, source_target_pairs={{0,16},{16,0},{1,17},{17,1},{2,18},{18,2},{3,19},{19,3},{4,20},{20... | collective-permute-start | bytes 86024 | tf_op jit(solution)/shard_map/ppermute | solution.py:465
  8.9 1.2 %shard_map.30 = (f32[64,16,128]{2,1,0:T(8,128)S(1)}, f32[2,16,128]{2,1,0:T(8,128)S(1)}, f32[1,8,128]{2,1,0:T(8,128)S(1)}) custom-call(f32[1024,128]{1,0:T(8,128)S(1)} %bitcast.3, s32[64,128]{1,0:T(8,128)S(1)} %copy-done.1, f32[5,8,128]{2,1,0:T(8,128)S(1)} %get-tuple-element.21.beside_ref), custom_call_target="tpu_custom_call" | custom-call | flops 99999997952 | bytes 1000000000 | tf_op jit(solution)/shard_map/pallas_call | solution.py:387
  10.1 1.2 %collective-permute-done.2.before_ref.after_ref = f32[7,8,128]{2,1,0:T(8,128)S(1)} collective-permute-done((f32[7,8,128]{2,1,0:T(8,128)S(1)}, f32[7,8,128]{2,1,0:T(8,128)S(1)}, u32[]{:S(2)}, u32[]{:S(2)}) %collective-permute-start.2) | collective-permute-done | bytes 28704 | tf_op jit(solution)/shard_map/ppermute | solution.py:465
  11.3 0.2 shard_map.31
  11.5 2.8 %collective-permute-start.3 = (f32[16,16,128]{2,1,0:T(8,128)S(1)}, f32[16,16,128]{2,1,0:T(8,128)S(1)}, u32[]{:S(2)}, u32[]{:S(2)}) collective-permute-start(f32[16,16,128]{2,1,0:T(8,128)S(1)} %get-tuple-element.26), channel_id=1, source_target_pairs={{0,3},{1,2},{2,1},{3,0},{4,7},{5,6},{6,5},{7,4},{8,11},{9,10},{10,... | collective-permute-start | bytes 393224 | tf_op jit(solution)/shard_map/ppermute | solution.py:401
  14.3 0.0 collective-permute-start.4
  14.3 1.7 %collective-permute-start.5 = (f32[5,8,128]{2,1,0:T(8,128)S(1)}, f32[5,8,128]{2,1,0:T(8,128)S(1)}, u32[]{:S(2)}, u32[]{:S(2)}) collective-permute-start(f32[5,8,128]{2,1,0:T(8,128)S(1)} %get-tuple-element.28), channel_id=1, source_target_pairs={{0,2},{1,3},{2,0},{3,1},{4,6},{5,7},{6,4},{7,5},{8,10},{9,11},{10,... | collective-permute-start | bytes 61448 | tf_op jit(solution)/shard_map/ppermute | solution.py:401
  16.0 4.5 %collective-permute-done.5.refs_2_ = f32[5,8,128]{2,1,0:T(8,128)S(1)} collective-permute-done((f32[5,8,128]{2,1,0:T(8,128)S(1)}, f32[5,8,128]{2,1,0:T(8,128)S(1)}, u32[]{:S(2)}, u32[]{:S(2)}) %collective-permute-start.5) | collective-permute-done | bytes 20512 | tf_op jit(solution)/shard_map/ppermute | solution.py:401
  20.5 0.6 %collective-permute-done.4.refs_1_ = f32[16,16,128]{2,1,0:T(8,128)S(1)} collective-permute-done((f32[16,16,128]{2,1,0:T(8,128)S(1)}, f32[16,16,128]{2,1,0:T(8,128)S(1)}, u32[]{:S(2)}, u32[]{:S(2)}) %collective-permute-start.4) | collective-permute-done | bytes 131104 | tf_op jit(solution)/shard_map/ppermute | solution.py:401
  21.0 0.8 %shard_map.32 = (f32[16,64,128]{2,1,0:T(8,128)S(1)}, f32[32,128]{1,0:T(8,128)S(1)}) custom-call(s32[64,128]{1,0:T(8,128)S(1)} %copy-done.1, f32[16,16,128]{2,1,0:T(8,128)S(1)} %collective-permute-done.3.refs_0_, f32[16,16,128]{2,1,0:T(8,128)S(1)} %collective-permute-done.4.refs_1_, f32[5,8,128]{2,1,0:T(8,128)S(1)} %collective-permute-done.5.refs_2_, ...), custom_call_target="tpu_custom_call" | custom-call | tf_op jit(solution)/shard_map/pallas_call | solution.py:387
  21.8 0.0 collective-permute-start.7
  21.8 1.2 %collective-permute-done.7 = f32[32,128]{1,0:T(8,128)S(1)} collective-permute-done((f32[32,128]{1,0:T(8,128)S(1)}, f32[32,128]{1,0:T(8,128)S(1)}, u32[]{:S(2)}, u32[]{:S(2)}) %collective-permute-start.7) | collective-permute-done | bytes 16416 | tf_op jit(solution)/shard_map/ppermute | solution.py:401
  23.0 0.9 %collective-permute-start.9 = (f32[32,128]{1,0:T(8,128)S(1)}, f32[32,128]{1,0:T(8,128)S(1)}, u32[]{:S(2)}, u32[]{:S(2)}) collective-permute-start(f32[32,128]{1,0:T(8,128)S(1)} %add.15), channel_id=1, source_target_pairs={{0,12},{1,13},{2,14},{3,15},{4,0},{5,1},{6,2},{7,3},{8,4},{9,5},{1... | collective-permute-start | bytes 49160 | tf_op jit(solution)/shard_map/ppermute | solution.py:501
  23.9 0.0 collective-permute-start.8
  23.9 1.4 %collective-permute-done.9 = f32[32,128]{1,0:T(8,128)S(1)} collective-permute-done((f32[32,128]{1,0:T(8,128)S(1)}, f32[32,128]{1,0:T(8,128)S(1)}, u32[]{:S(2)}, u32[]{:S(2)}) %collective-permute-start.9) | collective-permute-done | bytes 16416 | tf_op jit(solution)/shard_map/ppermute | solution.py:501
  25.4 1.0 %collective-permute-start.11 = (f32[32,128]{1,0:T(8,128)S(1)}, f32[32,128]{1,0:T(8,128)S(1)}, u32[]{:S(2)}, u32[]{:S(2)}) collective-permute-start(f32[32,128]{1,0:T(8,128)S(1)} %add.16), channel_id=1, source_target_pairs={{0,4},{1,5},{2,6},{3,7},{4,16},{5,17},{6,18},{7,19},{8,12},{9,13},... | collective-permute-start | bytes 49160 | tf_op jit(solution)/shard_map/ppermute | solution.py:501
  26.4 0.6 %collective-permute-start.10 = (f32[32,128]{1,0:T(8,128)S(1)}, f32[32,128]{1,0:T(8,128)S(1)}, u32[]{:S(2)}, u32[]{:S(2)}) collective-permute-start(f32[32,128]{1,0:T(8,128)S(1)} %add.16), channel_id=1, source_target_pairs={{0,4},{4,0},{8,12},{12,8},{1,5},{5,1},{9,13},{13,9},{2,6},{6,2},{1... | collective-permute-start | bytes 49160 | tf_op jit(solution)/shard_map/ppermute | solution.py:401
  27.0 1.9 %collective-permute-done.11 = f32[32,128]{1,0:T(8,128)S(1)} collective-permute-done((f32[32,128]{1,0:T(8,128)S(1)}, f32[32,128]{1,0:T(8,128)S(1)}, u32[]{:S(2)}, u32[]{:S(2)}) %collective-permute-start.11) | collective-permute-done | bytes 16416 | tf_op jit(solution)/shard_map/ppermute | solution.py:501
  28.9 0.3 collective-permute-start.13
  29.2 0.2 collective-permute-start.12
  29.5 1.2 %collective-permute-done.13 = f32[32,128]{1,0:T(8,128)S(1)} collective-permute-done((f32[32,128]{1,0:T(8,128)S(1)}, f32[32,128]{1,0:T(8,128)S(1)}, u32[]{:S(2)}, u32[]{:S(2)}) %collective-permute-start.13) | collective-permute-done | bytes 16416 | tf_op jit(solution)/shard_map/ppermute | solution.py:501
  30.7 1.0 %collective-permute-start.15 = (f32[32,128]{1,0:T(8,128)S(1)}, f32[32,128]{1,0:T(8,128)S(1)}, u32[]{:S(2)}, u32[]{:S(2)}) collective-permute-start(f32[32,128]{1,0:T(8,128)S(1)} %add.18), channel_id=1, source_target_pairs={{0,4},{1,5},{2,6},{3,7},{4,2},{5,3},{6,0},{7,1},{8,12},{9,13},{10,... | collective-permute-start | bytes 49160 | tf_op jit(solution)/shard_map/ppermute | solution.py:501
  31.7 1.1 %collective-permute-start.14 = (f32[32,128]{1,0:T(8,128)S(1)}, f32[32,128]{1,0:T(8,128)S(1)}, u32[]{:S(2)}, u32[]{:S(2)}) collective-permute-start(f32[32,128]{1,0:T(8,128)S(1)} %add.18), channel_id=1, source_target_pairs={{0,4},{4,0},{8,12},{12,8},{1,5},{5,1},{9,13},{13,9},{2,6},{6,2},{1... | collective-permute-start | bytes 49160 | tf_op jit(solution)/shard_map/ppermute | solution.py:401
  32.8 2.2 %collective-permute-done.15 = f32[32,128]{1,0:T(8,128)S(1)} collective-permute-done((f32[32,128]{1,0:T(8,128)S(1)}, f32[32,128]{1,0:T(8,128)S(1)}, u32[]{:S(2)}, u32[]{:S(2)}) %collective-permute-start.15) | collective-permute-done | bytes 16416 | tf_op jit(solution)/shard_map/ppermute | solution.py:501
  35.0 0.1 collective-permute-start.16
  35.1 1.2 %collective-permute-done.16.other_ref = f32[32,128]{1,0:T(8,128)S(1)} collective-permute-done((f32[32,128]{1,0:T(8,128)S(1)}, f32[32,128]{1,0:T(8,128)S(1)}, u32[]{:S(2)}, u32[]{:S(2)}) %collective-permute-start.16) | collective-permute-done | bytes 16416 | tf_op jit(solution)/shard_map/ppermute | solution.py:401
  36.3 3.0 %shard_map.33 = f32[1024,128]{1,0:T(8,128)} custom-call(f32[16,64,128]{2,1,0:T(8,128)S(1)} %get-tuple-element.31.whole_ref, f32[32,128]{1,0:T(8,128)S(1)} %add.19.gram_ref, f32[32,128]{1,0:T(8,128)S(1)} %collective-permute-done.16.other_ref), custom_call_target="tpu_custom_call" | custom-call | tf_op jit(solution)/shard_map/pallas_call | solution.py:387
  (17 shorter events, 0.1 us)
Async XLA Ops:
  0.0 8.9 %copy-start = (f32[16,64,128]{2,1,0:T(8,128)S(1)}, f32[16,64,128]{2,1,0:T(8,128)}, u32[]{:S(2)}) copy-start(f32[16,64,128]{2,1,0:T(8,128)} %param.2) | copy-start | bytes 1572868
  1.6 5.7 %collective-permute-start.1 = (f32[5,8,128]{2,1,0:T(8,128)S(1)}, f32[5,8,128]{2,1,0:T(8,128)S(1)}, u32[]{:S(2)}, u32[]{:S(2)}) collective-permute-start(f32[5,8,128]{2,1,0:T(8,128)S(1)} %get-tuple-element.20), channel_id=1, source_target_pairs={{0,12},{4,8},{8,4},{12,0},{1,13},{5,9},{9,5},{13,1},{2,14},{6,10},... | collective-permute-start | bytes 61448 | tf_op jit(solution)/shard_map/ppermute | solution.py:455
  4.1 3.3 %collective-permute-start = (f32[5,8,128]{2,1,0:T(8,128)S(1)}, f32[5,8,128]{2,1,0:T(8,128)S(1)}, u32[]{:S(2)}, u32[]{:S(2)}) collective-permute-start(f32[5,8,128]{2,1,0:T(8,128)S(1)} %get-tuple-element.20), channel_id=1, source_target_pairs={{0,4},{4,0},{8,12},{12,8},{1,5},{5,1},{9,13},{13,9},{2,6},{6,2},{1... | collective-permute-start | bytes 61448 | tf_op jit(solution)/shard_map/ppermute | solution.py:401
  4.7 15.7 %collective-permute-start.6 = (f32[16,16,128]{2,1,0:T(8,128)S(1)}, f32[16,16,128]{2,1,0:T(8,128)S(1)}, u32[]{:S(2)}, u32[]{:S(2)}) collective-permute-start(f32[16,16,128]{2,1,0:T(8,128)S(1)} %get-tuple-element.30), channel_id=1, source_target_pairs={{0,2},{1,3},{2,0},{3,1},{4,6},{5,7},{6,4},{7,5},{8,10},{9,11},{10,... | collective-permute-start | bytes 393224 | tf_op jit(solution)/shard_map/ppermute | solution.py:401
  7.3 1.6 %copy-start.1 = (s32[64,128]{1,0:T(8,128)S(1)}, s32[64,128]{1,0:T(8,128)}, u32[]{:S(2)}) copy-start(s32[64,128]{1,0:T(8,128)} %levels_ref.5) | copy-start | bytes 98308
  7.4 3.9 %collective-permute-start.2 = (f32[7,8,128]{2,1,0:T(8,128)S(1)}, f32[7,8,128]{2,1,0:T(8,128)S(1)}, u32[]{:S(2)}, u32[]{:S(2)}) collective-permute-start(f32[7,8,128]{2,1,0:T(8,128)S(1)} %get-tuple-element.25), channel_id=1, source_target_pairs={{0,16},{16,0},{1,17},{17,1},{2,18},{18,2},{3,19},{19,3},{4,20},{20... | collective-permute-start | bytes 86024 | tf_op jit(solution)/shard_map/ppermute | solution.py:465
  11.5 8.9 %collective-permute-start.3 = (f32[16,16,128]{2,1,0:T(8,128)S(1)}, f32[16,16,128]{2,1,0:T(8,128)S(1)}, u32[]{:S(2)}, u32[]{:S(2)}) collective-permute-start(f32[16,16,128]{2,1,0:T(8,128)S(1)} %get-tuple-element.26), channel_id=1, source_target_pairs={{0,3},{1,2},{2,1},{3,0},{4,7},{5,6},{6,5},{7,4},{8,11},{9,10},{10,... | collective-permute-start | bytes 393224 | tf_op jit(solution)/shard_map/ppermute | solution.py:401
  14.3 6.7 %collective-permute-start.4 = (f32[16,16,128]{2,1,0:T(8,128)S(1)}, f32[16,16,128]{2,1,0:T(8,128)S(1)}, u32[]{:S(2)}, u32[]{:S(2)}) collective-permute-start(f32[16,16,128]{2,1,0:T(8,128)S(1)} %get-tuple-element.27), channel_id=1, source_target_pairs={{0,1},{1,0},{2,3},{3,2},{4,5},{5,4},{6,7},{7,6},{8,9},{9,8},{10,11... | collective-permute-start | bytes 393224 | tf_op jit(solution)/shard_map/ppermute | solution.py:401
  14.3 6.1 %collective-permute-start.5 = (f32[5,8,128]{2,1,0:T(8,128)S(1)}, f32[5,8,128]{2,1,0:T(8,128)S(1)}, u32[]{:S(2)}, u32[]{:S(2)}) collective-permute-start(f32[5,8,128]{2,1,0:T(8,128)S(1)} %get-tuple-element.28), channel_id=1, source_target_pairs={{0,2},{1,3},{2,0},{3,1},{4,6},{5,7},{6,4},{7,5},{8,10},{9,11},{10,... | collective-permute-start | bytes 61448 | tf_op jit(solution)/shard_map/ppermute | solution.py:401
  21.8 1.2 %collective-permute-start.7 = (f32[32,128]{1,0:T(8,128)S(1)}, f32[32,128]{1,0:T(8,128)S(1)}, u32[]{:S(2)}, u32[]{:S(2)}) collective-permute-start(f32[32,128]{1,0:T(8,128)S(1)} %get-tuple-element.32), channel_id=1, source_target_pairs={{0,4},{4,0},{8,12},{12,8},{1,5},{5,1},{9,13},{13,9},{2,6},{6,2},{1... | collective-permute-start | bytes 49160 | tf_op jit(solution)/shard_map/ppermute | solution.py:401
  23.0 2.4 %collective-permute-start.9 = (f32[32,128]{1,0:T(8,128)S(1)}, f32[32,128]{1,0:T(8,128)S(1)}, u32[]{:S(2)}, u32[]{:S(2)}) collective-permute-start(f32[32,128]{1,0:T(8,128)S(1)} %add.15), channel_id=1, source_target_pairs={{0,12},{1,13},{2,14},{3,15},{4,0},{5,1},{6,2},{7,3},{8,4},{9,5},{1... | collective-permute-start | bytes 49160 | tf_op jit(solution)/shard_map/ppermute | solution.py:501
  23.9 1.4 %collective-permute-start.8 = (f32[32,128]{1,0:T(8,128)S(1)}, f32[32,128]{1,0:T(8,128)S(1)}, u32[]{:S(2)}, u32[]{:S(2)}) collective-permute-start(f32[32,128]{1,0:T(8,128)S(1)} %add.15), channel_id=1, source_target_pairs={{0,4},{4,0},{8,12},{12,8},{1,5},{5,1},{9,13},{13,9},{2,6},{6,2},{1... | collective-permute-start | bytes 49160 | tf_op jit(solution)/shard_map/ppermute | solution.py:401
  25.4 3.5 %collective-permute-start.11 = (f32[32,128]{1,0:T(8,128)S(1)}, f32[32,128]{1,0:T(8,128)S(1)}, u32[]{:S(2)}, u32[]{:S(2)}) collective-permute-start(f32[32,128]{1,0:T(8,128)S(1)} %add.16), channel_id=1, source_target_pairs={{0,4},{1,5},{2,6},{3,7},{4,16},{5,17},{6,18},{7,19},{8,12},{9,13},... | collective-permute-start | bytes 49160 | tf_op jit(solution)/shard_map/ppermute | solution.py:501
  26.4 2.5 %collective-permute-start.10 = (f32[32,128]{1,0:T(8,128)S(1)}, f32[32,128]{1,0:T(8,128)S(1)}, u32[]{:S(2)}, u32[]{:S(2)}) collective-permute-start(f32[32,128]{1,0:T(8,128)S(1)} %add.16), channel_id=1, source_target_pairs={{0,4},{4,0},{8,12},{12,8},{1,5},{5,1},{9,13},{13,9},{2,6},{6,2},{1... | collective-permute-start | bytes 49160 | tf_op jit(solution)/shard_map/ppermute | solution.py:401
  28.9 1.8 %collective-permute-start.13 = (f32[32,128]{1,0:T(8,128)S(1)}, f32[32,128]{1,0:T(8,128)S(1)}, u32[]{:S(2)}, u32[]{:S(2)}) collective-permute-start(f32[32,128]{1,0:T(8,128)S(1)} %add.17), channel_id=1, source_target_pairs={{0,5},{1,4},{2,7},{3,6},{4,0},{5,1},{6,2},{7,3},{8,13},{9,12},{10,... | collective-permute-start | bytes 49160 | tf_op jit(solution)/shard_map/ppermute | solution.py:501
  29.2 1.4 %collective-permute-start.12 = (f32[32,128]{1,0:T(8,128)S(1)}, f32[32,128]{1,0:T(8,128)S(1)}, u32[]{:S(2)}, u32[]{:S(2)}) collective-permute-start(f32[32,128]{1,0:T(8,128)S(1)} %add.17), channel_id=1, source_target_pairs={{0,4},{4,0},{8,12},{12,8},{1,5},{5,1},{9,13},{13,9},{2,6},{6,2},{1... | collective-permute-start | bytes 49160 | tf_op jit(solution)/shard_map/ppermute | solution.py:401
  30.7 4.3 %collective-permute-start.15 = (f32[32,128]{1,0:T(8,128)S(1)}, f32[32,128]{1,0:T(8,128)S(1)}, u32[]{:S(2)}, u32[]{:S(2)}) collective-permute-start(f32[32,128]{1,0:T(8,128)S(1)} %add.18), channel_id=1, source_target_pairs={{0,4},{1,5},{2,6},{3,7},{4,2},{5,3},{6,0},{7,1},{8,12},{9,13},{10,... | collective-permute-start | bytes 49160 | tf_op jit(solution)/shard_map/ppermute | solution.py:501
  31.7 3.4 %collective-permute-start.14 = (f32[32,128]{1,0:T(8,128)S(1)}, f32[32,128]{1,0:T(8,128)S(1)}, u32[]{:S(2)}, u32[]{:S(2)}) collective-permute-start(f32[32,128]{1,0:T(8,128)S(1)} %add.18), channel_id=1, source_target_pairs={{0,4},{4,0},{8,12},{12,8},{1,5},{5,1},{9,13},{13,9},{2,6},{6,2},{1... | collective-permute-start | bytes 49160 | tf_op jit(solution)/shard_map/ppermute | solution.py:401
  35.0 1.2 %collective-permute-start.16 = (f32[32,128]{1,0:T(8,128)S(1)}, f32[32,128]{1,0:T(8,128)S(1)}, u32[]{:S(2)}, u32[]{:S(2)}) collective-permute-start(f32[32,128]{1,0:T(8,128)S(1)} %add.19.gram_ref), channel_id=1, source_target_pairs={{0,4},{4,0},{8,12},{12,8},{1,5},{5,1},{9,13},{13,9},{2,6},{6,2},{1... | collective-permute-start | bytes 49160 | tf_op jit(solution)/shard_map/ppermute | solution.py:401

commit v6 on v5

--- a/solution.py
+++ b/solution.py
@@ -33,7 +33,7 @@
 def pack_edges(tiles):
     lane = iota((tile, lanes), 1)
     packed = jnp.zeros((tile, lanes), jnp.float32)
-    for k, values in enumerate(tiles):
+    for k, values in tiles:
         moved = pltpu.roll(values, (4 * k + 2) % lanes, 1)
         packed = jnp.where(lane // 4 == k, moved, packed)
     return packed
@@ -43,43 +43,50 @@
     return pltpu.roll(packed, lanes - (4 * k + 2), 1)
 
 
-def pack_kernel(cols, rows, parts, early, start_hbm, levels_hbm, edges_ref, outer_ref, *refs):
-    piece_refs, (start_ref, levels_ref, arrived) = refs[: len(early)], refs[len(early) :]
+def pack_kernel(
+    cols, rows, parts, early, start_hbm, levels_hbm, start_ref, levels_ref, edges_ref, outer_ref, *refs
+):
+    piece_refs, (arrived,) = refs[: len(early)], refs[len(early) :]
     chunks = cols // tile
     part_rows = rows // parts
-    copies = [
-        pltpu.make_async_copy(start_hbm, start_ref, arrived.at[0]),
-        pltpu.make_async_copy(levels_hbm, levels_ref, arrived.at[1]),
+    span = tile * rows
+    copies = [pltpu.make_async_copy(levels_hbm, levels_ref, arrived.at[chunks])] + [
+        pltpu.make_async_copy(
+            start_hbm.at[pl.ds(chunk * span, span)],
+            start_ref.at[pl.ds(chunk * span, span)],
+            arrived.at[chunk],
+        )
+        for chunk in range(chunks)
     ]
     for copy in copies:
         copy.start()
-    for copy in copies:
-        copy.wait()
-    for group in range(parts):
-        edges_ref[group] = pack_edges(
-            tile_at(start_ref, rows, group * part_rows + row, chunk)
-            for row in range(part_rows)
-            for chunk in range(chunks)
-        )
+    copies[0].wait()
     edges_ref[parts] = pack_edges(
-        levels_ref[k * tile : (k + 1) * tile, :].astype(jnp.float32) for k in range(rows // tile)
-    )
-    for chunk in range(chunks):
-        outer_ref[chunk] = tile_at(start_ref, rows, 0, chunk)
-        outer_ref[chunks + chunk] = tile_at(start_ref, rows, rows - 1, chunk)
+        (k, levels_ref[k * tile : (k + 1) * tile, :].astype(jnp.float32))
+        for k in range(rows // tile)
+    )
     first = levels_ref[0:1, :].astype(jnp.float32)
     last = levels_ref[rows - 1 : rows, :].astype(jnp.float32)
     outer_ref[2 * chunks] = jnp.where(iota((tile, lanes), 0) == 0, first, last)
-    for k, piece_ref in zip(early, piece_refs):
-        copy_piece(cols, rows, parts, k, start_ref, piece_ref)
-
-
-def copy_piece(cols, rows, parts, k, start_ref, piece_ref):
-    chunks = cols // tile
+    for chunk in range(chunks):
+        copies[1 + chunk].wait()
+        outer_ref[chunk] = tile_at(start_ref, rows, 0, chunk)
+        outer_ref[chunks + chunk] = tile_at(start_ref, rows, rows - 1, chunk)
+        for group in range(parts):
+            packed = pack_edges(
+                (row * chunks + chunk, tile_at(start_ref, rows, group * part_rows + row, chunk))
+                for row in range(part_rows)
+            )
+            edges_ref[group] = packed if chunk == 0 else edges_ref[group] + packed
+        for k, piece_ref in zip(early, piece_refs):
+            copy_piece(cols, rows, parts, k, start_ref, piece_ref, (chunk,))
+
+
+def copy_piece(cols, rows, parts, k, start_ref, piece_ref, which):
     part_rows = rows // parts
     base = (lax.axis_index("col") ^ k) * part_rows
     for row in range(part_rows):
-        for chunk in range(chunks):
+        for chunk in which:
             piece_ref[row, chunk * tile : (chunk + 1) * tile, :] = tile_at(
                 start_ref, rows, base + row, chunk
             )
@@ -156,7 +163,7 @@
     for at, k in enumerate(early):
         base = (lax.axis_index("col") ^ k) * part_rows
         packed_ref[at] = pack_edges(
-            done_ref[base + row, chunk * tile : (chunk + 1) * tile, :]
+            (row * chunks + chunk, done_ref[base + row, chunk * tile : (chunk + 1) * tile, :])
             for row in range(part_rows)
             for chunk in range(chunks)
         )
@@ -256,15 +263,33 @@
         out_ref[2 * chunks] = packed_ref[early.index(k)]
 
 
-def gram_kernel(cols, parts, early, order, levels_ref, *refs):
+def alone_kernel(cols, levels_ref, raw_ref, out_ref, once, factor):
+    part_rows = raw_ref.shape[0]
+    factor[...] = site_factor(levels_ref[...].astype(jnp.float32))
+    base = lax.axis_index("col") * part_rows
+    for row in range(part_rows):
+        above, below = raw_ref[min(row + 1, part_rows - 1)], raw_ref[max(row - 1, 0)]
+        here = raw_ref[row]
+        once[row] = factor_at(factor, base + row, cols) * here - inverse * (
+            sides(here, here) + upward(row, above, below)
+        )
+    for row in range(part_rows):
+        above, below = once[min(row + 1, part_rows - 1)], once[max(row - 1, 0)]
+        here = once[row]
+        twice = factor_at(factor, base + row, cols) * here - inverse * (
+            sides(here, here) + upward(row, above, below)
+        )
+        out_ref[row] = 2.0 * twice - raw_ref[row]
+
+
+def gram_kernel(cols, parts, early, order, *refs):
     late_refs, refs = dict(zip(order, refs)), refs[parts:]
-    raw_refs = dict(zip(early, refs))
-    whole_ref, gram_ref, once, factor = refs[len(early) :]
+    alone_refs = dict(zip(early, refs))
+    whole_ref, gram_ref = refs[len(early) :]
     chunks = cols // tile
     part_rows = whole_ref.shape[0]
     total = cols * parts
     place = lax.axis_index("col")
-    factor[...] = site_factor(levels_ref[...].astype(jnp.float32))
     lane = iota((cols, lanes), 1)
     outer_lanes = (lane < 2) | (lane >= lanes - 2)
     for k in range(parts):
@@ -273,30 +298,17 @@
         if k not in early:
             whole_ref[:, part, :] = late_ref[...]
             continue
-        raw_ref = raw_refs[k]
-        base = place * part_rows
-        for row in range(part_rows):
-            above, below = raw_ref[min(row + 1, part_rows - 1)], raw_ref[max(row - 1, 0)]
-            here = raw_ref[row]
-            once[row] = factor_at(factor, base + row, cols) * here - inverse * (
-                sides(here, here) + upward(row, above, below)
-            )
         packed = late_ref[2 * chunks]
         for row in range(part_rows):
             if row in (0, part_rows - 1):
                 at = 0 if row == 0 else chunks
-                whole_ref[row, part, :] = jnp.concatenate(
-                    [late_ref[at + chunk] for chunk in range(chunks)], axis=0
+                sent = [late_ref[at + chunk] for chunk in range(chunks)]
+                whole_ref[row, part, :] = jnp.concatenate(sent, axis=0)
+            else:
+                sent = [unpack_edges(packed, row * chunks + chunk) for chunk in range(chunks)]
+                whole_ref[row, part, :] = jnp.where(
+                    outer_lanes, jnp.concatenate(sent, axis=0), alone_refs[k][row]
                 )
-                continue
-            here = once[row]
-            twice = factor_at(factor, base + row, cols) * here - inverse * (
-                sides(here, here) + upward(row, once[row + 1], once[row - 1])
-            )
-            sent = jnp.concatenate(
-                [unpack_edges(packed, row * chunks + chunk) for chunk in range(chunks)], axis=0
-            )
-            whole_ref[row, part, :] = jnp.where(outer_lanes, sent, 2.0 * twice - raw_ref[row])
     products = jnp.zeros((3 * total, 3 * total), jnp.float32)
     for row in range(0, part_rows, 2):
         values = jnp.concatenate([whole_ref[row], whole_ref[row + 1]], axis=1)
@@ -386,7 +398,10 @@
 def call(kernel, outs, *operands, scratch=(), limit=32, **specs):
     return pl.pallas_call(
         kernel,
-        out_shape=[jax.ShapeDtypeStruct(shape, jnp.float32) for shape in outs],
+        out_shape=[
+            jax.ShapeDtypeStruct(shape, jnp.float32) if isinstance(shape, tuple) else shape
+            for shape in outs
+        ],
         scratch_shapes=[
             pltpu.VMEM(shape, jnp.float32) if isinstance(shape, tuple) else shape
             for shape in scratch
@@ -436,16 +451,12 @@
     order = (*sorted(range(1, parts), key=lambda k: (k in early, -k)), 0)
     flat = start.reshape(cols * rows, lanes)
     piece = (part_rows, cols, lanes)
-    edges, outer, *raws = call(
+    start_here, levels_here, edges, outer, *raws = call(
         functools.partial(pack_kernel, *sizes, early),
-        [(parts + 1, tile, lanes), (2 * chunks + 1, tile, lanes)] + [piece] * len(early),
+        [flat.shape, jax.ShapeDtypeStruct(levels.shape, levels.dtype), (parts + 1, tile, lanes), (2 * chunks + 1, tile, lanes)] + [piece] * len(early),
         pltpu.with_memory_space_constraint(flat, pltpu.HBM),
         pltpu.with_memory_space_constraint(levels, pltpu.HBM),
-        scratch=[
-            flat.shape,
-            pltpu.VMEM(levels.shape, levels.dtype),
-            pltpu.SemaphoreType.DMA((2,)),
-        ],
+        scratch=[pltpu.SemaphoreType.DMA((chunks + 1,))],
         limit=32,
         in_specs=[pl.BlockSpec(memory_space=pl.ANY)] * 2,
     )
@@ -469,8 +480,8 @@
     inner = call(
         functools.partial(inner_kernel, *sizes, early),
         [(rows, cols, lanes), (2, cols, lanes), (len(early), tile, lanes)],
-        flat,
-        levels,
+        start_here,
+        levels_here,
         beside,
         scratch=[(rows, cols, lanes)] * 4 + [(rows, lanes)] * 2,
         cost_estimate=pl.CostEstimate(flops=10**11, bytes_accessed=10**9, transcendentals=0),
@@ -478,21 +489,30 @@
     lates = call(
         functools.partial(late_kernel, *sizes, early, order),
         [(2 * chunks + 1, tile, lanes) if k in early else piece for k in order],
-        flat,
-        levels,
+        start_here,
+        levels_here,
         beside,
         *inner,
         before,
         after,
     )
     lates = [exchange(values, "col", k) if k else values for k, values in zip(order, lates)]
+    alones = [
+        call(
+            functools.partial(alone_kernel, cols),
+            [piece],
+            levels_here,
+            raw,
+            scratch=[piece, (rows, lanes)],
+            cost_estimate=pl.CostEstimate(flops=0, bytes_accessed=10**6, transcendentals=0),
+        )[0]
+        for raw in raws
+    ]
     whole, gram = call(
         functools.partial(gram_kernel, cols, parts, early, order),
         [(part_rows, total, lanes), (total // 2, 2 * total)],
-        levels,
         *lates,
-        *raws,
-        scratch=[piece, (rows, lanes)],
+        *alones,
     )
     gram = gram + exchange(gram, "ly", 1)
     holder = 0

time: 39.5 us -> 39.3 us (level)
    pallas_call x6 -> x7, Pallas kernels: 6.82 us -> 6.81 us  [call(): pl.pallas_call(kernel, out_shape=[jax.ShapeDtypeStruct(shape, jnp.float32...]
where the time goes in v6:
time: 39.3 us; the launch traced here: 39.1 us
  starting transfers between devices  17 us (43%)
  waiting for transfers between devices  15.2 us (39%)
  Pallas kernels  6.81 us (17%)
    ppermute x11, starting transfers between devices, exchange(): return lax.ppermute(values, axis, [(i, i ^ distance) for i in range(count)])  9.75 us
    ppermute x11, waiting for transfers between devices, exchange(): return lax.ppermute(values, axis, [(i, i ^ distance) for i in range(count)])  7.16 us
    ppermute x4, waiting for transfers between devices, shards(): gram = near + lax.ppermute(gram, axes, handover(holder, axis, bit))  6.82 us
    pallas_call x7, Pallas kernels, call(): pl.pallas_call(kernel, out_shape=[jax.ShapeDtypeStruct(shape, jnp.float32...  6.81 us
    ppermute x4, starting transfers between devices, shards(): gram = near + lax.ppermute(gram, axes, handover(holder, axis, bit))  3.24 us
    ppermute x1, starting transfers between devices, shards(): far = lax.ppermute(edges, 'ly', far_pairs)  2.47 us
    ppermute x1, starting transfers between devices, shards(): lax.ppermute(outer, 'lx', [(i, (i + 1) % count) for i in range(count)])  1.56 us
    ppermute x1, waiting for transfers between devices, shards(): lax.ppermute(outer, 'lx', [(i, (i + 1) % count) for i in range(count)])  1.2 us
  transfers between devices with their start and end apart: 17, of which 9 were waited for; matrix products, arithmetic and copies ran while one was open for 0% of the time, Pallas kernels for 4%

profile of v6, /device:TPU:0, one launch (start us, length us, event | category | flops | bytes accessed | tf_op | source)
XLA Modules:
  0.0 39.1 jit_solution(7079638412489712740)
XLA Ops:
  0.0 1.5 %shard_map.28 = (f32[1024,128]{1,0:T(8,128)S(1)}, s32[64,128]{1,0:T(8,128)S(1)}, f32[5,8,128]{2,1,0:T(8,128)S(1)}, f32[5,8,128]{2,1,0:T(8,128)S(1)}, f32[16,16,128]{2,1,0:T(8,128)S(1)}) custom-call(f32[1024,128]{1,0:T(8,128)} %bitcast.2, s32[64,128]{1,0:T(8,128)} %levels_hbm.1), custom_call_target="tpu_custom_call" | custom-call | tf_op jit(solution)/shard_map/pallas_call | solution.py:399
  1.5 2.5 %collective-permute-start.1 = (f32[5,8,128]{2,1,0:T(8,128)S(1)}, f32[5,8,128]{2,1,0:T(8,128)S(1)}, u32[]{:S(2)}, u32[]{:S(2)}) collective-permute-start(f32[5,8,128]{2,1,0:T(8,128)S(1)} %get-tuple-element.24), channel_id=1, source_target_pairs={{0,12},{4,8},{8,4},{12,0},{1,13},{5,9},{9,5},{13,1},{2,14},{6,10},... | collective-permute-start | bytes 61448 | tf_op jit(solution)/shard_map/ppermute | solution.py:466
  4.0 0.7 %collective-permute-start = (f32[5,8,128]{2,1,0:T(8,128)S(1)}, f32[5,8,128]{2,1,0:T(8,128)S(1)}, u32[]{:S(2)}, u32[]{:S(2)}) collective-permute-start(f32[5,8,128]{2,1,0:T(8,128)S(1)} %get-tuple-element.24), channel_id=1, source_target_pairs={{0,4},{4,0},{8,12},{12,8},{1,5},{5,1},{9,13},{13,9},{2,6},{6,2},{1... | collective-permute-start | bytes 61448 | tf_op jit(solution)/shard_map/ppermute | solution.py:416
  4.7 2.6 %collective-permute-start.6 = (f32[16,16,128]{2,1,0:T(8,128)S(1)}, f32[16,16,128]{2,1,0:T(8,128)S(1)}, u32[]{:S(2)}, u32[]{:S(2)}) collective-permute-start(f32[16,16,128]{2,1,0:T(8,128)S(1)} %get-tuple-element.34), channel_id=1, source_target_pairs={{0,2},{1,3},{2,0},{3,1},{4,6},{5,7},{6,4},{7,5},{8,10},{9,11},{10,... | collective-permute-start | bytes 393224 | tf_op jit(solution)/shard_map/ppermute | solution.py:416
  7.3 1.6 %collective-permute-start.2 = (f32[7,8,128]{2,1,0:T(8,128)S(1)}, f32[7,8,128]{2,1,0:T(8,128)S(1)}, u32[]{:S(2)}, u32[]{:S(2)}) collective-permute-start(f32[7,8,128]{2,1,0:T(8,128)S(1)} %get-tuple-element.29), channel_id=1, source_target_pairs={{0,16},{16,0},{1,17},{17,1},{2,18},{18,2},{3,19},{19,3},{4,20},{20... | collective-permute-start | bytes 86024 | tf_op jit(solution)/shard_map/ppermute | solution.py:476
  8.8 1.2 %shard_map.30 = (f32[64,16,128]{2,1,0:T(8,128)S(1)}, f32[2,16,128]{2,1,0:T(8,128)S(1)}, f32[1,8,128]{2,1,0:T(8,128)S(1)}) custom-call(f32[1024,128]{1,0:T(8,128)S(1)} %get-tuple-element.21.start_ref, s32[64,128]{1,0:T(8,128)S(1)} %get-tuple-element.22.levels_ref, f32[5,8,128]{2,1,0:T(8,128)S(1)} %get-tuple-element.25.beside_ref), custom_call_target="tpu_custom_call" | custom-call | flops 99999997952 | bytes 1000000000 | tf_op jit(solution)/shard_map/pallas_call | solution.py:399
  10.0 1.2 %collective-permute-done.2.before_ref.after_ref = f32[7,8,128]{2,1,0:T(8,128)S(1)} collective-permute-done((f32[7,8,128]{2,1,0:T(8,128)S(1)}, f32[7,8,128]{2,1,0:T(8,128)S(1)}, u32[]{:S(2)}, u32[]{:S(2)}) %collective-permute-start.2) | collective-permute-done | bytes 28704 | tf_op jit(solution)/shard_map/ppermute | solution.py:476
  11.2 0.2 shard_map.31
  11.4 2.8 %collective-permute-start.3 = (f32[16,16,128]{2,1,0:T(8,128)S(1)}, f32[16,16,128]{2,1,0:T(8,128)S(1)}, u32[]{:S(2)}, u32[]{:S(2)}) collective-permute-start(f32[16,16,128]{2,1,0:T(8,128)S(1)} %get-tuple-element.30), channel_id=1, source_target_pairs={{0,3},{1,2},{2,1},{3,0},{4,7},{5,6},{6,5},{7,4},{8,11},{9,10},{10,... | collective-permute-start | bytes 393224 | tf_op jit(solution)/shard_map/ppermute | solution.py:416
  14.2 0.0 collective-permute-start.4
  14.2 1.7 %collective-permute-start.5 = (f32[5,8,128]{2,1,0:T(8,128)S(1)}, f32[5,8,128]{2,1,0:T(8,128)S(1)}, u32[]{:S(2)}, u32[]{:S(2)}) collective-permute-start(f32[5,8,128]{2,1,0:T(8,128)S(1)} %get-tuple-element.32), channel_id=1, source_target_pairs={{0,2},{1,3},{2,0},{3,1},{4,6},{5,7},{6,4},{7,5},{8,10},{9,11},{10,... | collective-permute-start | bytes 61448 | tf_op jit(solution)/shard_map/ppermute | solution.py:416
  15.9 0.0 collective-permute-done.6.raw_ref
  15.9 0.2 shard_map.32.refs_4_
  16.1 4.2 %collective-permute-done.5.refs_2_ = f32[5,8,128]{2,1,0:T(8,128)S(1)} collective-permute-done((f32[5,8,128]{2,1,0:T(8,128)S(1)}, f32[5,8,128]{2,1,0:T(8,128)S(1)}, u32[]{:S(2)}, u32[]{:S(2)}) %collective-permute-start.5) | collective-permute-done | bytes 20512 | tf_op jit(solution)/shard_map/ppermute | solution.py:416
  20.4 0.6 %collective-permute-done.4.refs_1_ = f32[16,16,128]{2,1,0:T(8,128)S(1)} collective-permute-done((f32[16,16,128]{2,1,0:T(8,128)S(1)}, f32[16,16,128]{2,1,0:T(8,128)S(1)}, u32[]{:S(2)}, u32[]{:S(2)}) %collective-permute-start.4) | collective-permute-done | bytes 131104 | tf_op jit(solution)/shard_map/ppermute | solution.py:416
  20.9 0.6 %shard_map.33 = (f32[16,64,128]{2,1,0:T(8,128)S(1)}, f32[32,128]{1,0:T(8,128)S(1)}) custom-call(f32[16,16,128]{2,1,0:T(8,128)S(1)} %collective-permute-done.3.refs_0_, f32[16,16,128]{2,1,0:T(8,128)S(1)} %collective-permute-done.4.refs_1_, f32[5,8,128]{2,1,0:T(8,128)S(1)} %collective-permute-done.5.refs_2_, f32[16,16,128]{2,1,0:T(8,128)S(1)} %get-tuple-element.33.refs_3_, ...), custom_call_target="tpu_custom_call" | custom-call | tf_op jit(solution)/shard_map/pallas_call | solution.py:399
  21.6 0.0 collective-permute-start.7
  21.6 1.2 %collective-permute-done.7 = f32[32,128]{1,0:T(8,128)S(1)} collective-permute-done((f32[32,128]{1,0:T(8,128)S(1)}, f32[32,128]{1,0:T(8,128)S(1)}, u32[]{:S(2)}, u32[]{:S(2)}) %collective-permute-start.7) | collective-permute-done | bytes 16416 | tf_op jit(solution)/shard_map/ppermute | solution.py:416
  22.8 0.9 %collective-permute-start.9 = (f32[32,128]{1,0:T(8,128)S(1)}, f32[32,128]{1,0:T(8,128)S(1)}, u32[]{:S(2)}, u32[]{:S(2)}) collective-permute-start(f32[32,128]{1,0:T(8,128)S(1)} %add.15), channel_id=1, source_target_pairs={{0,12},{1,13},{2,14},{3,15},{4,0},{5,1},{6,2},{7,3},{8,4},{9,5},{1... | collective-permute-start | bytes 49160 | tf_op jit(solution)/shard_map/ppermute | solution.py:521
  23.7 1.4 %collective-permute-done.9 = f32[32,128]{1,0:T(8,128)S(1)} collective-permute-done((f32[32,128]{1,0:T(8,128)S(1)}, f32[32,128]{1,0:T(8,128)S(1)}, u32[]{:S(2)}, u32[]{:S(2)}) %collective-permute-start.9) | collective-permute-done | bytes 16416 | tf_op jit(solution)/shard_map/ppermute | solution.py:521
  25.2 1.0 %collective-permute-start.11 = (f32[32,128]{1,0:T(8,128)S(1)}, f32[32,128]{1,0:T(8,128)S(1)}, u32[]{:S(2)}, u32[]{:S(2)}) collective-permute-start(f32[32,128]{1,0:T(8,128)S(1)} %add.16), channel_id=1, source_target_pairs={{0,4},{1,5},{2,6},{3,7},{4,16},{5,17},{6,18},{7,19},{8,12},{9,13},... | collective-permute-start | bytes 49160 | tf_op jit(solution)/shard_map/ppermute | solution.py:521
  26.2 0.6 %collective-permute-start.10 = (f32[32,128]{1,0:T(8,128)S(1)}, f32[32,128]{1,0:T(8,128)S(1)}, u32[]{:S(2)}, u32[]{:S(2)}) collective-permute-start(f32[32,128]{1,0:T(8,128)S(1)} %add.16), channel_id=1, source_target_pairs={{0,4},{4,0},{8,12},{12,8},{1,5},{5,1},{9,13},{13,9},{2,6},{6,2},{1... | collective-permute-start | bytes 49160 | tf_op jit(solution)/shard_map/ppermute | solution.py:416
  26.8 1.9 %collective-permute-done.11 = f32[32,128]{1,0:T(8,128)S(1)} collective-permute-done((f32[32,128]{1,0:T(8,128)S(1)}, f32[32,128]{1,0:T(8,128)S(1)}, u32[]{:S(2)}, u32[]{:S(2)}) %collective-permute-start.11) | collective-permute-done | bytes 16416 | tf_op jit(solution)/shard_map/ppermute | solution.py:521
  28.7 0.3 collective-permute-start.13
  29.0 0.2 collective-permute-start.12
  29.3 1.2 %collective-permute-done.13 = f32[32,128]{1,0:T(8,128)S(1)} collective-permute-done((f32[32,128]{1,0:T(8,128)S(1)}, f32[32,128]{1,0:T(8,128)S(1)}, u32[]{:S(2)}, u32[]{:S(2)}) %collective-permute-start.13) | collective-permute-done | bytes 16416 | tf_op jit(solution)/shard_map/ppermute | solution.py:521
  30.5 1.0 %collective-permute-start.15 = (f32[32,128]{1,0:T(8,128)S(1)}, f32[32,128]{1,0:T(8,128)S(1)}, u32[]{:S(2)}, u32[]{:S(2)}) collective-permute-start(f32[32,128]{1,0:T(8,128)S(1)} %add.18), channel_id=1, source_target_pairs={{0,4},{1,5},{2,6},{3,7},{4,2},{5,3},{6,0},{7,1},{8,12},{9,13},{10,... | collective-permute-start | bytes 49160 | tf_op jit(solution)/shard_map/ppermute | solution.py:521
  31.5 1.1 %collective-permute-start.14 = (f32[32,128]{1,0:T(8,128)S(1)}, f32[32,128]{1,0:T(8,128)S(1)}, u32[]{:S(2)}, u32[]{:S(2)}) collective-permute-start(f32[32,128]{1,0:T(8,128)S(1)} %add.18), channel_id=1, source_target_pairs={{0,4},{4,0},{8,12},{12,8},{1,5},{5,1},{9,13},{13,9},{2,6},{6,2},{1... | collective-permute-start | bytes 49160 | tf_op jit(solution)/shard_map/ppermute | solution.py:416
  32.6 2.2 %collective-permute-done.15 = f32[32,128]{1,0:T(8,128)S(1)} collective-permute-done((f32[32,128]{1,0:T(8,128)S(1)}, f32[32,128]{1,0:T(8,128)S(1)}, u32[]{:S(2)}, u32[]{:S(2)}) %collective-permute-start.15) | collective-permute-done | bytes 16416 | tf_op jit(solution)/shard_map/ppermute | solution.py:521
  34.8 0.1 collective-permute-start.16
  34.9 1.2 %collective-permute-done.16.other_ref = f32[32,128]{1,0:T(8,128)S(1)} collective-permute-done((f32[32,128]{1,0:T(8,128)S(1)}, f32[32,128]{1,0:T(8,128)S(1)}, u32[]{:S(2)}, u32[]{:S(2)}) %collective-permute-start.16) | collective-permute-done | bytes 16416 | tf_op jit(solution)/shard_map/ppermute | solution.py:416
  36.1 3.0 %shard_map.34 = f32[1024,128]{1,0:T(8,128)} custom-call(f32[16,64,128]{2,1,0:T(8,128)S(1)} %get-tuple-element.35.whole_ref, f32[32,128]{1,0:T(8,128)S(1)} %add.19.gram_ref, f32[32,128]{1,0:T(8,128)S(1)} %collective-permute-done.16.other_ref), custom_call_target="tpu_custom_call" | custom-call | tf_op jit(solution)/shard_map/pallas_call | solution.py:399
  (14 shorter events, 0.1 us)
Async XLA Ops:
  1.5 5.7 %collective-permute-start.1 = (f32[5,8,128]{2,1,0:T(8,128)S(1)}, f32[5,8,128]{2,1,0:T(8,128)S(1)}, u32[]{:S(2)}, u32[]{:S(2)}) collective-permute-start(f32[5,8,128]{2,1,0:T(8,128)S(1)} %get-tuple-element.24), channel_id=1, source_target_pairs={{0,12},{4,8},{8,4},{12,0},{1,13},{5,9},{9,5},{13,1},{2,14},{6,10},... | collective-permute-start | bytes 61448 | tf_op jit(solution)/shard_map/ppermute | solution.py:466
  4.0 3.3 %collective-permute-start = (f32[5,8,128]{2,1,0:T(8,128)S(1)}, f32[5,8,128]{2,1,0:T(8,128)S(1)}, u32[]{:S(2)}, u32[]{:S(2)}) collective-permute-start(f32[5,8,128]{2,1,0:T(8,128)S(1)} %get-tuple-element.24), channel_id=1, source_target_pairs={{0,4},{4,0},{8,12},{12,8},{1,5},{5,1},{9,13},{13,9},{2,6},{6,2},{1... | collective-permute-start | bytes 61448 | tf_op jit(solution)/shard_map/ppermute | solution.py:416
  4.7 11.3 %collective-permute-start.6 = (f32[16,16,128]{2,1,0:T(8,128)S(1)}, f32[16,16,128]{2,1,0:T(8,128)S(1)}, u32[]{:S(2)}, u32[]{:S(2)}) collective-permute-start(f32[16,16,128]{2,1,0:T(8,128)S(1)} %get-tuple-element.34), channel_id=1, source_target_pairs={{0,2},{1,3},{2,0},{3,1},{4,6},{5,7},{6,4},{7,5},{8,10},{9,11},{10,... | collective-permute-start | bytes 393224 | tf_op jit(solution)/shard_map/ppermute | solution.py:416
  7.3 3.9 %collective-permute-start.2 = (f32[7,8,128]{2,1,0:T(8,128)S(1)}, f32[7,8,128]{2,1,0:T(8,128)S(1)}, u32[]{:S(2)}, u32[]{:S(2)}) collective-permute-start(f32[7,8,128]{2,1,0:T(8,128)S(1)} %get-tuple-element.29), channel_id=1, source_target_pairs={{0,16},{16,0},{1,17},{17,1},{2,18},{18,2},{3,19},{19,3},{4,20},{20... | collective-permute-start | bytes 86024 | tf_op jit(solution)/shard_map/ppermute | solution.py:476
  11.4 8.9 %collective-permute-start.3 = (f32[16,16,128]{2,1,0:T(8,128)S(1)}, f32[16,16,128]{2,1,0:T(8,128)S(1)}, u32[]{:S(2)}, u32[]{:S(2)}) collective-permute-start(f32[16,16,128]{2,1,0:T(8,128)S(1)} %get-tuple-element.30), channel_id=1, source_target_pairs={{0,3},{1,2},{2,1},{3,0},{4,7},{5,6},{6,5},{7,4},{8,11},{9,10},{10,... | collective-permute-start | bytes 393224 | tf_op jit(solution)/shard_map/ppermute | solution.py:416
  14.2 6.7 %collective-permute-start.4 = (f32[16,16,128]{2,1,0:T(8,128)S(1)}, f32[16,16,128]{2,1,0:T(8,128)S(1)}, u32[]{:S(2)}, u32[]{:S(2)}) collective-permute-start(f32[16,16,128]{2,1,0:T(8,128)S(1)} %get-tuple-element.31), channel_id=1, source_target_pairs={{0,1},{1,0},{2,3},{3,2},{4,5},{5,4},{6,7},{7,6},{8,9},{9,8},{10,11... | collective-permute-start | bytes 393224 | tf_op jit(solution)/shard_map/ppermute | solution.py:416
  14.2 6.1 %collective-permute-start.5 = (f32[5,8,128]{2,1,0:T(8,128)S(1)}, f32[5,8,128]{2,1,0:T(8,128)S(1)}, u32[]{:S(2)}, u32[]{:S(2)}) collective-permute-start(f32[5,8,128]{2,1,0:T(8,128)S(1)} %get-tuple-element.32), channel_id=1, source_target_pairs={{0,2},{1,3},{2,0},{3,1},{4,6},{5,7},{6,4},{7,5},{8,10},{9,11},{10,... | collective-permute-start | bytes 61448 | tf_op jit(solution)/shard_map/ppermute | solution.py:416
  21.6 1.2 %collective-permute-start.7 = (f32[32,128]{1,0:T(8,128)S(1)}, f32[32,128]{1,0:T(8,128)S(1)}, u32[]{:S(2)}, u32[]{:S(2)}) collective-permute-start(f32[32,128]{1,0:T(8,128)S(1)} %get-tuple-element.36), channel_id=1, source_target_pairs={{0,4},{4,0},{8,12},{12,8},{1,5},{5,1},{9,13},{13,9},{2,6},{6,2},{1... | collective-permute-start | bytes 49160 | tf_op jit(solution)/shard_map/ppermute | solution.py:416
  22.8 2.4 %collective-permute-start.9 = (f32[32,128]{1,0:T(8,128)S(1)}, f32[32,128]{1,0:T(8,128)S(1)}, u32[]{:S(2)}, u32[]{:S(2)}) collective-permute-start(f32[32,128]{1,0:T(8,128)S(1)} %add.15), channel_id=1, source_target_pairs={{0,12},{1,13},{2,14},{3,15},{4,0},{5,1},{6,2},{7,3},{8,4},{9,5},{1... | collective-permute-start | bytes 49160 | tf_op jit(solution)/shard_map/ppermute | solution.py:521
  23.7 1.4 %collective-permute-start.8 = (f32[32,128]{1,0:T(8,128)S(1)}, f32[32,128]{1,0:T(8,128)S(1)}, u32[]{:S(2)}, u32[]{:S(2)}) collective-permute-start(f32[32,128]{1,0:T(8,128)S(1)} %add.15), channel_id=1, source_target_pairs={{0,4},{4,0},{8,12},{12,8},{1,5},{5,1},{9,13},{13,9},{2,6},{6,2},{1... | collective-permute-start | bytes 49160 | tf_op jit(solution)/shard_map/ppermute | solution.py:416
  25.2 3.5 %collective-permute-start.11 = (f32[32,128]{1,0:T(8,128)S(1)}, f32[32,128]{1,0:T(8,128)S(1)}, u32[]{:S(2)}, u32[]{:S(2)}) collective-permute-start(f32[32,128]{1,0:T(8,128)S(1)} %add.16), channel_id=1, source_target_pairs={{0,4},{1,5},{2,6},{3,7},{4,16},{5,17},{6,18},{7,19},{8,12},{9,13},... | collective-permute-start | bytes 49160 | tf_op jit(solution)/shard_map/ppermute | solution.py:521
  26.2 2.5 %collective-permute-start.10 = (f32[32,128]{1,0:T(8,128)S(1)}, f32[32,128]{1,0:T(8,128)S(1)}, u32[]{:S(2)}, u32[]{:S(2)}) collective-permute-start(f32[32,128]{1,0:T(8,128)S(1)} %add.16), channel_id=1, source_target_pairs={{0,4},{4,0},{8,12},{12,8},{1,5},{5,1},{9,13},{13,9},{2,6},{6,2},{1... | collective-permute-start | bytes 49160 | tf_op jit(solution)/shard_map/ppermute | solution.py:416
  28.7 1.8 %collective-permute-start.13 = (f32[32,128]{1,0:T(8,128)S(1)}, f32[32,128]{1,0:T(8,128)S(1)}, u32[]{:S(2)}, u32[]{:S(2)}) collective-permute-start(f32[32,128]{1,0:T(8,128)S(1)} %add.17), channel_id=1, source_target_pairs={{0,5},{1,4},{2,7},{3,6},{4,0},{5,1},{6,2},{7,3},{8,13},{9,12},{10,... | collective-permute-start | bytes 49160 | tf_op jit(solution)/shard_map/ppermute | solution.py:521
  29.0 1.4 %collective-permute-start.12 = (f32[32,128]{1,0:T(8,128)S(1)}, f32[32,128]{1,0:T(8,128)S(1)}, u32[]{:S(2)}, u32[]{:S(2)}) collective-permute-start(f32[32,128]{1,0:T(8,128)S(1)} %add.17), channel_id=1, source_target_pairs={{0,4},{4,0},{8,12},{12,8},{1,5},{5,1},{9,13},{13,9},{2,6},{6,2},{1... | collective-permute-start | bytes 49160 | tf_op jit(solution)/shard_map/ppermute | solution.py:416
  30.5 4.3 %collective-permute-start.15 = (f32[32,128]{1,0:T(8,128)S(1)}, f32[32,128]{1,0:T(8,128)S(1)}, u32[]{:S(2)}, u32[]{:S(2)}) collective-permute-start(f32[32,128]{1,0:T(8,128)S(1)} %add.18), channel_id=1, source_target_pairs={{0,4},{1,5},{2,6},{3,7},{4,2},{5,3},{6,0},{7,1},{8,12},{9,13},{10,... | collective-permute-start | bytes 49160 | tf_op jit(solution)/shard_map/ppermute | solution.py:521
  31.5 3.4 %collective-permute-start.14 = (f32[32,128]{1,0:T(8,128)S(1)}, f32[32,128]{1,0:T(8,128)S(1)}, u32[]{:S(2)}, u32[]{:S(2)}) collective-permute-start(f32[32,128]{1,0:T(8,128)S(1)} %add.18), channel_id=1, source_target_pairs={{0,4},{4,0},{8,12},{12,8},{1,5},{5,1},{9,13},{13,9},{2,6},{6,2},{1... | collective-permute-start | bytes 49160 | tf_op jit(solution)/shard_map/ppermute | solution.py:416
  34.8 1.2 %collective-permute-start.16 = (f32[32,128]{1,0:T(8,128)S(1)}, f32[32,128]{1,0:T(8,128)S(1)}, u32[]{:S(2)}, u32[]{:S(2)}) collective-permute-start(f32[32,128]{1,0:T(8,128)S(1)} %add.19.gram_ref), channel_id=1, source_target_pairs={{0,4},{4,0},{8,12},{12,8},{1,5},{5,1},{9,13},{13,9},{2,6},{6,2},{1... | collective-permute-start | bytes 49160 | tf_op jit(solution)/shard_map/ppermute | solution.py:416

commit v7 on v6

--- a/solution.py
+++ b/solution.py
@@ -332,7 +332,49 @@
     return high, middle, low
 
 
-def solve_kernel(scale, holder, whole_ref, gram_ref, other_ref, out_ref):
+def eliminate(work, b, columns_ref, rows_ref):
+    shape = (tile, lanes)
+    sub = iota(shape, 0)
+
+    def spread(ref, *place):
+        return jnp.broadcast_to(ref[(*place[:-1], pl.ds(place[-1], 1), slice(None))], shape)
+
+    column = [
+        [jnp.broadcast_to(rows[:, b * tile + m : b * tile + m + 1], shape) for m in range(tile)]
+        for rows in work[b:]
+    ]
+    slot = b % 2
+    for m in range(tile):
+        columns_ref[slot, m] = column[0][m]
+    rows_ref[slot] = work[b]
+    factor = {(p, q): spread(columns_ref, slot, q, p) for p in range(tile) for q in range(p + 1)}
+    pivots = [spread(rows_ref, slot, m) for m in range(tile)]
+    roots = []
+    for m in range(tile):
+        roots.append(lax.rsqrt(factor[m, m]))
+        for p in range(m + 1, tile):
+            factor[p, m] = factor[p, m] * roots[m]
+        for p in range(m + 1, tile):
+            for q in range(m + 1, p + 1):
+                factor[p, q] = factor[p, q] - factor[p, m] * factor[q, m]
+    for m in range(tile):
+        for p in range(m):
+            pivots[m] = pivots[m] - factor[m, p] * pivots[p]
+        pivots[m] = pivots[m] * roots[m]
+    for m in range(tile):
+        work[b] = jnp.where(sub == m, pivots[m], work[b])
+    for i in range(b + 1, len(work)):
+        ratio = column[i - b]
+        for m in range(tile):
+            for p in range(m):
+                ratio[m] = ratio[m] - ratio[p] * factor[m, p]
+            ratio[m] = ratio[m] * roots[m]
+            work[i] = work[i] - ratio[m] * pivots[m]
+
+
+def solve_kernel(
+    scale, holder, whole_ref, gram_ref, other_ref, out_hbm, out_ref, columns_ref, rows_ref, copied
+):
     part_rows, total, _ = whole_ref.shape
     blocks = total // tile
     half = total // 2
@@ -340,7 +382,6 @@
     packed = jnp.where(holds, gram_ref[...], other_ref[...])
     lane = iota((tile, lanes), 1)
     sub = iota((tile, lanes), 0)
-    shape = (tile, lanes)
     work = []
     for i in range(blocks):
         at = i * tile % half
@@ -349,50 +390,37 @@
             block = pltpu.roll(block, total, 1)
         unit = jnp.where(lane - total == sub + i * tile, 1.0, 0.0)
         work.append(jnp.where(lane < total, block, unit))
-    for b in range(blocks):
-        column = {
-            i: [
-                jnp.broadcast_to(work[i][:, b * tile + m : b * tile + m + 1], shape)
-                for m in range(tile)
-            ]
-            for i in range(b, blocks)
-        }
-        for m in range(tile):
-            pivot = jnp.broadcast_to(column[b][m][m : m + 1, :], shape)
-            root = lax.rsqrt(pivot)
-            row = jnp.broadcast_to(work[b][m : m + 1, :], shape) * root
-            heads = [
-                jnp.broadcast_to(column[b][p][m : m + 1, :], shape) * root
-                for p in range(m + 1, tile)
-            ]
-            for i in range(b, blocks):
-                ratio = column[i][m] * root
-                if i == b:
-                    ratio = jnp.where(sub > m, ratio, 0.0)
-                    work[i] = jnp.where(sub == m, row, work[i] - ratio * row)
-                else:
-                    work[i] = work[i] - ratio * row
-                for p in range(m + 1, tile):
-                    column[i][p] = column[i][p] - ratio * heads[p - m - 1]
-    solver = jnp.concatenate(work, axis=0) * scale
-    wide = iota((total, lanes), 1)
-    high, middle, low = (piece.astype(jnp.float32) for piece in split(solver))
-
-    def pair(left, right):
-        return jnp.where(wide < total, pltpu.roll(left, total, 1), right).astype(jnp.bfloat16)
-
-    left_main = jnp.concatenate([pair(high, high), pair(middle, middle)], axis=1)
-    left_rest = pair(high, low)
-    for row in range(0, part_rows, 2):
-        values = jnp.concatenate([whole_ref[row], whole_ref[row + 1]], axis=1)
-        f_high, f_middle, f_low = split(values)
-        right_main = jnp.concatenate([f_high, f_middle, f_high, f_middle], axis=0)
-        right_rest = jnp.concatenate([f_low, f_high], axis=0)
-        result = jnp.dot(left_rest, right_rest, preferred_element_type=jnp.float32) + jnp.dot(
-            left_main, right_main, preferred_element_type=jnp.float32
-        )
-        out_ref[pl.ds(row, total, stride=part_rows), :] = result[:, :lanes]
-        out_ref[pl.ds(row + 1, total, stride=part_rows), :] = result[:, lanes:]
+    copies = []
+    cuts = (0, 3 * blocks // 4, blocks)
+    for part, (first, last) in enumerate(zip(cuts, cuts[1:])):
+        for b in range(first, last):
+            eliminate(work, b, columns_ref, rows_ref)
+        solver = jnp.concatenate(work[first:last], axis=0) * scale
+        wide = iota(solver.shape, 1)
+        high, middle, low = (piece.astype(jnp.float32) for piece in split(solver))
+
+        def pair(left, right):
+            return jnp.where(wide < total, pltpu.roll(left, total, 1), right).astype(jnp.bfloat16)
+
+        left_main = jnp.concatenate([pair(high, high), pair(middle, middle)], axis=1)
+        left_rest = pair(high, low)
+        height = (last - first) * tile
+        base = first * tile * part_rows
+        for row in range(0, part_rows, 2):
+            values = jnp.concatenate([whole_ref[row], whole_ref[row + 1]], axis=1)
+            f_high, f_middle, f_low = split(values)
+            right_main = jnp.concatenate([f_high, f_middle, f_high, f_middle], axis=0)
+            right_rest = jnp.concatenate([f_low, f_high], axis=0)
+            result = jnp.dot(left_rest, right_rest, preferred_element_type=jnp.float32) + jnp.dot(
+                left_main, right_main, preferred_element_type=jnp.float32
+            )
+            out_ref[pl.ds(base + row, height, stride=part_rows), :] = result[:, :lanes]
+            out_ref[pl.ds(base + row + 1, height, stride=part_rows), :] = result[:, lanes:]
+        span = pl.ds(base, height * part_rows)
+        copies.append(pltpu.make_async_copy(out_ref.at[span], out_hbm.at[span], copied.at[part]))
+        copies[-1].start()
+    for copy in copies:
+        copy.wait()
 
 
 def call(kernel, outs, *operands, scratch=(), limit=32, **specs):
@@ -527,6 +555,13 @@
         whole,
         gram,
         exchange(gram, "ly", 1),
+        scratch=[
+            (total * part_rows, lanes),
+            (2, tile, tile, lanes),
+            (2, tile, lanes),
+            pltpu.SemaphoreType.DMA((2,)),
+        ],
+        out_specs=[pl.BlockSpec(memory_space=pl.ANY)],
     )
     return basis.reshape(total, part_rows, lanes)
 

time: 39.3 us -> 38.8 us (0.987)
  Pallas kernels: 6.81 us -> 6.4 us
    pallas_call x7, Pallas kernels: 6.81 us -> 6.4 us  [call(): pl.pallas_call(kernel, out_shape=[jax.ShapeDtypeStruct(shape, jnp.float32...]
where the time goes in v7:
time: 38.8 us; the launch traced here: 38.7 us
  starting transfers between devices  17 us (44%)
  waiting for transfers between devices  15.2 us (39%)
  Pallas kernels  6.4 us (16%)
    ppermute x11, starting transfers between devices, exchange(): return lax.ppermute(values, axis, [(i, i ^ distance) for i in range(count)])  9.75 us
    ppermute x11, waiting for transfers between devices, exchange(): return lax.ppermute(values, axis, [(i, i ^ distance) for i in range(count)])  7.16 us
    ppermute x4, waiting for transfers between devices, shards(): gram = near + lax.ppermute(gram, axes, handover(holder, axis, bit))  6.82 us
    pallas_call x7, Pallas kernels, call(): pl.pallas_call(kernel, out_shape=[jax.ShapeDtypeStruct(shape, jnp.float32...  6.4 us
    ppermute x4, starting transfers between devices, shards(): gram = near + lax.ppermute(gram, axes, handover(holder, axis, bit))  3.24 us
    ppermute x1, starting transfers between devices, shards(): far = lax.ppermute(edges, 'ly', far_pairs)  2.47 us
    ppermute x1, starting transfers between devices, shards(): lax.ppermute(outer, 'lx', [(i, (i + 1) % count) for i in range(count)])  1.56 us
    ppermute x1, waiting for transfers between devices, shards(): lax.ppermute(outer, 'lx', [(i, (i + 1) % count) for i in range(count)])  1.2 us
  transfers between devices with their start and end apart: 17, of which 9 were waited for; matrix products, arithmetic and copies ran while one was open for 0% of the time, Pallas kernels for 4%

profile of v7, /device:TPU:0, one launch (start us, length us, event | category | flops | bytes accessed | tf_op | source)
XLA Modules:
  0.0 38.7 jit_solution(15020917811914037878)
XLA Ops:
  0.0 1.5 %shard_map.28 = (f32[1024,128]{1,0:T(8,128)S(1)}, s32[64,128]{1,0:T(8,128)S(1)}, f32[5,8,128]{2,1,0:T(8,128)S(1)}, f32[5,8,128]{2,1,0:T(8,128)S(1)}, f32[16,16,128]{2,1,0:T(8,128)S(1)}) custom-call(f32[1024,128]{1,0:T(8,128)} %bitcast.2, s32[64,128]{1,0:T(8,128)} %levels_hbm.1), custom_call_target="tpu_custom_call" | custom-call | tf_op jit(solution)/shard_map/pallas_call | solution.py:427
  1.5 2.5 %collective-permute-start.1 = (f32[5,8,128]{2,1,0:T(8,128)S(1)}, f32[5,8,128]{2,1,0:T(8,128)S(1)}, u32[]{:S(2)}, u32[]{:S(2)}) collective-permute-start(f32[5,8,128]{2,1,0:T(8,128)S(1)} %get-tuple-element.24), channel_id=1, source_target_pairs={{0,12},{4,8},{8,4},{12,0},{1,13},{5,9},{9,5},{13,1},{2,14},{6,10},... | collective-permute-start | bytes 61448 | tf_op jit(solution)/shard_map/ppermute | solution.py:494
  4.0 0.7 %collective-permute-start = (f32[5,8,128]{2,1,0:T(8,128)S(1)}, f32[5,8,128]{2,1,0:T(8,128)S(1)}, u32[]{:S(2)}, u32[]{:S(2)}) collective-permute-start(f32[5,8,128]{2,1,0:T(8,128)S(1)} %get-tuple-element.24), channel_id=1, source_target_pairs={{0,4},{4,0},{8,12},{12,8},{1,5},{5,1},{9,13},{13,9},{2,6},{6,2},{1... | collective-permute-start | bytes 61448 | tf_op jit(solution)/shard_map/ppermute | solution.py:444
  4.7 2.6 %collective-permute-start.6 = (f32[16,16,128]{2,1,0:T(8,128)S(1)}, f32[16,16,128]{2,1,0:T(8,128)S(1)}, u32[]{:S(2)}, u32[]{:S(2)}) collective-permute-start(f32[16,16,128]{2,1,0:T(8,128)S(1)} %get-tuple-element.34), channel_id=1, source_target_pairs={{0,2},{1,3},{2,0},{3,1},{4,6},{5,7},{6,4},{7,5},{8,10},{9,11},{10,... | collective-permute-start | bytes 393224 | tf_op jit(solution)/shard_map/ppermute | solution.py:444
  7.2 0.0 collective-permute-done.near_ref
  7.3 1.6 %collective-permute-start.2 = (f32[7,8,128]{2,1,0:T(8,128)S(1)}, f32[7,8,128]{2,1,0:T(8,128)S(1)}, u32[]{:S(2)}, u32[]{:S(2)}) collective-permute-start(f32[7,8,128]{2,1,0:T(8,128)S(1)} %get-tuple-element.29), channel_id=1, source_target_pairs={{0,16},{16,0},{1,17},{17,1},{2,18},{18,2},{3,19},{19,3},{4,20},{20... | collective-permute-start | bytes 86024 | tf_op jit(solution)/shard_map/ppermute | solution.py:504
  8.8 1.2 %shard_map.30 = (f32[64,16,128]{2,1,0:T(8,128)S(1)}, f32[2,16,128]{2,1,0:T(8,128)S(1)}, f32[1,8,128]{2,1,0:T(8,128)S(1)}) custom-call(f32[1024,128]{1,0:T(8,128)S(1)} %get-tuple-element.21.start_ref, s32[64,128]{1,0:T(8,128)S(1)} %get-tuple-element.22.levels_ref, f32[5,8,128]{2,1,0:T(8,128)S(1)} %get-tuple-element.25.beside_ref), custom_call_target="tpu_custom_call" | custom-call | flops 99999997952 | bytes 1000000000 | tf_op jit(solution)/shard_map/pallas_call | solution.py:427
  10.0 1.2 %collective-permute-done.2.before_ref.after_ref = f32[7,8,128]{2,1,0:T(8,128)S(1)} collective-permute-done((f32[7,8,128]{2,1,0:T(8,128)S(1)}, f32[7,8,128]{2,1,0:T(8,128)S(1)}, u32[]{:S(2)}, u32[]{:S(2)}) %collective-permute-start.2) | collective-permute-done | bytes 28704 | tf_op jit(solution)/shard_map/ppermute | solution.py:504
  11.2 0.2 shard_map.31
  11.4 2.8 %collective-permute-start.3 = (f32[16,16,128]{2,1,0:T(8,128)S(1)}, f32[16,16,128]{2,1,0:T(8,128)S(1)}, u32[]{:S(2)}, u32[]{:S(2)}) collective-permute-start(f32[16,16,128]{2,1,0:T(8,128)S(1)} %get-tuple-element.30), channel_id=1, source_target_pairs={{0,3},{1,2},{2,1},{3,0},{4,7},{5,6},{6,5},{7,4},{8,11},{9,10},{10,... | collective-permute-start | bytes 393224 | tf_op jit(solution)/shard_map/ppermute | solution.py:444
  14.2 0.0 collective-permute-start.4
  14.2 1.7 %collective-permute-start.5 = (f32[5,8,128]{2,1,0:T(8,128)S(1)}, f32[5,8,128]{2,1,0:T(8,128)S(1)}, u32[]{:S(2)}, u32[]{:S(2)}) collective-permute-start(f32[5,8,128]{2,1,0:T(8,128)S(1)} %get-tuple-element.32), channel_id=1, source_target_pairs={{0,2},{1,3},{2,0},{3,1},{4,6},{5,7},{6,4},{7,5},{8,10},{9,11},{10,... | collective-permute-start | bytes 61448 | tf_op jit(solution)/shard_map/ppermute | solution.py:444
  15.9 0.2 shard_map.32.refs_4_
  16.1 4.2 %collective-permute-done.5.refs_2_ = f32[5,8,128]{2,1,0:T(8,128)S(1)} collective-permute-done((f32[5,8,128]{2,1,0:T(8,128)S(1)}, f32[5,8,128]{2,1,0:T(8,128)S(1)}, u32[]{:S(2)}, u32[]{:S(2)}) %collective-permute-start.5) | collective-permute-done | bytes 20512 | tf_op jit(solution)/shard_map/ppermute | solution.py:444
  20.4 0.6 %collective-permute-done.4.refs_1_ = f32[16,16,128]{2,1,0:T(8,128)S(1)} collective-permute-done((f32[16,16,128]{2,1,0:T(8,128)S(1)}, f32[16,16,128]{2,1,0:T(8,128)S(1)}, u32[]{:S(2)}, u32[]{:S(2)}) %collective-permute-start.4) | collective-permute-done | bytes 131104 | tf_op jit(solution)/shard_map/ppermute | solution.py:444
  20.9 0.6 %shard_map.33 = (f32[16,64,128]{2,1,0:T(8,128)S(1)}, f32[32,128]{1,0:T(8,128)S(1)}) custom-call(f32[16,16,128]{2,1,0:T(8,128)S(1)} %collective-permute-done.3.refs_0_, f32[16,16,128]{2,1,0:T(8,128)S(1)} %collective-permute-done.4.refs_1_, f32[5,8,128]{2,1,0:T(8,128)S(1)} %collective-permute-done.5.refs_2_, f32[16,16,128]{2,1,0:T(8,128)S(1)} %get-tuple-element.33.refs_3_, ...), custom_call_target="tpu_custom_call" | custom-call | tf_op jit(solution)/shard_map/pallas_call | solution.py:427
  21.6 0.0 collective-permute-start.7
  21.6 1.2 %collective-permute-done.7 = f32[32,128]{1,0:T(8,128)S(1)} collective-permute-done((f32[32,128]{1,0:T(8,128)S(1)}, f32[32,128]{1,0:T(8,128)S(1)}, u32[]{:S(2)}, u32[]{:S(2)}) %collective-permute-start.7) | collective-permute-done | bytes 16416 | tf_op jit(solution)/shard_map/ppermute | solution.py:444
  22.8 0.9 %collective-permute-start.9 = (f32[32,128]{1,0:T(8,128)S(1)}, f32[32,128]{1,0:T(8,128)S(1)}, u32[]{:S(2)}, u32[]{:S(2)}) collective-permute-start(f32[32,128]{1,0:T(8,128)S(1)} %add.15), channel_id=1, source_target_pairs={{0,12},{1,13},{2,14},{3,15},{4,0},{5,1},{6,2},{7,3},{8,4},{9,5},{1... | collective-permute-start | bytes 49160 | tf_op jit(solution)/shard_map/ppermute | solution.py:549
  23.7 1.4 %collective-permute-done.9 = f32[32,128]{1,0:T(8,128)S(1)} collective-permute-done((f32[32,128]{1,0:T(8,128)S(1)}, f32[32,128]{1,0:T(8,128)S(1)}, u32[]{:S(2)}, u32[]{:S(2)}) %collective-permute-start.9) | collective-permute-done | bytes 16416 | tf_op jit(solution)/shard_map/ppermute | solution.py:549
  25.2 1.0 %collective-permute-start.11 = (f32[32,128]{1,0:T(8,128)S(1)}, f32[32,128]{1,0:T(8,128)S(1)}, u32[]{:S(2)}, u32[]{:S(2)}) collective-permute-start(f32[32,128]{1,0:T(8,128)S(1)} %add.16), channel_id=1, source_target_pairs={{0,4},{1,5},{2,6},{3,7},{4,16},{5,17},{6,18},{7,19},{8,12},{9,13},... | collective-permute-start | bytes 49160 | tf_op jit(solution)/shard_map/ppermute | solution.py:549
  26.2 0.6 %collective-permute-start.10 = (f32[32,128]{1,0:T(8,128)S(1)}, f32[32,128]{1,0:T(8,128)S(1)}, u32[]{:S(2)}, u32[]{:S(2)}) collective-permute-start(f32[32,128]{1,0:T(8,128)S(1)} %add.16), channel_id=1, source_target_pairs={{0,4},{4,0},{8,12},{12,8},{1,5},{5,1},{9,13},{13,9},{2,6},{6,2},{1... | collective-permute-start | bytes 49160 | tf_op jit(solution)/shard_map/ppermute | solution.py:444
  26.8 1.9 %collective-permute-done.11 = f32[32,128]{1,0:T(8,128)S(1)} collective-permute-done((f32[32,128]{1,0:T(8,128)S(1)}, f32[32,128]{1,0:T(8,128)S(1)}, u32[]{:S(2)}, u32[]{:S(2)}) %collective-permute-start.11) | collective-permute-done | bytes 16416 | tf_op jit(solution)/shard_map/ppermute | solution.py:549
  28.7 0.3 collective-permute-start.13
  29.0 0.2 collective-permute-start.12
  29.3 1.2 %collective-permute-done.13 = f32[32,128]{1,0:T(8,128)S(1)} collective-permute-done((f32[32,128]{1,0:T(8,128)S(1)}, f32[32,128]{1,0:T(8,128)S(1)}, u32[]{:S(2)}, u32[]{:S(2)}) %collective-permute-start.13) | collective-permute-done | bytes 16416 | tf_op jit(solution)/shard_map/ppermute | solution.py:549
  30.5 1.0 %collective-permute-start.15 = (f32[32,128]{1,0:T(8,128)S(1)}, f32[32,128]{1,0:T(8,128)S(1)}, u32[]{:S(2)}, u32[]{:S(2)}) collective-permute-start(f32[32,128]{1,0:T(8,128)S(1)} %add.18), channel_id=1, source_target_pairs={{0,4},{1,5},{2,6},{3,7},{4,2},{5,3},{6,0},{7,1},{8,12},{9,13},{10,... | collective-permute-start | bytes 49160 | tf_op jit(solution)/shard_map/ppermute | solution.py:549
  31.5 1.1 %collective-permute-start.14 = (f32[32,128]{1,0:T(8,128)S(1)}, f32[32,128]{1,0:T(8,128)S(1)}, u32[]{:S(2)}, u32[]{:S(2)}) collective-permute-start(f32[32,128]{1,0:T(8,128)S(1)} %add.18), channel_id=1, source_target_pairs={{0,4},{4,0},{8,12},{12,8},{1,5},{5,1},{9,13},{13,9},{2,6},{6,2},{1... | collective-permute-start | bytes 49160 | tf_op jit(solution)/shard_map/ppermute | solution.py:444
  32.6 2.2 %collective-permute-done.15 = f32[32,128]{1,0:T(8,128)S(1)} collective-permute-done((f32[32,128]{1,0:T(8,128)S(1)}, f32[32,128]{1,0:T(8,128)S(1)}, u32[]{:S(2)}, u32[]{:S(2)}) %collective-permute-start.15) | collective-permute-done | bytes 16416 | tf_op jit(solution)/shard_map/ppermute | solution.py:549
  34.8 0.1 collective-permute-start.16
  34.9 1.2 %collective-permute-done.16.other_ref = f32[32,128]{1,0:T(8,128)S(1)} collective-permute-done((f32[32,128]{1,0:T(8,128)S(1)}, f32[32,128]{1,0:T(8,128)S(1)}, u32[]{:S(2)}, u32[]{:S(2)}) %collective-permute-start.16) | collective-permute-done | bytes 16416 | tf_op jit(solution)/shard_map/ppermute | solution.py:444
  36.1 2.6 %shard_map.34 = f32[1024,128]{1,0:T(8,128)} custom-call(f32[16,64,128]{2,1,0:T(8,128)S(1)} %get-tuple-element.35.whole_ref, f32[32,128]{1,0:T(8,128)S(1)} %add.19.gram_ref, f32[32,128]{1,0:T(8,128)S(1)} %collective-permute-done.16.other_ref), custom_call_target="tpu_custom_call" | custom-call | tf_op jit(solution)/shard_map/pallas_call | solution.py:427
  (14 shorter events, 0.1 us)
Async XLA Ops:
  1.5 5.7 %collective-permute-start.1 = (f32[5,8,128]{2,1,0:T(8,128)S(1)}, f32[5,8,128]{2,1,0:T(8,128)S(1)}, u32[]{:S(2)}, u32[]{:S(2)}) collective-permute-start(f32[5,8,128]{2,1,0:T(8,128)S(1)} %get-tuple-element.24), channel_id=1, source_target_pairs={{0,12},{4,8},{8,4},{12,0},{1,13},{5,9},{9,5},{13,1},{2,14},{6,10},... | collective-permute-start | bytes 61448 | tf_op jit(solution)/shard_map/ppermute | solution.py:494
  4.0 3.3 %collective-permute-start = (f32[5,8,128]{2,1,0:T(8,128)S(1)}, f32[5,8,128]{2,1,0:T(8,128)S(1)}, u32[]{:S(2)}, u32[]{:S(2)}) collective-permute-start(f32[5,8,128]{2,1,0:T(8,128)S(1)} %get-tuple-element.24), channel_id=1, source_target_pairs={{0,4},{4,0},{8,12},{12,8},{1,5},{5,1},{9,13},{13,9},{2,6},{6,2},{1... | collective-permute-start | bytes 61448 | tf_op jit(solution)/shard_map/ppermute | solution.py:444
  4.7 11.3 %collective-permute-start.6 = (f32[16,16,128]{2,1,0:T(8,128)S(1)}, f32[16,16,128]{2,1,0:T(8,128)S(1)}, u32[]{:S(2)}, u32[]{:S(2)}) collective-permute-start(f32[16,16,128]{2,1,0:T(8,128)S(1)} %get-tuple-element.34), channel_id=1, source_target_pairs={{0,2},{1,3},{2,0},{3,1},{4,6},{5,7},{6,4},{7,5},{8,10},{9,11},{10,... | collective-permute-start | bytes 393224 | tf_op jit(solution)/shard_map/ppermute | solution.py:444
  7.3 3.9 %collective-permute-start.2 = (f32[7,8,128]{2,1,0:T(8,128)S(1)}, f32[7,8,128]{2,1,0:T(8,128)S(1)}, u32[]{:S(2)}, u32[]{:S(2)}) collective-permute-start(f32[7,8,128]{2,1,0:T(8,128)S(1)} %get-tuple-element.29), channel_id=1, source_target_pairs={{0,16},{16,0},{1,17},{17,1},{2,18},{18,2},{3,19},{19,3},{4,20},{20... | collective-permute-start | bytes 86024 | tf_op jit(solution)/shard_map/ppermute | solution.py:504
  11.4 8.9 %collective-permute-start.3 = (f32[16,16,128]{2,1,0:T(8,128)S(1)}, f32[16,16,128]{2,1,0:T(8,128)S(1)}, u32[]{:S(2)}, u32[]{:S(2)}) collective-permute-start(f32[16,16,128]{2,1,0:T(8,128)S(1)} %get-tuple-element.30), channel_id=1, source_target_pairs={{0,3},{1,2},{2,1},{3,0},{4,7},{5,6},{6,5},{7,4},{8,11},{9,10},{10,... | collective-permute-start | bytes 393224 | tf_op jit(solution)/shard_map/ppermute | solution.py:444
  14.2 6.7 %collective-permute-start.4 = (f32[16,16,128]{2,1,0:T(8,128)S(1)}, f32[16,16,128]{2,1,0:T(8,128)S(1)}, u32[]{:S(2)}, u32[]{:S(2)}) collective-permute-start(f32[16,16,128]{2,1,0:T(8,128)S(1)} %get-tuple-element.31), channel_id=1, source_target_pairs={{0,1},{1,0},{2,3},{3,2},{4,5},{5,4},{6,7},{7,6},{8,9},{9,8},{10,11... | collective-permute-start | bytes 393224 | tf_op jit(solution)/shard_map/ppermute | solution.py:444
  14.2 6.1 %collective-permute-start.5 = (f32[5,8,128]{2,1,0:T(8,128)S(1)}, f32[5,8,128]{2,1,0:T(8,128)S(1)}, u32[]{:S(2)}, u32[]{:S(2)}) collective-permute-start(f32[5,8,128]{2,1,0:T(8,128)S(1)} %get-tuple-element.32), channel_id=1, source_target_pairs={{0,2},{1,3},{2,0},{3,1},{4,6},{5,7},{6,4},{7,5},{8,10},{9,11},{10,... | collective-permute-start | bytes 61448 | tf_op jit(solution)/shard_map/ppermute | solution.py:444
  21.6 1.2 %collective-permute-start.7 = (f32[32,128]{1,0:T(8,128)S(1)}, f32[32,128]{1,0:T(8,128)S(1)}, u32[]{:S(2)}, u32[]{:S(2)}) collective-permute-start(f32[32,128]{1,0:T(8,128)S(1)} %get-tuple-element.36), channel_id=1, source_target_pairs={{0,4},{4,0},{8,12},{12,8},{1,5},{5,1},{9,13},{13,9},{2,6},{6,2},{1... | collective-permute-start | bytes 49160 | tf_op jit(solution)/shard_map/ppermute | solution.py:444
  22.8 2.4 %collective-permute-start.9 = (f32[32,128]{1,0:T(8,128)S(1)}, f32[32,128]{1,0:T(8,128)S(1)}, u32[]{:S(2)}, u32[]{:S(2)}) collective-permute-start(f32[32,128]{1,0:T(8,128)S(1)} %add.15), channel_id=1, source_target_pairs={{0,12},{1,13},{2,14},{3,15},{4,0},{5,1},{6,2},{7,3},{8,4},{9,5},{1... | collective-permute-start | bytes 49160 | tf_op jit(solution)/shard_map/ppermute | solution.py:549
  23.7 1.4 %collective-permute-start.8 = (f32[32,128]{1,0:T(8,128)S(1)}, f32[32,128]{1,0:T(8,128)S(1)}, u32[]{:S(2)}, u32[]{:S(2)}) collective-permute-start(f32[32,128]{1,0:T(8,128)S(1)} %add.15), channel_id=1, source_target_pairs={{0,4},{4,0},{8,12},{12,8},{1,5},{5,1},{9,13},{13,9},{2,6},{6,2},{1... | collective-permute-start | bytes 49160 | tf_op jit(solution)/shard_map/ppermute | solution.py:444
  25.2 3.5 %collective-permute-start.11 = (f32[32,128]{1,0:T(8,128)S(1)}, f32[32,128]{1,0:T(8,128)S(1)}, u32[]{:S(2)}, u32[]{:S(2)}) collective-permute-start(f32[32,128]{1,0:T(8,128)S(1)} %add.16), channel_id=1, source_target_pairs={{0,4},{1,5},{2,6},{3,7},{4,16},{5,17},{6,18},{7,19},{8,12},{9,13},... | collective-permute-start | bytes 49160 | tf_op jit(solution)/shard_map/ppermute | solution.py:549
  26.2 2.5 %collective-permute-start.10 = (f32[32,128]{1,0:T(8,128)S(1)}, f32[32,128]{1,0:T(8,128)S(1)}, u32[]{:S(2)}, u32[]{:S(2)}) collective-permute-start(f32[32,128]{1,0:T(8,128)S(1)} %add.16), channel_id=1, source_target_pairs={{0,4},{4,0},{8,12},{12,8},{1,5},{5,1},{9,13},{13,9},{2,6},{6,2},{1... | collective-permute-start | bytes 49160 | tf_op jit(solution)/shard_map/ppermute | solution.py:444
  28.7 1.8 %collective-permute-start.13 = (f32[32,128]{1,0:T(8,128)S(1)}, f32[32,128]{1,0:T(8,128)S(1)}, u32[]{:S(2)}, u32[]{:S(2)}) collective-permute-start(f32[32,128]{1,0:T(8,128)S(1)} %add.17), channel_id=1, source_target_pairs={{0,5},{1,4},{2,7},{3,6},{4,0},{5,1},{6,2},{7,3},{8,13},{9,12},{10,... | collective-permute-start | bytes 49160 | tf_op jit(solution)/shard_map/ppermute | solution.py:549
  29.0 1.4 %collective-permute-start.12 = (f32[32,128]{1,0:T(8,128)S(1)}, f32[32,128]{1,0:T(8,128)S(1)}, u32[]{:S(2)}, u32[]{:S(2)}) collective-permute-start(f32[32,128]{1,0:T(8,128)S(1)} %add.17), channel_id=1, source_target_pairs={{0,4},{4,0},{8,12},{12,8},{1,5},{5,1},{9,13},{13,9},{2,6},{6,2},{1... | collective-permute-start | bytes 49160 | tf_op jit(solution)/shard_map/ppermute | solution.py:444
  30.5 4.3 %collective-permute-start.15 = (f32[32,128]{1,0:T(8,128)S(1)}, f32[32,128]{1,0:T(8,128)S(1)}, u32[]{:S(2)}, u32[]{:S(2)}) collective-permute-start(f32[32,128]{1,0:T(8,128)S(1)} %add.18), channel_id=1, source_target_pairs={{0,4},{1,5},{2,6},{3,7},{4,2},{5,3},{6,0},{7,1},{8,12},{9,13},{10,... | collective-permute-start | bytes 49160 | tf_op jit(solution)/shard_map/ppermute | solution.py:549
  31.5 3.4 %collective-permute-start.14 = (f32[32,128]{1,0:T(8,128)S(1)}, f32[32,128]{1,0:T(8,128)S(1)}, u32[]{:S(2)}, u32[]{:S(2)}) collective-permute-start(f32[32,128]{1,0:T(8,128)S(1)} %add.18), channel_id=1, source_target_pairs={{0,4},{4,0},{8,12},{12,8},{1,5},{5,1},{9,13},{13,9},{2,6},{6,2},{1... | collective-permute-start | bytes 49160 | tf_op jit(solution)/shard_map/ppermute | solution.py:444
  34.8 1.2 %collective-permute-start.16 = (f32[32,128]{1,0:T(8,128)S(1)}, f32[32,128]{1,0:T(8,128)S(1)}, u32[]{:S(2)}, u32[]{:S(2)}) collective-permute-start(f32[32,128]{1,0:T(8,128)S(1)} %add.19.gram_ref), channel_id=1, source_target_pairs={{0,4},{4,0},{8,12},{12,8},{1,5},{5,1},{9,13},{13,9},{2,6},{6,2},{1... | collective-permute-start | bytes 49160 | tf_op jit(solution)/shard_map/ppermute | solution.py:444

commit v8 on v7

--- a/solution.py
+++ b/solution.py
@@ -475,7 +475,7 @@
     total = cols * parts
     part_rows = rows // parts
     sizes = (cols, rows, parts)
-    early = (parts // 2,)
+    early = (parts - 1,)
     order = (*sorted(range(1, parts), key=lambda k: (k in early, -k)), 0)
     flat = start.reshape(cols * rows, lanes)
     piece = (part_rows, cols, lanes)

time: 38.8 us -> 38.3 us (0.987)
  waiting for transfers between devices: 15.2 us -> 13.4 us
  starting transfers between devices: 17 us -> 18.2 us
    ppermute x11, starting transfers between devices: 9.75 us -> 11.2 us  [exchange(): return lax.ppermute(values, axis, [(i, i ^ distance) for i in range(count)])]
    ppermute x11, waiting for transfers between devices: 7.16 us -> 6.07 us  [exchange(): return lax.ppermute(values, axis, [(i, i ^ distance) for i in range(count)])]
    ppermute x4, waiting for transfers between devices: 6.82 us -> 6.16 us  [shards(): gram = near + lax.ppermute(gram, axes, handover(holder, axis, bit))]
where the time goes in v8:
time: 38.3 us; the launch traced here: 38.1 us
  starting transfers between devices  18.2 us (48%)
  waiting for transfers between devices  13.4 us (35%)
  Pallas kernels  6.39 us (17%)
    ppermute x11, starting transfers between devices, exchange(): return lax.ppermute(values, axis, [(i, i ^ distance) for i in range(count)])  11.2 us
    pallas_call x7, Pallas kernels, call(): pl.pallas_call(kernel, out_shape=[jax.ShapeDtypeStruct(shape, jnp.float32...  6.39 us
    ppermute x4, waiting for transfers between devices, shards(): gram = near + lax.ppermute(gram, axes, handover(holder, axis, bit))  6.16 us
    ppermute x11, waiting for transfers between devices, exchange(): return lax.ppermute(values, axis, [(i, i ^ distance) for i in range(count)])  6.07 us
    ppermute x4, starting transfers between devices, shards(): gram = near + lax.ppermute(gram, axes, handover(holder, axis, bit))  3 us
    ppermute x1, starting transfers between devices, shards(): far = lax.ppermute(edges, 'ly', far_pairs)  2.47 us
    ppermute x1, starting transfers between devices, shards(): lax.ppermute(outer, 'lx', [(i, (i + 1) % count) for i in range(count)])  1.56 us
    ppermute x1, waiting for transfers between devices, shards(): lax.ppermute(outer, 'lx', [(i, (i + 1) % count) for i in range(count)])  1.2 us
  transfers between devices with their start and end apart: 17, of which 9 were waited for; matrix products, arithmetic and copies ran while one was open for 0% of the time, Pallas kernels for 4%

profile of v8, /device:TPU:0, one launch (start us, length us, event | category | flops | bytes accessed | tf_op | source)
XLA Modules:
  0.0 38.1 jit_solution(14541373038673891900)
XLA Ops:
  0.0 1.5 %shard_map.28 = (f32[1024,128]{1,0:T(8,128)S(1)}, s32[64,128]{1,0:T(8,128)S(1)}, f32[5,8,128]{2,1,0:T(8,128)S(1)}, f32[5,8,128]{2,1,0:T(8,128)S(1)}, f32[16,16,128]{2,1,0:T(8,128)S(1)}) custom-call(f32[1024,128]{1,0:T(8,128)} %bitcast.2, s32[64,128]{1,0:T(8,128)} %levels_hbm.1), custom_call_target="tpu_custom_call" | custom-call | tf_op jit(solution)/shard_map/pallas_call | solution.py:427
  1.5 2.5 %collective-permute-start.1 = (f32[5,8,128]{2,1,0:T(8,128)S(1)}, f32[5,8,128]{2,1,0:T(8,128)S(1)}, u32[]{:S(2)}, u32[]{:S(2)}) collective-permute-start(f32[5,8,128]{2,1,0:T(8,128)S(1)} %get-tuple-element.24), channel_id=1, source_target_pairs={{0,12},{4,8},{8,4},{12,0},{1,13},{5,9},{9,5},{13,1},{2,14},{6,10},... | collective-permute-start | bytes 61448 | tf_op jit(solution)/shard_map/ppermute | solution.py:494
  4.0 0.7 %collective-permute-start = (f32[5,8,128]{2,1,0:T(8,128)S(1)}, f32[5,8,128]{2,1,0:T(8,128)S(1)}, u32[]{:S(2)}, u32[]{:S(2)}) collective-permute-start(f32[5,8,128]{2,1,0:T(8,128)S(1)} %get-tuple-element.24), channel_id=1, source_target_pairs={{0,4},{4,0},{8,12},{12,8},{1,5},{5,1},{9,13},{13,9},{2,6},{6,2},{1... | collective-permute-start | bytes 61448 | tf_op jit(solution)/shard_map/ppermute | solution.py:444
  4.7 3.6 %collective-permute-start.6 = (f32[16,16,128]{2,1,0:T(8,128)S(1)}, f32[16,16,128]{2,1,0:T(8,128)S(1)}, u32[]{:S(2)}, u32[]{:S(2)}) collective-permute-start(f32[16,16,128]{2,1,0:T(8,128)S(1)} %get-tuple-element.34), channel_id=1, source_target_pairs={{0,3},{1,2},{2,1},{3,0},{4,7},{5,6},{6,5},{7,4},{8,11},{9,10},{10,... | collective-permute-start | bytes 393224 | tf_op jit(solution)/shard_map/ppermute | solution.py:444
  8.3 0.0 collective-permute-done.1.far_ref
  8.3 1.6 %collective-permute-start.2 = (f32[7,8,128]{2,1,0:T(8,128)S(1)}, f32[7,8,128]{2,1,0:T(8,128)S(1)}, u32[]{:S(2)}, u32[]{:S(2)}) collective-permute-start(f32[7,8,128]{2,1,0:T(8,128)S(1)} %get-tuple-element.29), channel_id=1, source_target_pairs={{0,16},{16,0},{1,17},{17,1},{2,18},{18,2},{3,19},{19,3},{4,20},{20... | collective-permute-start | bytes 86024 | tf_op jit(solution)/shard_map/ppermute | solution.py:504
  9.8 1.2 %shard_map.30 = (f32[64,16,128]{2,1,0:T(8,128)S(1)}, f32[2,16,128]{2,1,0:T(8,128)S(1)}, f32[1,8,128]{2,1,0:T(8,128)S(1)}) custom-call(f32[1024,128]{1,0:T(8,128)S(1)} %get-tuple-element.21.start_ref, s32[64,128]{1,0:T(8,128)S(1)} %get-tuple-element.22.levels_ref, f32[5,8,128]{2,1,0:T(8,128)S(1)} %get-tuple-element.25.beside_ref), custom_call_target="tpu_custom_call" | custom-call | flops 99999997952 | bytes 1000000000 | tf_op jit(solution)/shard_map/pallas_call | solution.py:427
  11.0 1.2 %collective-permute-done.2.before_ref.after_ref = f32[7,8,128]{2,1,0:T(8,128)S(1)} collective-permute-done((f32[7,8,128]{2,1,0:T(8,128)S(1)}, f32[7,8,128]{2,1,0:T(8,128)S(1)}, u32[]{:S(2)}, u32[]{:S(2)}) %collective-permute-start.2) | collective-permute-done | bytes 28704 | tf_op jit(solution)/shard_map/ppermute | solution.py:504
  12.2 0.2 shard_map.31
  12.5 0.8 %collective-permute-start.3 = (f32[16,16,128]{2,1,0:T(8,128)S(1)}, f32[16,16,128]{2,1,0:T(8,128)S(1)}, u32[]{:S(2)}, u32[]{:S(2)}) collective-permute-start(f32[16,16,128]{2,1,0:T(8,128)S(1)} %get-tuple-element.30), channel_id=1, source_target_pairs={{0,2},{1,3},{2,0},{3,1},{4,6},{5,7},{6,4},{7,5},{8,10},{9,11},{10,... | collective-permute-start | bytes 393224 | tf_op jit(solution)/shard_map/ppermute | solution.py:444
  13.2 1.6 %collective-permute-start.4 = (f32[16,16,128]{2,1,0:T(8,128)S(1)}, f32[16,16,128]{2,1,0:T(8,128)S(1)}, u32[]{:S(2)}, u32[]{:S(2)}) collective-permute-start(f32[16,16,128]{2,1,0:T(8,128)S(1)} %get-tuple-element.31), channel_id=1, source_target_pairs={{0,1},{1,0},{2,3},{3,2},{4,5},{5,4},{6,7},{7,6},{8,9},{9,8},{10,11... | collective-permute-start | bytes 393224 | tf_op jit(solution)/shard_map/ppermute | solution.py:444
  14.8 2.1 %collective-permute-start.5 = (f32[5,8,128]{2,1,0:T(8,128)S(1)}, f32[5,8,128]{2,1,0:T(8,128)S(1)}, u32[]{:S(2)}, u32[]{:S(2)}) collective-permute-start(f32[5,8,128]{2,1,0:T(8,128)S(1)} %get-tuple-element.32), channel_id=1, source_target_pairs={{0,3},{1,2},{2,1},{3,0},{4,7},{5,6},{6,5},{7,4},{8,11},{9,10},{10,... | collective-permute-start | bytes 61448 | tf_op jit(solution)/shard_map/ppermute | solution.py:444
  16.9 0.2 shard_map.32.refs_4_
  17.1 3.6 %collective-permute-done.5.refs_2_ = f32[5,8,128]{2,1,0:T(8,128)S(1)} collective-permute-done((f32[5,8,128]{2,1,0:T(8,128)S(1)}, f32[5,8,128]{2,1,0:T(8,128)S(1)}, u32[]{:S(2)}, u32[]{:S(2)}) %collective-permute-start.5) | collective-permute-done | bytes 20512 | tf_op jit(solution)/shard_map/ppermute | solution.py:444
  20.7 0.1 collective-permute-done.4.refs_1_
  20.9 0.6 %shard_map.33 = (f32[16,64,128]{2,1,0:T(8,128)S(1)}, f32[32,128]{1,0:T(8,128)S(1)}) custom-call(f32[16,16,128]{2,1,0:T(8,128)S(1)} %collective-permute-done.3.refs_0_, f32[16,16,128]{2,1,0:T(8,128)S(1)} %collective-permute-done.4.refs_1_, f32[5,8,128]{2,1,0:T(8,128)S(1)} %collective-permute-done.5.refs_2_, f32[16,16,128]{2,1,0:T(8,128)S(1)} %get-tuple-element.33.refs_3_, ...), custom_call_target="tpu_custom_call" | custom-call | tf_op jit(solution)/shard_map/pallas_call | solution.py:427
  21.5 0.0 collective-permute-start.7
  21.5 1.2 %collective-permute-done.7 = f32[32,128]{1,0:T(8,128)S(1)} collective-permute-done((f32[32,128]{1,0:T(8,128)S(1)}, f32[32,128]{1,0:T(8,128)S(1)}, u32[]{:S(2)}, u32[]{:S(2)}) %collective-permute-start.7) | collective-permute-done | bytes 16416 | tf_op jit(solution)/shard_map/ppermute | solution.py:444
  22.7 1.0 %collective-permute-start.9 = (f32[32,128]{1,0:T(8,128)S(1)}, f32[32,128]{1,0:T(8,128)S(1)}, u32[]{:S(2)}, u32[]{:S(2)}) collective-permute-start(f32[32,128]{1,0:T(8,128)S(1)} %add.15), channel_id=1, source_target_pairs={{0,12},{1,13},{2,14},{3,15},{4,0},{5,1},{6,2},{7,3},{8,4},{9,5},{1... | collective-permute-start | bytes 49160 | tf_op jit(solution)/shard_map/ppermute | solution.py:549
  23.7 1.4 %collective-permute-done.9 = f32[32,128]{1,0:T(8,128)S(1)} collective-permute-done((f32[32,128]{1,0:T(8,128)S(1)}, f32[32,128]{1,0:T(8,128)S(1)}, u32[]{:S(2)}, u32[]{:S(2)}) %collective-permute-start.9) | collective-permute-done | bytes 16416 | tf_op jit(solution)/shard_map/ppermute | solution.py:549
  25.1 1.0 %collective-permute-start.11 = (f32[32,128]{1,0:T(8,128)S(1)}, f32[32,128]{1,0:T(8,128)S(1)}, u32[]{:S(2)}, u32[]{:S(2)}) collective-permute-start(f32[32,128]{1,0:T(8,128)S(1)} %add.16), channel_id=1, source_target_pairs={{0,4},{1,5},{2,6},{3,7},{4,16},{5,17},{6,18},{7,19},{8,12},{9,13},... | collective-permute-start | bytes 49160 | tf_op jit(solution)/shard_map/ppermute | solution.py:549
  26.1 0.6 %collective-permute-start.10 = (f32[32,128]{1,0:T(8,128)S(1)}, f32[32,128]{1,0:T(8,128)S(1)}, u32[]{:S(2)}, u32[]{:S(2)}) collective-permute-start(f32[32,128]{1,0:T(8,128)S(1)} %add.16), channel_id=1, source_target_pairs={{0,4},{4,0},{8,12},{12,8},{1,5},{5,1},{9,13},{13,9},{2,6},{6,2},{1... | collective-permute-start | bytes 49160 | tf_op jit(solution)/shard_map/ppermute | solution.py:444
  26.7 1.9 %collective-permute-done.11 = f32[32,128]{1,0:T(8,128)S(1)} collective-permute-done((f32[32,128]{1,0:T(8,128)S(1)}, f32[32,128]{1,0:T(8,128)S(1)}, u32[]{:S(2)}, u32[]{:S(2)}) %collective-permute-start.11) | collective-permute-done | bytes 16416 | tf_op jit(solution)/shard_map/ppermute | solution.py:549
  28.6 0.1 collective-permute-start.13
  28.7 0.5 %collective-permute-start.12 = (f32[32,128]{1,0:T(8,128)S(1)}, f32[32,128]{1,0:T(8,128)S(1)}, u32[]{:S(2)}, u32[]{:S(2)}) collective-permute-start(f32[32,128]{1,0:T(8,128)S(1)} %add.17), channel_id=1, source_target_pairs={{0,4},{4,0},{8,12},{12,8},{1,5},{5,1},{9,13},{13,9},{2,6},{6,2},{1... | collective-permute-start | bytes 49160 | tf_op jit(solution)/shard_map/ppermute | solution.py:444
  29.2 0.9 %collective-permute-done.13 = f32[32,128]{1,0:T(8,128)S(1)} collective-permute-done((f32[32,128]{1,0:T(8,128)S(1)}, f32[32,128]{1,0:T(8,128)S(1)}, u32[]{:S(2)}, u32[]{:S(2)}) %collective-permute-start.13) | collective-permute-done | bytes 16416 | tf_op jit(solution)/shard_map/ppermute | solution.py:549
  30.1 1.0 %collective-permute-start.15 = (f32[32,128]{1,0:T(8,128)S(1)}, f32[32,128]{1,0:T(8,128)S(1)}, u32[]{:S(2)}, u32[]{:S(2)}) collective-permute-start(f32[32,128]{1,0:T(8,128)S(1)} %add.18), channel_id=1, source_target_pairs={{0,4},{1,5},{2,6},{3,7},{4,2},{5,3},{6,0},{7,1},{8,12},{9,13},{10,... | collective-permute-start | bytes 49160 | tf_op jit(solution)/shard_map/ppermute | solution.py:549
  31.1 1.2 %collective-permute-start.14 = (f32[32,128]{1,0:T(8,128)S(1)}, f32[32,128]{1,0:T(8,128)S(1)}, u32[]{:S(2)}, u32[]{:S(2)}) collective-permute-start(f32[32,128]{1,0:T(8,128)S(1)} %add.18), channel_id=1, source_target_pairs={{0,4},{4,0},{8,12},{12,8},{1,5},{5,1},{9,13},{13,9},{2,6},{6,2},{1... | collective-permute-start | bytes 49160 | tf_op jit(solution)/shard_map/ppermute | solution.py:444
  32.3 1.9 %collective-permute-done.15 = f32[32,128]{1,0:T(8,128)S(1)} collective-permute-done((f32[32,128]{1,0:T(8,128)S(1)}, f32[32,128]{1,0:T(8,128)S(1)}, u32[]{:S(2)}, u32[]{:S(2)}) %collective-permute-start.15) | collective-permute-done | bytes 16416 | tf_op jit(solution)/shard_map/ppermute | solution.py:549
  34.2 0.1 collective-permute-start.16
  34.3 1.2 %collective-permute-done.16.other_ref = f32[32,128]{1,0:T(8,128)S(1)} collective-permute-done((f32[32,128]{1,0:T(8,128)S(1)}, f32[32,128]{1,0:T(8,128)S(1)}, u32[]{:S(2)}, u32[]{:S(2)}) %collective-permute-start.16) | collective-permute-done | bytes 16416 | tf_op jit(solution)/shard_map/ppermute | solution.py:444
  35.5 2.6 %shard_map.34 = f32[1024,128]{1,0:T(8,128)} custom-call(f32[16,64,128]{2,1,0:T(8,128)S(1)} %get-tuple-element.35.whole_ref, f32[32,128]{1,0:T(8,128)S(1)} %add.19.gram_ref, f32[32,128]{1,0:T(8,128)S(1)} %collective-permute-done.16.other_ref), custom_call_target="tpu_custom_call" | custom-call | tf_op jit(solution)/shard_map/pallas_call | solution.py:427
  (14 shorter events, 0.1 us)
Async XLA Ops:
  1.5 6.8 %collective-permute-start.1 = (f32[5,8,128]{2,1,0:T(8,128)S(1)}, f32[5,8,128]{2,1,0:T(8,128)S(1)}, u32[]{:S(2)}, u32[]{:S(2)}) collective-permute-start(f32[5,8,128]{2,1,0:T(8,128)S(1)} %get-tuple-element.24), channel_id=1, source_target_pairs={{0,12},{4,8},{8,4},{12,0},{1,13},{5,9},{9,5},{13,1},{2,14},{6,10},... | collective-permute-start | bytes 61448 | tf_op jit(solution)/shard_map/ppermute | solution.py:494
  4.0 4.3 %collective-permute-start = (f32[5,8,128]{2,1,0:T(8,128)S(1)}, f32[5,8,128]{2,1,0:T(8,128)S(1)}, u32[]{:S(2)}, u32[]{:S(2)}) collective-permute-start(f32[5,8,128]{2,1,0:T(8,128)S(1)} %get-tuple-element.24), channel_id=1, source_target_pairs={{0,4},{4,0},{8,12},{12,8},{1,5},{5,1},{9,13},{13,9},{2,6},{6,2},{1... | collective-permute-start | bytes 61448 | tf_op jit(solution)/shard_map/ppermute | solution.py:444
  4.7 12.3 %collective-permute-start.6 = (f32[16,16,128]{2,1,0:T(8,128)S(1)}, f32[16,16,128]{2,1,0:T(8,128)S(1)}, u32[]{:S(2)}, u32[]{:S(2)}) collective-permute-start(f32[16,16,128]{2,1,0:T(8,128)S(1)} %get-tuple-element.34), channel_id=1, source_target_pairs={{0,3},{1,2},{2,1},{3,0},{4,7},{5,6},{6,5},{7,4},{8,11},{9,10},{10,... | collective-permute-start | bytes 393224 | tf_op jit(solution)/shard_map/ppermute | solution.py:444
  8.3 3.9 %collective-permute-start.2 = (f32[7,8,128]{2,1,0:T(8,128)S(1)}, f32[7,8,128]{2,1,0:T(8,128)S(1)}, u32[]{:S(2)}, u32[]{:S(2)}) collective-permute-start(f32[7,8,128]{2,1,0:T(8,128)S(1)} %get-tuple-element.29), channel_id=1, source_target_pairs={{0,16},{16,0},{1,17},{17,1},{2,18},{18,2},{3,19},{19,3},{4,20},{20... | collective-permute-start | bytes 86024 | tf_op jit(solution)/shard_map/ppermute | solution.py:504
  12.5 8.3 %collective-permute-start.3 = (f32[16,16,128]{2,1,0:T(8,128)S(1)}, f32[16,16,128]{2,1,0:T(8,128)S(1)}, u32[]{:S(2)}, u32[]{:S(2)}) collective-permute-start(f32[16,16,128]{2,1,0:T(8,128)S(1)} %get-tuple-element.30), channel_id=1, source_target_pairs={{0,2},{1,3},{2,0},{3,1},{4,6},{5,7},{6,4},{7,5},{8,10},{9,11},{10,... | collective-permute-start | bytes 393224 | tf_op jit(solution)/shard_map/ppermute | solution.py:444
  13.2 7.6 %collective-permute-start.4 = (f32[16,16,128]{2,1,0:T(8,128)S(1)}, f32[16,16,128]{2,1,0:T(8,128)S(1)}, u32[]{:S(2)}, u32[]{:S(2)}) collective-permute-start(f32[16,16,128]{2,1,0:T(8,128)S(1)} %get-tuple-element.31), channel_id=1, source_target_pairs={{0,1},{1,0},{2,3},{3,2},{4,5},{5,4},{6,7},{7,6},{8,9},{9,8},{10,11... | collective-permute-start | bytes 393224 | tf_op jit(solution)/shard_map/ppermute | solution.py:444
  14.8 5.9 %collective-permute-start.5 = (f32[5,8,128]{2,1,0:T(8,128)S(1)}, f32[5,8,128]{2,1,0:T(8,128)S(1)}, u32[]{:S(2)}, u32[]{:S(2)}) collective-permute-start(f32[5,8,128]{2,1,0:T(8,128)S(1)} %get-tuple-element.32), channel_id=1, source_target_pairs={{0,3},{1,2},{2,1},{3,0},{4,7},{5,6},{6,5},{7,4},{8,11},{9,10},{10,... | collective-permute-start | bytes 61448 | tf_op jit(solution)/shard_map/ppermute | solution.py:444
  21.5 1.2 %collective-permute-start.7 = (f32[32,128]{1,0:T(8,128)S(1)}, f32[32,128]{1,0:T(8,128)S(1)}, u32[]{:S(2)}, u32[]{:S(2)}) collective-permute-start(f32[32,128]{1,0:T(8,128)S(1)} %get-tuple-element.36), channel_id=1, source_target_pairs={{0,4},{4,0},{8,12},{12,8},{1,5},{5,1},{9,13},{13,9},{2,6},{6,2},{1... | collective-permute-start | bytes 49160 | tf_op jit(solution)/shard_map/ppermute | solution.py:444
  22.7 2.4 %collective-permute-start.9 = (f32[32,128]{1,0:T(8,128)S(1)}, f32[32,128]{1,0:T(8,128)S(1)}, u32[]{:S(2)}, u32[]{:S(2)}) collective-permute-start(f32[32,128]{1,0:T(8,128)S(1)} %add.15), channel_id=1, source_target_pairs={{0,12},{1,13},{2,14},{3,15},{4,0},{5,1},{6,2},{7,3},{8,4},{9,5},{1... | collective-permute-start | bytes 49160 | tf_op jit(solution)/shard_map/ppermute | solution.py:549
  23.7 1.4 %collective-permute-start.8 = (f32[32,128]{1,0:T(8,128)S(1)}, f32[32,128]{1,0:T(8,128)S(1)}, u32[]{:S(2)}, u32[]{:S(2)}) collective-permute-start(f32[32,128]{1,0:T(8,128)S(1)} %add.15), channel_id=1, source_target_pairs={{0,4},{4,0},{8,12},{12,8},{1,5},{5,1},{9,13},{13,9},{2,6},{6,2},{1... | collective-permute-start | bytes 49160 | tf_op jit(solution)/shard_map/ppermute | solution.py:444
  25.1 3.5 %collective-permute-start.11 = (f32[32,128]{1,0:T(8,128)S(1)}, f32[32,128]{1,0:T(8,128)S(1)}, u32[]{:S(2)}, u32[]{:S(2)}) collective-permute-start(f32[32,128]{1,0:T(8,128)S(1)} %add.16), channel_id=1, source_target_pairs={{0,4},{1,5},{2,6},{3,7},{4,16},{5,17},{6,18},{7,19},{8,12},{9,13},... | collective-permute-start | bytes 49160 | tf_op jit(solution)/shard_map/ppermute | solution.py:549
  26.1 2.5 %collective-permute-start.10 = (f32[32,128]{1,0:T(8,128)S(1)}, f32[32,128]{1,0:T(8,128)S(1)}, u32[]{:S(2)}, u32[]{:S(2)}) collective-permute-start(f32[32,128]{1,0:T(8,128)S(1)} %add.16), channel_id=1, source_target_pairs={{0,4},{4,0},{8,12},{12,8},{1,5},{5,1},{9,13},{13,9},{2,6},{6,2},{1... | collective-permute-start | bytes 49160 | tf_op jit(solution)/shard_map/ppermute | solution.py:444
  28.6 1.5 %collective-permute-start.13 = (f32[32,128]{1,0:T(8,128)S(1)}, f32[32,128]{1,0:T(8,128)S(1)}, u32[]{:S(2)}, u32[]{:S(2)}) collective-permute-start(f32[32,128]{1,0:T(8,128)S(1)} %add.17), channel_id=1, source_target_pairs={{0,5},{1,4},{2,7},{3,6},{4,0},{5,1},{6,2},{7,3},{8,13},{9,12},{10,... | collective-permute-start | bytes 49160 | tf_op jit(solution)/shard_map/ppermute | solution.py:549
  28.7 1.4 %collective-permute-start.12 = (f32[32,128]{1,0:T(8,128)S(1)}, f32[32,128]{1,0:T(8,128)S(1)}, u32[]{:S(2)}, u32[]{:S(2)}) collective-permute-start(f32[32,128]{1,0:T(8,128)S(1)} %add.17), channel_id=1, source_target_pairs={{0,4},{4,0},{8,12},{12,8},{1,5},{5,1},{9,13},{13,9},{2,6},{6,2},{1... | collective-permute-start | bytes 49160 | tf_op jit(solution)/shard_map/ppermute | solution.py:444
  30.1 4.1 %collective-permute-start.15 = (f32[32,128]{1,0:T(8,128)S(1)}, f32[32,128]{1,0:T(8,128)S(1)}, u32[]{:S(2)}, u32[]{:S(2)}) collective-permute-start(f32[32,128]{1,0:T(8,128)S(1)} %add.18), channel_id=1, source_target_pairs={{0,4},{1,5},{2,6},{3,7},{4,2},{5,3},{6,0},{7,1},{8,12},{9,13},{10,... | collective-permute-start | bytes 49160 | tf_op jit(solution)/shard_map/ppermute | solution.py:549
  31.1 3.1 %collective-permute-start.14 = (f32[32,128]{1,0:T(8,128)S(1)}, f32[32,128]{1,0:T(8,128)S(1)}, u32[]{:S(2)}, u32[]{:S(2)}) collective-permute-start(f32[32,128]{1,0:T(8,128)S(1)} %add.18), channel_id=1, source_target_pairs={{0,4},{4,0},{8,12},{12,8},{1,5},{5,1},{9,13},{13,9},{2,6},{6,2},{1... | collective-permute-start | bytes 49160 | tf_op jit(solution)/shard_map/ppermute | solution.py:444
  34.2 1.2 %collective-permute-start.16 = (f32[32,128]{1,0:T(8,128)S(1)}, f32[32,128]{1,0:T(8,128)S(1)}, u32[]{:S(2)}, u32[]{:S(2)}) collective-permute-start(f32[32,128]{1,0:T(8,128)S(1)} %add.19.gram_ref), channel_id=1, source_target_pairs={{0,4},{4,0},{8,12},{12,8},{1,5},{5,1},{9,13},{13,9},{2,6},{6,2},{1... | collective-permute-start | bytes 49160 | tf_op jit(solution)/shard_map/ppermute | solution.py:444

commit v9 on v8

--- a/solution.py
+++ b/solution.py
@@ -44,7 +44,18 @@
 
 
 def pack_kernel(
-    cols, rows, parts, early, start_hbm, levels_hbm, start_ref, levels_ref, edges_ref, outer_ref, *refs
+    cols,
+    rows,
+    parts,
+    early,
+    start_hbm,
+    levels_hbm,
+    whole_hbm,
+    start_ref,
+    levels_ref,
+    edges_ref,
+    outer_ref,
+    *refs,
 ):
     piece_refs, (arrived,) = refs[: len(early)], refs[len(early) :]
     chunks = cols // tile
@@ -58,6 +69,13 @@
         )
         for chunk in range(chunks)
     ]
+    for at, (k, piece_ref) in enumerate(zip(early, piece_refs)):
+        base = pl.multiple_of((lax.axis_index("col") ^ k) * part_rows, part_rows)
+        copies.append(
+            pltpu.make_async_copy(
+                whole_hbm.at[:, pl.ds(base, part_rows), :], piece_ref, arrived.at[chunks + 1 + at]
+            )
+        )
     for copy in copies:
         copy.start()
     copies[0].wait()
@@ -78,18 +96,8 @@
                 for row in range(part_rows)
             )
             edges_ref[group] = packed if chunk == 0 else edges_ref[group] + packed
-        for k, piece_ref in zip(early, piece_refs):
-            copy_piece(cols, rows, parts, k, start_ref, piece_ref, (chunk,))
-
-
-def copy_piece(cols, rows, parts, k, start_ref, piece_ref, which):
-    part_rows = rows // parts
-    base = (lax.axis_index("col") ^ k) * part_rows
-    for row in range(part_rows):
-        for chunk in which:
-            piece_ref[row, chunk * tile : (chunk + 1) * tile, :] = tile_at(
-                start_ref, rows, base + row, chunk
-            )
+    for copy in copies[1 + chunks :]:
+        copy.wait()
 
 
 def outer_kernel(parts, outer_ref, near_ref, far_ref, beside_ref, send_ref):
@@ -102,8 +110,8 @@
         )
     count = outer_ref.shape[0]
     send_ref[:count] = outer_ref[...]
-    send_ref[count] = beside_ref[0]
-    send_ref[count + 1] = beside_ref[parts - 1]
+    first_row = iota((tile, lanes), 1) < 4 * (count // 2)
+    send_ref[count] = jnp.where(first_row, beside_ref[0], beside_ref[parts - 1])
 
 
 inverse = 1.0 / half_width
@@ -193,7 +201,7 @@
             row, inside = 0, 1
             field_out = joined(before_ref[chunks + chunk] for chunk in range(chunks))
             edge_out = joined(
-                unpack_edges(before_ref[2 * chunks + 2], (part_rows - 1) * chunks + chunk)
+                unpack_edges(before_ref[2 * chunks + 1], (part_rows - 1) * chunks + chunk)
                 for chunk in range(chunks)
             )
             factor_out = factor(before_ref[2 * chunks, 1:2, :])
@@ -263,13 +271,14 @@
         out_ref[2 * chunks] = packed_ref[early.index(k)]
 
 
-def alone_kernel(cols, levels_ref, raw_ref, out_ref, once, factor):
-    part_rows = raw_ref.shape[0]
+def alone_kernel(cols, part_rows, levels_ref, raw_ref, out_ref, field, once, factor):
     factor[...] = site_factor(levels_ref[...].astype(jnp.float32))
     base = lax.axis_index("col") * part_rows
     for row in range(part_rows):
-        above, below = raw_ref[min(row + 1, part_rows - 1)], raw_ref[max(row - 1, 0)]
-        here = raw_ref[row]
+        field[row] = raw_ref[pl.ds(row, cols, stride=part_rows), :]
+    for row in range(part_rows):
+        above, below = field[min(row + 1, part_rows - 1)], field[max(row - 1, 0)]
+        here = field[row]
         once[row] = factor_at(factor, base + row, cols) * here - inverse * (
             sides(here, here) + upward(row, above, below)
         )
@@ -279,7 +288,7 @@
         twice = factor_at(factor, base + row, cols) * here - inverse * (
             sides(here, here) + upward(row, above, below)
         )
-        out_ref[row] = 2.0 * twice - raw_ref[row]
+        out_ref[row] = 2.0 * twice - field[row]
 
 
 def gram_kernel(cols, parts, early, order, *refs):
@@ -481,12 +490,14 @@
     piece = (part_rows, cols, lanes)
     start_here, levels_here, edges, outer, *raws = call(
         functools.partial(pack_kernel, *sizes, early),
-        [flat.shape, jax.ShapeDtypeStruct(levels.shape, levels.dtype), (parts + 1, tile, lanes), (2 * chunks + 1, tile, lanes)] + [piece] * len(early),
+        [flat.shape, jax.ShapeDtypeStruct(levels.shape, levels.dtype), (parts + 1, tile, lanes), (2 * chunks + 1, tile, lanes)]
+        + [(cols, part_rows, lanes)] * len(early),
         pltpu.with_memory_space_constraint(flat, pltpu.HBM),
         pltpu.with_memory_space_constraint(levels, pltpu.HBM),
-        scratch=[pltpu.SemaphoreType.DMA((chunks + 1,))],
+        pltpu.with_memory_space_constraint(start, pltpu.HBM),
+        scratch=[pltpu.SemaphoreType.DMA((chunks + 1 + len(early),))],
         limit=32,
-        in_specs=[pl.BlockSpec(memory_space=pl.ANY)] * 2,
+        in_specs=[pl.BlockSpec(memory_space=pl.ANY)] * 3,
     )
     count = lax.axis_size("ly")
     near = exchange(edges, "ly", 1)
@@ -495,7 +506,7 @@
     raws = [exchange(values, "col", k) for k, values in zip(early, raws)]
     beside, outer = call(
         functools.partial(outer_kernel, parts),
-        [(parts + 1, tile, lanes), (2 * chunks + 3, tile, lanes)],
+        [(parts + 1, tile, lanes), (2 * chunks + 2, tile, lanes)],
         outer,
         near,
         far,
@@ -527,11 +538,11 @@
     lates = [exchange(values, "col", k) if k else values for k, values in zip(order, lates)]
     alones = [
         call(
-            functools.partial(alone_kernel, cols),
+            functools.partial(alone_kernel, cols, part_rows),
             [piece],
             levels_here,
-            raw,
-            scratch=[piece, (rows, lanes)],
+            raw.reshape(cols * part_rows, lanes),
+            scratch=[piece, piece, (rows, lanes)],
             cost_estimate=pl.CostEstimate(flops=0, bytes_accessed=10**6, transcendentals=0),
         )[0]
         for raw in raws

time: 38.3 us -> 38.2 us (level)
  no operation moved by 1% of the time
where the time goes in v9:
time: 38.2 us; the launch traced here: 38 us
  starting transfers between devices  18.2 us (48%)
  waiting for transfers between devices  13.4 us (35%)
  Pallas kernels  6.33 us (17%)
    ppermute x11, starting transfers between devices, exchange(): return lax.ppermute(values, axis, [(i, i ^ distance) for i in range(count)])  11.2 us
    pallas_call x7, Pallas kernels, call(): pl.pallas_call(kernel, out_shape=[jax.ShapeDtypeStruct(shape, jnp.float32...  6.33 us
    ppermute x4, waiting for transfers between devices, shards(): gram = near + lax.ppermute(gram, axes, handover(holder, axis, bit))  6.16 us
    ppermute x11, waiting for transfers between devices, exchange(): return lax.ppermute(values, axis, [(i, i ^ distance) for i in range(count)])  6.08 us
    ppermute x4, starting transfers between devices, shards(): gram = near + lax.ppermute(gram, axes, handover(holder, axis, bit))  3 us
    ppermute x1, starting transfers between devices, shards(): far = lax.ppermute(edges, 'ly', far_pairs)  2.47 us
    ppermute x1, starting transfers between devices, shards(): lax.ppermute(outer, 'lx', [(i, (i + 1) % count) for i in range(count)])  1.56 us
    ppermute x1, waiting for transfers between devices, shards(): lax.ppermute(outer, 'lx', [(i, (i + 1) % count) for i in range(count)])  1.16 us
  transfers between devices with their start and end apart: 17, of which 9 were waited for; matrix products, arithmetic and copies ran while one was open for 0% of the time, Pallas kernels for 4%

profile of v9, /device:TPU:0, one launch (start us, length us, event | category | flops | bytes accessed | tf_op | source)
XLA Modules:
  0.0 38.0 jit_solution(4294078014315459139)
XLA Ops:
  0.0 1.4 %shard_map.28 = (f32[1024,128]{1,0:T(8,128)S(1)}, s32[64,128]{1,0:T(8,128)S(1)}, f32[5,8,128]{2,1,0:T(8,128)S(1)}, f32[5,8,128]{2,1,0:T(8,128)S(1)}, f32[16,16,128]{2,1,0:T(8,128)S(1)}) custom-call(f32[1024,128]{1,0:T(8,128)} %bitcast.4, s32[64,128]{1,0:T(8,128)} %levels_hbm.1, f32[16,64,128]{2,1,0:T(8,128)} %whole_hbm.1), custom_call_target="tpu_custom_call" | custom-call | tf_op jit(solution)/shard_map/pallas_call | solution.py:436
  1.4 2.5 %collective-permute-start.1 = (f32[5,8,128]{2,1,0:T(8,128)S(1)}, f32[5,8,128]{2,1,0:T(8,128)S(1)}, u32[]{:S(2)}, u32[]{:S(2)}) collective-permute-start(f32[5,8,128]{2,1,0:T(8,128)S(1)} %get-tuple-element.24), channel_id=1, source_target_pairs={{0,12},{4,8},{8,4},{12,0},{1,13},{5,9},{9,5},{13,1},{2,14},{6,10},... | collective-permute-start | bytes 61448 | tf_op jit(solution)/shard_map/ppermute | solution.py:505
  3.9 0.7 %collective-permute-start = (f32[5,8,128]{2,1,0:T(8,128)S(1)}, f32[5,8,128]{2,1,0:T(8,128)S(1)}, u32[]{:S(2)}, u32[]{:S(2)}) collective-permute-start(f32[5,8,128]{2,1,0:T(8,128)S(1)} %get-tuple-element.24), channel_id=1, source_target_pairs={{0,4},{4,0},{8,12},{12,8},{1,5},{5,1},{9,13},{13,9},{2,6},{6,2},{1... | collective-permute-start | bytes 61448 | tf_op jit(solution)/shard_map/ppermute | solution.py:453
  4.6 3.6 %collective-permute-start.6 = (f32[16,16,128]{2,1,0:T(8,128)S(1)}, f32[16,16,128]{2,1,0:T(8,128)S(1)}, u32[]{:S(2)}, u32[]{:S(2)}) collective-permute-start(f32[16,16,128]{2,1,0:T(8,128)S(1)} %get-tuple-element.34), channel_id=1, source_target_pairs={{0,3},{1,2},{2,1},{3,0},{4,7},{5,6},{6,5},{7,4},{8,11},{9,10},{10,... | collective-permute-start | bytes 393224 | tf_op jit(solution)/shard_map/ppermute | solution.py:453
  8.2 1.6 %collective-permute-start.2 = (f32[6,8,128]{2,1,0:T(8,128)S(1)}, f32[6,8,128]{2,1,0:T(8,128)S(1)}, u32[]{:S(2)}, u32[]{:S(2)}) collective-permute-start(f32[6,8,128]{2,1,0:T(8,128)S(1)} %get-tuple-element.29), channel_id=1, source_target_pairs={{0,16},{16,0},{1,17},{17,1},{2,18},{18,2},{3,19},{19,3},{4,20},{20... | collective-permute-start | bytes 73736 | tf_op jit(solution)/shard_map/ppermute | solution.py:515
  9.8 1.2 %shard_map.30 = (f32[64,16,128]{2,1,0:T(8,128)S(1)}, f32[2,16,128]{2,1,0:T(8,128)S(1)}, f32[1,8,128]{2,1,0:T(8,128)S(1)}) custom-call(f32[1024,128]{1,0:T(8,128)S(1)} %get-tuple-element.21.start_ref, s32[64,128]{1,0:T(8,128)S(1)} %get-tuple-element.22.levels_ref, f32[5,8,128]{2,1,0:T(8,128)S(1)} %get-tuple-element.25.beside_ref), custom_call_target="tpu_custom_call" | custom-call | flops 99999997952 | bytes 1000000000 | tf_op jit(solution)/shard_map/pallas_call | solution.py:436
  11.0 1.2 %collective-permute-done.2.before_ref.after_ref = f32[6,8,128]{2,1,0:T(8,128)S(1)} collective-permute-done((f32[6,8,128]{2,1,0:T(8,128)S(1)}, f32[6,8,128]{2,1,0:T(8,128)S(1)}, u32[]{:S(2)}, u32[]{:S(2)}) %collective-permute-start.2) | collective-permute-done | bytes 24608 | tf_op jit(solution)/shard_map/ppermute | solution.py:515
  12.1 0.2 shard_map.31
  12.4 0.8 %collective-permute-start.3 = (f32[16,16,128]{2,1,0:T(8,128)S(1)}, f32[16,16,128]{2,1,0:T(8,128)S(1)}, u32[]{:S(2)}, u32[]{:S(2)}) collective-permute-start(f32[16,16,128]{2,1,0:T(8,128)S(1)} %get-tuple-element.30), channel_id=1, source_target_pairs={{0,2},{1,3},{2,0},{3,1},{4,6},{5,7},{6,4},{7,5},{8,10},{9,11},{10,... | collective-permute-start | bytes 393224 | tf_op jit(solution)/shard_map/ppermute | solution.py:453
  13.1 1.6 %collective-permute-start.4 = (f32[16,16,128]{2,1,0:T(8,128)S(1)}, f32[16,16,128]{2,1,0:T(8,128)S(1)}, u32[]{:S(2)}, u32[]{:S(2)}) collective-permute-start(f32[16,16,128]{2,1,0:T(8,128)S(1)} %get-tuple-element.31), channel_id=1, source_target_pairs={{0,1},{1,0},{2,3},{3,2},{4,5},{5,4},{6,7},{7,6},{8,9},{9,8},{10,11... | collective-permute-start | bytes 393224 | tf_op jit(solution)/shard_map/ppermute | solution.py:453
  14.7 2.1 %collective-permute-start.5 = (f32[5,8,128]{2,1,0:T(8,128)S(1)}, f32[5,8,128]{2,1,0:T(8,128)S(1)}, u32[]{:S(2)}, u32[]{:S(2)}) collective-permute-start(f32[5,8,128]{2,1,0:T(8,128)S(1)} %get-tuple-element.32), channel_id=1, source_target_pairs={{0,3},{1,2},{2,1},{3,0},{4,7},{5,6},{6,5},{7,4},{8,11},{9,10},{10,... | collective-permute-start | bytes 61448 | tf_op jit(solution)/shard_map/ppermute | solution.py:453
  16.8 0.0 collective-permute-done.6
  16.8 0.2 shard_map.32.refs_4_
  17.0 3.6 %collective-permute-done.5.refs_2_ = f32[5,8,128]{2,1,0:T(8,128)S(1)} collective-permute-done((f32[5,8,128]{2,1,0:T(8,128)S(1)}, f32[5,8,128]{2,1,0:T(8,128)S(1)}, u32[]{:S(2)}, u32[]{:S(2)}) %collective-permute-start.5) | collective-permute-done | bytes 20512 | tf_op jit(solution)/shard_map/ppermute | solution.py:453
  20.6 0.1 collective-permute-done.4.refs_1_
  20.7 0.6 %shard_map.33 = (f32[16,64,128]{2,1,0:T(8,128)S(1)}, f32[32,128]{1,0:T(8,128)S(1)}) custom-call(f32[16,16,128]{2,1,0:T(8,128)S(1)} %collective-permute-done.3.refs_0_, f32[16,16,128]{2,1,0:T(8,128)S(1)} %collective-permute-done.4.refs_1_, f32[5,8,128]{2,1,0:T(8,128)S(1)} %collective-permute-done.5.refs_2_, f32[16,16,128]{2,1,0:T(8,128)S(1)} %get-tuple-element.33.refs_3_, ...), custom_call_target="tpu_custom_call" | custom-call | tf_op jit(solution)/shard_map/pallas_call | solution.py:436
  21.4 0.0 collective-permute-start.7
  21.4 1.2 %collective-permute-done.7 = f32[32,128]{1,0:T(8,128)S(1)} collective-permute-done((f32[32,128]{1,0:T(8,128)S(1)}, f32[32,128]{1,0:T(8,128)S(1)}, u32[]{:S(2)}, u32[]{:S(2)}) %collective-permute-start.7) | collective-permute-done | bytes 16416 | tf_op jit(solution)/shard_map/ppermute | solution.py:453
  22.6 1.0 %collective-permute-start.9 = (f32[32,128]{1,0:T(8,128)S(1)}, f32[32,128]{1,0:T(8,128)S(1)}, u32[]{:S(2)}, u32[]{:S(2)}) collective-permute-start(f32[32,128]{1,0:T(8,128)S(1)} %add.15), channel_id=1, source_target_pairs={{0,12},{1,13},{2,14},{3,15},{4,0},{5,1},{6,2},{7,3},{8,4},{9,5},{1... | collective-permute-start | bytes 49160 | tf_op jit(solution)/shard_map/ppermute | solution.py:560
  23.6 1.4 %collective-permute-done.9 = f32[32,128]{1,0:T(8,128)S(1)} collective-permute-done((f32[32,128]{1,0:T(8,128)S(1)}, f32[32,128]{1,0:T(8,128)S(1)}, u32[]{:S(2)}, u32[]{:S(2)}) %collective-permute-start.9) | collective-permute-done | bytes 16416 | tf_op jit(solution)/shard_map/ppermute | solution.py:560
  25.0 1.0 %collective-permute-start.11 = (f32[32,128]{1,0:T(8,128)S(1)}, f32[32,128]{1,0:T(8,128)S(1)}, u32[]{:S(2)}, u32[]{:S(2)}) collective-permute-start(f32[32,128]{1,0:T(8,128)S(1)} %add.16), channel_id=1, source_target_pairs={{0,4},{1,5},{2,6},{3,7},{4,16},{5,17},{6,18},{7,19},{8,12},{9,13},... | collective-permute-start | bytes 49160 | tf_op jit(solution)/shard_map/ppermute | solution.py:560
  26.0 0.6 %collective-permute-start.10 = (f32[32,128]{1,0:T(8,128)S(1)}, f32[32,128]{1,0:T(8,128)S(1)}, u32[]{:S(2)}, u32[]{:S(2)}) collective-permute-start(f32[32,128]{1,0:T(8,128)S(1)} %add.16), channel_id=1, source_target_pairs={{0,4},{4,0},{8,12},{12,8},{1,5},{5,1},{9,13},{13,9},{2,6},{6,2},{1... | collective-permute-start | bytes 49160 | tf_op jit(solution)/shard_map/ppermute | solution.py:453
  26.6 1.9 %collective-permute-done.11 = f32[32,128]{1,0:T(8,128)S(1)} collective-permute-done((f32[32,128]{1,0:T(8,128)S(1)}, f32[32,128]{1,0:T(8,128)S(1)}, u32[]{:S(2)}, u32[]{:S(2)}) %collective-permute-start.11) | collective-permute-done | bytes 16416 | tf_op jit(solution)/shard_map/ppermute | solution.py:560
  28.5 0.1 collective-permute-start.13
  28.6 0.5 %collective-permute-start.12 = (f32[32,128]{1,0:T(8,128)S(1)}, f32[32,128]{1,0:T(8,128)S(1)}, u32[]{:S(2)}, u32[]{:S(2)}) collective-permute-start(f32[32,128]{1,0:T(8,128)S(1)} %add.17), channel_id=1, source_target_pairs={{0,4},{4,0},{8,12},{12,8},{1,5},{5,1},{9,13},{13,9},{2,6},{6,2},{1... | collective-permute-start | bytes 49160 | tf_op jit(solution)/shard_map/ppermute | solution.py:453
  29.1 0.9 %collective-permute-done.13 = f32[32,128]{1,0:T(8,128)S(1)} collective-permute-done((f32[32,128]{1,0:T(8,128)S(1)}, f32[32,128]{1,0:T(8,128)S(1)}, u32[]{:S(2)}, u32[]{:S(2)}) %collective-permute-start.13) | collective-permute-done | bytes 16416 | tf_op jit(solution)/shard_map/ppermute | solution.py:560
  30.0 1.0 %collective-permute-start.15 = (f32[32,128]{1,0:T(8,128)S(1)}, f32[32,128]{1,0:T(8,128)S(1)}, u32[]{:S(2)}, u32[]{:S(2)}) collective-permute-start(f32[32,128]{1,0:T(8,128)S(1)} %add.18), channel_id=1, source_target_pairs={{0,4},{1,5},{2,6},{3,7},{4,2},{5,3},{6,0},{7,1},{8,12},{9,13},{10,... | collective-permute-start | bytes 49160 | tf_op jit(solution)/shard_map/ppermute | solution.py:560
  31.0 1.2 %collective-permute-start.14 = (f32[32,128]{1,0:T(8,128)S(1)}, f32[32,128]{1,0:T(8,128)S(1)}, u32[]{:S(2)}, u32[]{:S(2)}) collective-permute-start(f32[32,128]{1,0:T(8,128)S(1)} %add.18), channel_id=1, source_target_pairs={{0,4},{4,0},{8,12},{12,8},{1,5},{5,1},{9,13},{13,9},{2,6},{6,2},{1... | collective-permute-start | bytes 49160 | tf_op jit(solution)/shard_map/ppermute | solution.py:453
  32.2 1.9 %collective-permute-done.15 = f32[32,128]{1,0:T(8,128)S(1)} collective-permute-done((f32[32,128]{1,0:T(8,128)S(1)}, f32[32,128]{1,0:T(8,128)S(1)}, u32[]{:S(2)}, u32[]{:S(2)}) %collective-permute-start.15) | collective-permute-done | bytes 16416 | tf_op jit(solution)/shard_map/ppermute | solution.py:560
  34.1 0.1 collective-permute-start.16
  34.2 1.2 %collective-permute-done.16.other_ref = f32[32,128]{1,0:T(8,128)S(1)} collective-permute-done((f32[32,128]{1,0:T(8,128)S(1)}, f32[32,128]{1,0:T(8,128)S(1)}, u32[]{:S(2)}, u32[]{:S(2)}) %collective-permute-start.16) | collective-permute-done | bytes 16416 | tf_op jit(solution)/shard_map/ppermute | solution.py:453
  35.4 2.6 %shard_map.34 = f32[1024,128]{1,0:T(8,128)} custom-call(f32[16,64,128]{2,1,0:T(8,128)S(1)} %get-tuple-element.35.whole_ref, f32[32,128]{1,0:T(8,128)S(1)} %add.19.gram_ref, f32[32,128]{1,0:T(8,128)S(1)} %collective-permute-done.16.other_ref), custom_call_target="tpu_custom_call" | custom-call | tf_op jit(solution)/shard_map/pallas_call | solution.py:436
  (14 shorter events, 0.1 us)
Async XLA Ops:
  1.4 6.8 %collective-permute-start.1 = (f32[5,8,128]{2,1,0:T(8,128)S(1)}, f32[5,8,128]{2,1,0:T(8,128)S(1)}, u32[]{:S(2)}, u32[]{:S(2)}) collective-permute-start(f32[5,8,128]{2,1,0:T(8,128)S(1)} %get-tuple-element.24), channel_id=1, source_target_pairs={{0,12},{4,8},{8,4},{12,0},{1,13},{5,9},{9,5},{13,1},{2,14},{6,10},... | collective-permute-start | bytes 61448 | tf_op jit(solution)/shard_map/ppermute | solution.py:505
  3.9 4.3 %collective-permute-start = (f32[5,8,128]{2,1,0:T(8,128)S(1)}, f32[5,8,128]{2,1,0:T(8,128)S(1)}, u32[]{:S(2)}, u32[]{:S(2)}) collective-permute-start(f32[5,8,128]{2,1,0:T(8,128)S(1)} %get-tuple-element.24), channel_id=1, source_target_pairs={{0,4},{4,0},{8,12},{12,8},{1,5},{5,1},{9,13},{13,9},{2,6},{6,2},{1... | collective-permute-start | bytes 61448 | tf_op jit(solution)/shard_map/ppermute | solution.py:453
  4.6 12.2 %collective-permute-start.6 = (f32[16,16,128]{2,1,0:T(8,128)S(1)}, f32[16,16,128]{2,1,0:T(8,128)S(1)}, u32[]{:S(2)}, u32[]{:S(2)}) collective-permute-start(f32[16,16,128]{2,1,0:T(8,128)S(1)} %get-tuple-element.34), channel_id=1, source_target_pairs={{0,3},{1,2},{2,1},{3,0},{4,7},{5,6},{6,5},{7,4},{8,11},{9,10},{10,... | collective-permute-start | bytes 393224 | tf_op jit(solution)/shard_map/ppermute | solution.py:453
  8.2 3.9 %collective-permute-start.2 = (f32[6,8,128]{2,1,0:T(8,128)S(1)}, f32[6,8,128]{2,1,0:T(8,128)S(1)}, u32[]{:S(2)}, u32[]{:S(2)}) collective-permute-start(f32[6,8,128]{2,1,0:T(8,128)S(1)} %get-tuple-element.29), channel_id=1, source_target_pairs={{0,16},{16,0},{1,17},{17,1},{2,18},{18,2},{3,19},{19,3},{4,20},{20... | collective-permute-start | bytes 73736 | tf_op jit(solution)/shard_map/ppermute | solution.py:515
  12.4 8.3 %collective-permute-start.3 = (f32[16,16,128]{2,1,0:T(8,128)S(1)}, f32[16,16,128]{2,1,0:T(8,128)S(1)}, u32[]{:S(2)}, u32[]{:S(2)}) collective-permute-start(f32[16,16,128]{2,1,0:T(8,128)S(1)} %get-tuple-element.30), channel_id=1, source_target_pairs={{0,2},{1,3},{2,0},{3,1},{4,6},{5,7},{6,4},{7,5},{8,10},{9,11},{10,... | collective-permute-start | bytes 393224 | tf_op jit(solution)/shard_map/ppermute | solution.py:453
  13.1 7.6 %collective-permute-start.4 = (f32[16,16,128]{2,1,0:T(8,128)S(1)}, f32[16,16,128]{2,1,0:T(8,128)S(1)}, u32[]{:S(2)}, u32[]{:S(2)}) collective-permute-start(f32[16,16,128]{2,1,0:T(8,128)S(1)} %get-tuple-element.31), channel_id=1, source_target_pairs={{0,1},{1,0},{2,3},{3,2},{4,5},{5,4},{6,7},{7,6},{8,9},{9,8},{10,11... | collective-permute-start | bytes 393224 | tf_op jit(solution)/shard_map/ppermute | solution.py:453
  14.7 5.9 %collective-permute-start.5 = (f32[5,8,128]{2,1,0:T(8,128)S(1)}, f32[5,8,128]{2,1,0:T(8,128)S(1)}, u32[]{:S(2)}, u32[]{:S(2)}) collective-permute-start(f32[5,8,128]{2,1,0:T(8,128)S(1)} %get-tuple-element.32), channel_id=1, source_target_pairs={{0,3},{1,2},{2,1},{3,0},{4,7},{5,6},{6,5},{7,4},{8,11},{9,10},{10,... | collective-permute-start | bytes 61448 | tf_op jit(solution)/shard_map/ppermute | solution.py:453
  21.4 1.2 %collective-permute-start.7 = (f32[32,128]{1,0:T(8,128)S(1)}, f32[32,128]{1,0:T(8,128)S(1)}, u32[]{:S(2)}, u32[]{:S(2)}) collective-permute-start(f32[32,128]{1,0:T(8,128)S(1)} %get-tuple-element.36), channel_id=1, source_target_pairs={{0,4},{4,0},{8,12},{12,8},{1,5},{5,1},{9,13},{13,9},{2,6},{6,2},{1... | collective-permute-start | bytes 49160 | tf_op jit(solution)/shard_map/ppermute | solution.py:453
  22.6 2.4 %collective-permute-start.9 = (f32[32,128]{1,0:T(8,128)S(1)}, f32[32,128]{1,0:T(8,128)S(1)}, u32[]{:S(2)}, u32[]{:S(2)}) collective-permute-start(f32[32,128]{1,0:T(8,128)S(1)} %add.15), channel_id=1, source_target_pairs={{0,12},{1,13},{2,14},{3,15},{4,0},{5,1},{6,2},{7,3},{8,4},{9,5},{1... | collective-permute-start | bytes 49160 | tf_op jit(solution)/shard_map/ppermute | solution.py:560
  23.5 1.4 %collective-permute-start.8 = (f32[32,128]{1,0:T(8,128)S(1)}, f32[32,128]{1,0:T(8,128)S(1)}, u32[]{:S(2)}, u32[]{:S(2)}) collective-permute-start(f32[32,128]{1,0:T(8,128)S(1)} %add.15), channel_id=1, source_target_pairs={{0,4},{4,0},{8,12},{12,8},{1,5},{5,1},{9,13},{13,9},{2,6},{6,2},{1... | collective-permute-start | bytes 49160 | tf_op jit(solution)/shard_map/ppermute | solution.py:453
  25.0 3.5 %collective-permute-start.11 = (f32[32,128]{1,0:T(8,128)S(1)}, f32[32,128]{1,0:T(8,128)S(1)}, u32[]{:S(2)}, u32[]{:S(2)}) collective-permute-start(f32[32,128]{1,0:T(8,128)S(1)} %add.16), channel_id=1, source_target_pairs={{0,4},{1,5},{2,6},{3,7},{4,16},{5,17},{6,18},{7,19},{8,12},{9,13},... | collective-permute-start | bytes 49160 | tf_op jit(solution)/shard_map/ppermute | solution.py:560
  26.0 2.5 %collective-permute-start.10 = (f32[32,128]{1,0:T(8,128)S(1)}, f32[32,128]{1,0:T(8,128)S(1)}, u32[]{:S(2)}, u32[]{:S(2)}) collective-permute-start(f32[32,128]{1,0:T(8,128)S(1)} %add.16), channel_id=1, source_target_pairs={{0,4},{4,0},{8,12},{12,8},{1,5},{5,1},{9,13},{13,9},{2,6},{6,2},{1... | collective-permute-start | bytes 49160 | tf_op jit(solution)/shard_map/ppermute | solution.py:453
  28.5 1.5 %collective-permute-start.13 = (f32[32,128]{1,0:T(8,128)S(1)}, f32[32,128]{1,0:T(8,128)S(1)}, u32[]{:S(2)}, u32[]{:S(2)}) collective-permute-start(f32[32,128]{1,0:T(8,128)S(1)} %add.17), channel_id=1, source_target_pairs={{0,5},{1,4},{2,7},{3,6},{4,0},{5,1},{6,2},{7,3},{8,13},{9,12},{10,... | collective-permute-start | bytes 49160 | tf_op jit(solution)/shard_map/ppermute | solution.py:560
  28.6 1.4 %collective-permute-start.12 = (f32[32,128]{1,0:T(8,128)S(1)}, f32[32,128]{1,0:T(8,128)S(1)}, u32[]{:S(2)}, u32[]{:S(2)}) collective-permute-start(f32[32,128]{1,0:T(8,128)S(1)} %add.17), channel_id=1, source_target_pairs={{0,4},{4,0},{8,12},{12,8},{1,5},{5,1},{9,13},{13,9},{2,6},{6,2},{1... | collective-permute-start | bytes 49160 | tf_op jit(solution)/shard_map/ppermute | solution.py:453
  30.0 4.1 %collective-permute-start.15 = (f32[32,128]{1,0:T(8,128)S(1)}, f32[32,128]{1,0:T(8,128)S(1)}, u32[]{:S(2)}, u32[]{:S(2)}) collective-permute-start(f32[32,128]{1,0:T(8,128)S(1)} %add.18), channel_id=1, source_target_pairs={{0,4},{1,5},{2,6},{3,7},{4,2},{5,3},{6,0},{7,1},{8,12},{9,13},{10,... | collective-permute-start | bytes 49160 | tf_op jit(solution)/shard_map/ppermute | solution.py:560
  31.0 3.1 %collective-permute-start.14 = (f32[32,128]{1,0:T(8,128)S(1)}, f32[32,128]{1,0:T(8,128)S(1)}, u32[]{:S(2)}, u32[]{:S(2)}) collective-permute-start(f32[32,128]{1,0:T(8,128)S(1)} %add.18), channel_id=1, source_target_pairs={{0,4},{4,0},{8,12},{12,8},{1,5},{5,1},{9,13},{13,9},{2,6},{6,2},{1... | collective-permute-start | bytes 49160 | tf_op jit(solution)/shard_map/ppermute | solution.py:453
  34.1 1.2 %collective-permute-start.16 = (f32[32,128]{1,0:T(8,128)S(1)}, f32[32,128]{1,0:T(8,128)S(1)}, u32[]{:S(2)}, u32[]{:S(2)}) collective-permute-start(f32[32,128]{1,0:T(8,128)S(1)} %add.19.gram_ref), channel_id=1, source_target_pairs={{0,4},{4,0},{8,12},{12,8},{1,5},{5,1},{9,13},{13,9},{2,6},{6,2},{1... | collective-permute-start | bytes 49160 | tf_op jit(solution)/shard_map/ppermute | solution.py:453

commit v10 on v9

--- a/solution.py
+++ b/solution.py
@@ -341,6 +341,14 @@
     return high, middle, low
 
 
+def split_kernel(whole_ref, main_ref, rest_ref):
+    for pair in range(whole_ref.shape[0] // 2):
+        values = jnp.concatenate([whole_ref[2 * pair], whole_ref[2 * pair + 1]], axis=1)
+        high, middle, low = split(values)
+        main_ref[pair] = jnp.concatenate([high, middle], axis=0)
+        rest_ref[pair] = jnp.concatenate([low, high], axis=0)
+
+
 def eliminate(work, b, columns_ref, rows_ref):
     shape = (tile, lanes)
     sub = iota(shape, 0)
@@ -359,13 +367,22 @@
     factor = {(p, q): spread(columns_ref, slot, q, p) for p in range(tile) for q in range(p + 1)}
     pivots = [spread(rows_ref, slot, m) for m in range(tile)]
     roots = []
-    for m in range(tile):
-        roots.append(lax.rsqrt(factor[m, m]))
-        for p in range(m + 1, tile):
+    for m in range(0, tile, 2):
+        n = m + 1
+        first, cross = factor[m, m], factor[n, m]
+        roots.append(lax.rsqrt(first))
+        both = lax.rsqrt(first * factor[n, n] - cross * cross)
+        roots.append(both * (first * roots[m]))
+        both = both * roots[m]
+        factor[n, m] = cross * roots[m]
+        for p in range(n + 1, tile):
+            factor[p, n] = (factor[p, n] * first - factor[p, m] * cross) * both
             factor[p, m] = factor[p, m] * roots[m]
-        for p in range(m + 1, tile):
-            for q in range(m + 1, p + 1):
-                factor[p, q] = factor[p, q] - factor[p, m] * factor[q, m]
+        for p in range(n + 1, tile):
+            for q in range(n + 1, p + 1):
+                factor[p, q] = (
+                    factor[p, q] - factor[p, m] * factor[q, m] - factor[p, n] * factor[q, n]
+                )
     for m in range(tile):
         for p in range(m):
             pivots[m] = pivots[m] - factor[m, p] * pivots[p]
@@ -382,9 +399,9 @@
 
 
 def solve_kernel(
-    scale, holder, whole_ref, gram_ref, other_ref, out_hbm, out_ref, columns_ref, rows_ref, copied
+    scale, holder, main_ref, rest_ref, gram_ref, other_ref, out_hbm, out_ref, columns_ref, rows_ref, copied
 ):
-    part_rows, total, _ = whole_ref.shape
+    part_rows, total = 2 * main_ref.shape[0], main_ref.shape[1] // 2
     blocks = total // tile
     half = total // 2
     holds = lax.axis_index("ly") % 2 == holder
@@ -392,13 +409,20 @@
     lane = iota((tile, lanes), 1)
     sub = iota((tile, lanes), 0)
     work = []
+    diagonal = []
     for i in range(blocks):
         at = i * tile % half
         block = packed[at : at + tile, :]
         if i * tile >= half:
             block = pltpu.roll(block, total, 1)
-        unit = jnp.where(lane - total == sub + i * tile, 1.0, 0.0)
-        work.append(jnp.where(lane < total, block, unit))
+        work.append(block)
+        diagonal.append(jnp.where(lane == sub + i * tile, block, 0.0))
+    across = jnp.sum(sum(diagonal), axis=0, keepdims=True)
+    across = lax.rsqrt(jnp.where(lane[:1] < total, across, 1.0))
+    for i in range(blocks):
+        down = lax.rsqrt(jnp.sum(diagonal[i], axis=1, keepdims=True))
+        unit = jnp.where(lane - total == sub + i * tile, down, 0.0)
+        work[i] = jnp.where(lane < total, work[i] * down * across, unit)
     copies = []
     cuts = (0, 3 * blocks // 4, blocks)
     for part, (first, last) in enumerate(zip(cuts, cuts[1:])):
@@ -416,10 +440,8 @@
         height = (last - first) * tile
         base = first * tile * part_rows
         for row in range(0, part_rows, 2):
-            values = jnp.concatenate([whole_ref[row], whole_ref[row + 1]], axis=1)
-            f_high, f_middle, f_low = split(values)
-            right_main = jnp.concatenate([f_high, f_middle, f_high, f_middle], axis=0)
-            right_rest = jnp.concatenate([f_low, f_high], axis=0)
+            right_main = jnp.concatenate([main_ref[row // 2], main_ref[row // 2]], axis=0)
+            right_rest = rest_ref[row // 2]
             result = jnp.dot(left_rest, right_rest, preferred_element_type=jnp.float32) + jnp.dot(
                 left_main, right_main, preferred_element_type=jnp.float32
             )
@@ -560,10 +582,12 @@
         gram = near + lax.ppermute(gram, axes, handover(holder, axis, bit))
         holder = 1 - holder
     scale = math.sqrt(rows * lax.axis_size("lx") * lanes * lax.axis_size("ly"))
+    halves = jax.ShapeDtypeStruct((part_rows // 2, 2 * total, 2 * lanes), jnp.bfloat16)
+    split_whole = call(split_kernel, [halves, halves], whole)
     (basis,) = call(
         functools.partial(solve_kernel, scale, holder),
         [(total * part_rows, lanes)],
-        whole,
+        *split_whole,
         gram,
         exchange(gram, "ly", 1),
         scratch=[

time: 38.2 us -> 38 us (level)
    pallas_call x7 -> x8, Pallas kernels: 6.33 us -> 6.33 us  [call(): pl.pallas_call(kernel, out_shape=[jax.ShapeDtypeStruct(shape, jnp.float32...]
  transfers between devices with their start and end apart: 17 -> 17, of which waited for: 9 -> 9; matrix products, arithmetic and copies ran while one was open for 0% -> 0% of each run, Pallas kernels for 4% -> 5%
where the time goes in v10:
time: 38 us; the launch traced here: 37.9 us
  starting transfers between devices  18.2 us (48%)
  waiting for transfers between devices  13.3 us (35%)
  Pallas kernels  6.33 us (17%)
    ppermute x11, starting transfers between devices, exchange(): return lax.ppermute(values, axis, [(i, i ^ distance) for i in range(count)])  11.2 us
    pallas_call x8, Pallas kernels, call(): pl.pallas_call(kernel, out_shape=[jax.ShapeDtypeStruct(shape, jnp.float32...  6.33 us
    ppermute x4, waiting for transfers between devices, shards(): gram = near + lax.ppermute(gram, axes, handover(holder, axis, bit))  6.16 us
    ppermute x11, waiting for transfers between devices, exchange(): return lax.ppermute(values, axis, [(i, i ^ distance) for i in range(count)])  5.95 us
    ppermute x4, starting transfers between devices, shards(): gram = near + lax.ppermute(gram, axes, handover(holder, axis, bit))  3 us
    ppermute x1, starting transfers between devices, shards(): far = lax.ppermute(edges, 'ly', far_pairs)  2.47 us
    ppermute x1, starting transfers between devices, shards(): lax.ppermute(outer, 'lx', [(i, (i + 1) % count) for i in range(count)])  1.56 us
    ppermute x1, waiting for transfers between devices, shards(): lax.ppermute(outer, 'lx', [(i, (i + 1) % count) for i in range(count)])  1.16 us
  transfers between devices with their start and end apart: 17, of which 9 were waited for; matrix products, arithmetic and copies ran while one was open for 0% of the time, Pallas kernels for 5%

profile of v10, /device:TPU:0, one launch (start us, length us, event | category | flops | bytes accessed | tf_op | source)
XLA Modules:
  0.0 37.9 jit_solution(16821911970030839264)
XLA Ops:
  0.0 1.4 %shard_map.28 = (f32[1024,128]{1,0:T(8,128)S(1)}, s32[64,128]{1,0:T(8,128)S(1)}, f32[5,8,128]{2,1,0:T(8,128)S(1)}, f32[5,8,128]{2,1,0:T(8,128)S(1)}, f32[16,16,128]{2,1,0:T(8,128)S(1)}) custom-call(f32[1024,128]{1,0:T(8,128)} %bitcast.4, s32[64,128]{1,0:T(8,128)} %levels_hbm.1, f32[16,64,128]{2,1,0:T(8,128)} %whole_hbm.1), custom_call_target="tpu_custom_call" | custom-call | tf_op jit(solution)/shard_map/pallas_call | solution.py:458
  1.4 2.5 %collective-permute-start.1 = (f32[5,8,128]{2,1,0:T(8,128)S(1)}, f32[5,8,128]{2,1,0:T(8,128)S(1)}, u32[]{:S(2)}, u32[]{:S(2)}) collective-permute-start(f32[5,8,128]{2,1,0:T(8,128)S(1)} %get-tuple-element.26), channel_id=1, source_target_pairs={{0,12},{4,8},{8,4},{12,0},{1,13},{5,9},{9,5},{13,1},{2,14},{6,10},... | collective-permute-start | bytes 61448 | tf_op jit(solution)/shard_map/ppermute | solution.py:527
  3.9 0.7 %collective-permute-start = (f32[5,8,128]{2,1,0:T(8,128)S(1)}, f32[5,8,128]{2,1,0:T(8,128)S(1)}, u32[]{:S(2)}, u32[]{:S(2)}) collective-permute-start(f32[5,8,128]{2,1,0:T(8,128)S(1)} %get-tuple-element.26), channel_id=1, source_target_pairs={{0,4},{4,0},{8,12},{12,8},{1,5},{5,1},{9,13},{13,9},{2,6},{6,2},{1... | collective-permute-start | bytes 61448 | tf_op jit(solution)/shard_map/ppermute | solution.py:475
  4.6 3.6 %collective-permute-start.6 = (f32[16,16,128]{2,1,0:T(8,128)S(1)}, f32[16,16,128]{2,1,0:T(8,128)S(1)}, u32[]{:S(2)}, u32[]{:S(2)}) collective-permute-start(f32[16,16,128]{2,1,0:T(8,128)S(1)} %get-tuple-element.36), channel_id=1, source_target_pairs={{0,3},{1,2},{2,1},{3,0},{4,7},{5,6},{6,5},{7,4},{8,11},{9,10},{10,... | collective-permute-start | bytes 393224 | tf_op jit(solution)/shard_map/ppermute | solution.py:475
  8.2 1.6 %collective-permute-start.2 = (f32[6,8,128]{2,1,0:T(8,128)S(1)}, f32[6,8,128]{2,1,0:T(8,128)S(1)}, u32[]{:S(2)}, u32[]{:S(2)}) collective-permute-start(f32[6,8,128]{2,1,0:T(8,128)S(1)} %get-tuple-element.31), channel_id=1, source_target_pairs={{0,16},{16,0},{1,17},{17,1},{2,18},{18,2},{3,19},{19,3},{4,20},{20... | collective-permute-start | bytes 73736 | tf_op jit(solution)/shard_map/ppermute | solution.py:537
  9.8 1.2 %shard_map.30 = (f32[64,16,128]{2,1,0:T(8,128)S(1)}, f32[2,16,128]{2,1,0:T(8,128)S(1)}, f32[1,8,128]{2,1,0:T(8,128)S(1)}) custom-call(f32[1024,128]{1,0:T(8,128)S(1)} %get-tuple-element.23.start_ref, s32[64,128]{1,0:T(8,128)S(1)} %get-tuple-element.24.levels_ref, f32[5,8,128]{2,1,0:T(8,128)S(1)} %get-tuple-element.27.beside_ref), custom_call_target="tpu_custom_call" | custom-call | flops 99999997952 | bytes 1000000000 | tf_op jit(solution)/shard_map/pallas_call | solution.py:458
  11.0 1.2 %collective-permute-done.2.before_ref.after_ref = f32[6,8,128]{2,1,0:T(8,128)S(1)} collective-permute-done((f32[6,8,128]{2,1,0:T(8,128)S(1)}, f32[6,8,128]{2,1,0:T(8,128)S(1)}, u32[]{:S(2)}, u32[]{:S(2)}) %collective-permute-start.2) | collective-permute-done | bytes 24608 | tf_op jit(solution)/shard_map/ppermute | solution.py:537
  12.1 0.2 shard_map.31
  12.4 0.8 %collective-permute-start.3 = (f32[16,16,128]{2,1,0:T(8,128)S(1)}, f32[16,16,128]{2,1,0:T(8,128)S(1)}, u32[]{:S(2)}, u32[]{:S(2)}) collective-permute-start(f32[16,16,128]{2,1,0:T(8,128)S(1)} %get-tuple-element.32), channel_id=1, source_target_pairs={{0,2},{1,3},{2,0},{3,1},{4,6},{5,7},{6,4},{7,5},{8,10},{9,11},{10,... | collective-permute-start | bytes 393224 | tf_op jit(solution)/shard_map/ppermute | solution.py:475
  13.1 1.6 %collective-permute-start.4 = (f32[16,16,128]{2,1,0:T(8,128)S(1)}, f32[16,16,128]{2,1,0:T(8,128)S(1)}, u32[]{:S(2)}, u32[]{:S(2)}) collective-permute-start(f32[16,16,128]{2,1,0:T(8,128)S(1)} %get-tuple-element.33), channel_id=1, source_target_pairs={{0,1},{1,0},{2,3},{3,2},{4,5},{5,4},{6,7},{7,6},{8,9},{9,8},{10,11... | collective-permute-start | bytes 393224 | tf_op jit(solution)/shard_map/ppermute | solution.py:475
  14.7 2.1 %collective-permute-start.5 = (f32[5,8,128]{2,1,0:T(8,128)S(1)}, f32[5,8,128]{2,1,0:T(8,128)S(1)}, u32[]{:S(2)}, u32[]{:S(2)}) collective-permute-start(f32[5,8,128]{2,1,0:T(8,128)S(1)} %get-tuple-element.34), channel_id=1, source_target_pairs={{0,3},{1,2},{2,1},{3,0},{4,7},{5,6},{6,5},{7,4},{8,11},{9,10},{10,... | collective-permute-start | bytes 61448 | tf_op jit(solution)/shard_map/ppermute | solution.py:475
  16.8 0.2 shard_map.32.refs_4_
  17.0 3.6 %collective-permute-done.5.refs_2_ = f32[5,8,128]{2,1,0:T(8,128)S(1)} collective-permute-done((f32[5,8,128]{2,1,0:T(8,128)S(1)}, f32[5,8,128]{2,1,0:T(8,128)S(1)}, u32[]{:S(2)}, u32[]{:S(2)}) %collective-permute-start.5) | collective-permute-done | bytes 20512 | tf_op jit(solution)/shard_map/ppermute | solution.py:475
  20.6 0.1 collective-permute-done.4.refs_1_
  20.7 0.6 %shard_map.33 = (f32[16,64,128]{2,1,0:T(8,128)S(1)}, f32[32,128]{1,0:T(8,128)S(1)}) custom-call(f32[16,16,128]{2,1,0:T(8,128)S(1)} %collective-permute-done.3.refs_0_, f32[16,16,128]{2,1,0:T(8,128)S(1)} %collective-permute-done.4.refs_1_, f32[5,8,128]{2,1,0:T(8,128)S(1)} %collective-permute-done.5.refs_2_, f32[16,16,128]{2,1,0:T(8,128)S(1)} %get-tuple-element.35.refs_3_, ...), custom_call_target="tpu_custom_call" | custom-call | tf_op jit(solution)/shard_map/pallas_call | solution.py:458
  21.4 0.0 collective-permute-start.7
  21.4 1.2 %collective-permute-done.7 = f32[32,128]{1,0:T(8,128)S(1)} collective-permute-done((f32[32,128]{1,0:T(8,128)S(1)}, f32[32,128]{1,0:T(8,128)S(1)}, u32[]{:S(2)}, u32[]{:S(2)}) %collective-permute-start.7) | collective-permute-done | bytes 16416 | tf_op jit(solution)/shard_map/ppermute | solution.py:475
  22.6 1.0 %collective-permute-start.9 = (f32[32,128]{1,0:T(8,128)S(1)}, f32[32,128]{1,0:T(8,128)S(1)}, u32[]{:S(2)}, u32[]{:S(2)}) collective-permute-start(f32[32,128]{1,0:T(8,128)S(1)} %add.15), channel_id=1, source_target_pairs={{0,12},{1,13},{2,14},{3,15},{4,0},{5,1},{6,2},{7,3},{8,4},{9,5},{1... | collective-permute-start | bytes 49160 | tf_op jit(solution)/shard_map/ppermute | solution.py:582
  23.6 1.4 %collective-permute-done.9 = f32[32,128]{1,0:T(8,128)S(1)} collective-permute-done((f32[32,128]{1,0:T(8,128)S(1)}, f32[32,128]{1,0:T(8,128)S(1)}, u32[]{:S(2)}, u32[]{:S(2)}) %collective-permute-start.9) | collective-permute-done | bytes 16416 | tf_op jit(solution)/shard_map/ppermute | solution.py:582
  25.0 1.0 %collective-permute-start.11 = (f32[32,128]{1,0:T(8,128)S(1)}, f32[32,128]{1,0:T(8,128)S(1)}, u32[]{:S(2)}, u32[]{:S(2)}) collective-permute-start(f32[32,128]{1,0:T(8,128)S(1)} %add.16), channel_id=1, source_target_pairs={{0,4},{1,5},{2,6},{3,7},{4,16},{5,17},{6,18},{7,19},{8,12},{9,13},... | collective-permute-start | bytes 49160 | tf_op jit(solution)/shard_map/ppermute | solution.py:582
  26.0 0.6 %collective-permute-start.10 = (f32[32,128]{1,0:T(8,128)S(1)}, f32[32,128]{1,0:T(8,128)S(1)}, u32[]{:S(2)}, u32[]{:S(2)}) collective-permute-start(f32[32,128]{1,0:T(8,128)S(1)} %add.16), channel_id=1, source_target_pairs={{0,4},{4,0},{8,12},{12,8},{1,5},{5,1},{9,13},{13,9},{2,6},{6,2},{1... | collective-permute-start | bytes 49160 | tf_op jit(solution)/shard_map/ppermute | solution.py:475
  26.6 1.9 %collective-permute-done.11 = f32[32,128]{1,0:T(8,128)S(1)} collective-permute-done((f32[32,128]{1,0:T(8,128)S(1)}, f32[32,128]{1,0:T(8,128)S(1)}, u32[]{:S(2)}, u32[]{:S(2)}) %collective-permute-start.11) | collective-permute-done | bytes 16416 | tf_op jit(solution)/shard_map/ppermute | solution.py:582
  28.5 0.1 collective-permute-start.13
  28.6 0.5 %collective-permute-start.12 = (f32[32,128]{1,0:T(8,128)S(1)}, f32[32,128]{1,0:T(8,128)S(1)}, u32[]{:S(2)}, u32[]{:S(2)}) collective-permute-start(f32[32,128]{1,0:T(8,128)S(1)} %add.17), channel_id=1, source_target_pairs={{0,4},{4,0},{8,12},{12,8},{1,5},{5,1},{9,13},{13,9},{2,6},{6,2},{1... | collective-permute-start | bytes 49160 | tf_op jit(solution)/shard_map/ppermute | solution.py:475
  29.1 0.9 %collective-permute-done.13 = f32[32,128]{1,0:T(8,128)S(1)} collective-permute-done((f32[32,128]{1,0:T(8,128)S(1)}, f32[32,128]{1,0:T(8,128)S(1)}, u32[]{:S(2)}, u32[]{:S(2)}) %collective-permute-start.13) | collective-permute-done | bytes 16416 | tf_op jit(solution)/shard_map/ppermute | solution.py:582
  30.0 1.0 %collective-permute-start.15 = (f32[32,128]{1,0:T(8,128)S(1)}, f32[32,128]{1,0:T(8,128)S(1)}, u32[]{:S(2)}, u32[]{:S(2)}) collective-permute-start(f32[32,128]{1,0:T(8,128)S(1)} %add.18), channel_id=1, source_target_pairs={{0,4},{1,5},{2,6},{3,7},{4,2},{5,3},{6,0},{7,1},{8,12},{9,13},{10,... | collective-permute-start | bytes 49160 | tf_op jit(solution)/shard_map/ppermute | solution.py:582
  31.0 1.2 %collective-permute-start.14 = (f32[32,128]{1,0:T(8,128)S(1)}, f32[32,128]{1,0:T(8,128)S(1)}, u32[]{:S(2)}, u32[]{:S(2)}) collective-permute-start(f32[32,128]{1,0:T(8,128)S(1)} %add.18), channel_id=1, source_target_pairs={{0,4},{4,0},{8,12},{12,8},{1,5},{5,1},{9,13},{13,9},{2,6},{6,2},{1... | collective-permute-start | bytes 49160 | tf_op jit(solution)/shard_map/ppermute | solution.py:475
  32.2 1.9 %collective-permute-done.15 = f32[32,128]{1,0:T(8,128)S(1)} collective-permute-done((f32[32,128]{1,0:T(8,128)S(1)}, f32[32,128]{1,0:T(8,128)S(1)}, u32[]{:S(2)}, u32[]{:S(2)}) %collective-permute-start.15) | collective-permute-done | bytes 16416 | tf_op jit(solution)/shard_map/ppermute | solution.py:582
  34.1 0.1 collective-permute-start.16
  34.2 0.1 shard_map.34
  34.3 1.0 %collective-permute-done.16.other_ref = f32[32,128]{1,0:T(8,128)S(1)} collective-permute-done((f32[32,128]{1,0:T(8,128)S(1)}, f32[32,128]{1,0:T(8,128)S(1)}, u32[]{:S(2)}, u32[]{:S(2)}) %collective-permute-start.16) | collective-permute-done | bytes 16416 | tf_op jit(solution)/shard_map/ppermute | solution.py:475
  35.4 2.5 %shard_map.35 = f32[1024,128]{1,0:T(8,128)} custom-call(bf16[8,128,256]{2,1,0:T(8,128)(2,1)S(1)} %get-tuple-element.38.main_ref, bf16[8,128,256]{2,1,0:T(8,128)(2,1)S(1)} %get-tuple-element.39.rest_ref, f32[32,128]{1,0:T(8,128)S(1)} %add.19.gram_ref, f32[32,128]{1,0:T(8,128)S(1)} %collective-permute-done.16.other_ref), custom_call_target="tpu_custom_call" | custom-call | tf_op jit(solution)/shard_map/pallas_call | solution.py:458
  (15 shorter events, 0.1 us)
Async XLA Ops:
  1.4 6.8 %collective-permute-start.1 = (f32[5,8,128]{2,1,0:T(8,128)S(1)}, f32[5,8,128]{2,1,0:T(8,128)S(1)}, u32[]{:S(2)}, u32[]{:S(2)}) collective-permute-start(f32[5,8,128]{2,1,0:T(8,128)S(1)} %get-tuple-element.26), channel_id=1, source_target_pairs={{0,12},{4,8},{8,4},{12,0},{1,13},{5,9},{9,5},{13,1},{2,14},{6,10},... | collective-permute-start | bytes 61448 | tf_op jit(solution)/shard_map/ppermute | solution.py:527
  3.9 4.3 %collective-permute-start = (f32[5,8,128]{2,1,0:T(8,128)S(1)}, f32[5,8,128]{2,1,0:T(8,128)S(1)}, u32[]{:S(2)}, u32[]{:S(2)}) collective-permute-start(f32[5,8,128]{2,1,0:T(8,128)S(1)} %get-tuple-element.26), channel_id=1, source_target_pairs={{0,4},{4,0},{8,12},{12,8},{1,5},{5,1},{9,13},{13,9},{2,6},{6,2},{1... | collective-permute-start | bytes 61448 | tf_op jit(solution)/shard_map/ppermute | solution.py:475
  4.6 12.2 %collective-permute-start.6 = (f32[16,16,128]{2,1,0:T(8,128)S(1)}, f32[16,16,128]{2,1,0:T(8,128)S(1)}, u32[]{:S(2)}, u32[]{:S(2)}) collective-permute-start(f32[16,16,128]{2,1,0:T(8,128)S(1)} %get-tuple-element.36), channel_id=1, source_target_pairs={{0,3},{1,2},{2,1},{3,0},{4,7},{5,6},{6,5},{7,4},{8,11},{9,10},{10,... | collective-permute-start | bytes 393224 | tf_op jit(solution)/shard_map/ppermute | solution.py:475
  8.2 3.9 %collective-permute-start.2 = (f32[6,8,128]{2,1,0:T(8,128)S(1)}, f32[6,8,128]{2,1,0:T(8,128)S(1)}, u32[]{:S(2)}, u32[]{:S(2)}) collective-permute-start(f32[6,8,128]{2,1,0:T(8,128)S(1)} %get-tuple-element.31), channel_id=1, source_target_pairs={{0,16},{16,0},{1,17},{17,1},{2,18},{18,2},{3,19},{19,3},{4,20},{20... | collective-permute-start | bytes 73736 | tf_op jit(solution)/shard_map/ppermute | solution.py:537
  12.4 8.3 %collective-permute-start.3 = (f32[16,16,128]{2,1,0:T(8,128)S(1)}, f32[16,16,128]{2,1,0:T(8,128)S(1)}, u32[]{:S(2)}, u32[]{:S(2)}) collective-permute-start(f32[16,16,128]{2,1,0:T(8,128)S(1)} %get-tuple-element.32), channel_id=1, source_target_pairs={{0,2},{1,3},{2,0},{3,1},{4,6},{5,7},{6,4},{7,5},{8,10},{9,11},{10,... | collective-permute-start | bytes 393224 | tf_op jit(solution)/shard_map/ppermute | solution.py:475
  13.1 7.6 %collective-permute-start.4 = (f32[16,16,128]{2,1,0:T(8,128)S(1)}, f32[16,16,128]{2,1,0:T(8,128)S(1)}, u32[]{:S(2)}, u32[]{:S(2)}) collective-permute-start(f32[16,16,128]{2,1,0:T(8,128)S(1)} %get-tuple-element.33), channel_id=1, source_target_pairs={{0,1},{1,0},{2,3},{3,2},{4,5},{5,4},{6,7},{7,6},{8,9},{9,8},{10,11... | collective-permute-start | bytes 393224 | tf_op jit(solution)/shard_map/ppermute | solution.py:475
  14.7 5.9 %collective-permute-start.5 = (f32[5,8,128]{2,1,0:T(8,128)S(1)}, f32[5,8,128]{2,1,0:T(8,128)S(1)}, u32[]{:S(2)}, u32[]{:S(2)}) collective-permute-start(f32[5,8,128]{2,1,0:T(8,128)S(1)} %get-tuple-element.34), channel_id=1, source_target_pairs={{0,3},{1,2},{2,1},{3,0},{4,7},{5,6},{6,5},{7,4},{8,11},{9,10},{10,... | collective-permute-start | bytes 61448 | tf_op jit(solution)/shard_map/ppermute | solution.py:475
  21.4 1.2 %collective-permute-start.7 = (f32[32,128]{1,0:T(8,128)S(1)}, f32[32,128]{1,0:T(8,128)S(1)}, u32[]{:S(2)}, u32[]{:S(2)}) collective-permute-start(f32[32,128]{1,0:T(8,128)S(1)} %get-tuple-element.40), channel_id=1, source_target_pairs={{0,4},{4,0},{8,12},{12,8},{1,5},{5,1},{9,13},{13,9},{2,6},{6,2},{1... | collective-permute-start | bytes 49160 | tf_op jit(solution)/shard_map/ppermute | solution.py:475
  22.6 2.4 %collective-permute-start.9 = (f32[32,128]{1,0:T(8,128)S(1)}, f32[32,128]{1,0:T(8,128)S(1)}, u32[]{:S(2)}, u32[]{:S(2)}) collective-permute-start(f32[32,128]{1,0:T(8,128)S(1)} %add.15), channel_id=1, source_target_pairs={{0,12},{1,13},{2,14},{3,15},{4,0},{5,1},{6,2},{7,3},{8,4},{9,5},{1... | collective-permute-start | bytes 49160 | tf_op jit(solution)/shard_map/ppermute | solution.py:582
  23.5 1.4 %collective-permute-start.8 = (f32[32,128]{1,0:T(8,128)S(1)}, f32[32,128]{1,0:T(8,128)S(1)}, u32[]{:S(2)}, u32[]{:S(2)}) collective-permute-start(f32[32,128]{1,0:T(8,128)S(1)} %add.15), channel_id=1, source_target_pairs={{0,4},{4,0},{8,12},{12,8},{1,5},{5,1},{9,13},{13,9},{2,6},{6,2},{1... | collective-permute-start | bytes 49160 | tf_op jit(solution)/shard_map/ppermute | solution.py:475
  25.0 3.5 %collective-permute-start.11 = (f32[32,128]{1,0:T(8,128)S(1)}, f32[32,128]{1,0:T(8,128)S(1)}, u32[]{:S(2)}, u32[]{:S(2)}) collective-permute-start(f32[32,128]{1,0:T(8,128)S(1)} %add.16), channel_id=1, source_target_pairs={{0,4},{1,5},{2,6},{3,7},{4,16},{5,17},{6,18},{7,19},{8,12},{9,13},... | collective-permute-start | bytes 49160 | tf_op jit(solution)/shard_map/ppermute | solution.py:582
  26.0 2.5 %collective-permute-start.10 = (f32[32,128]{1,0:T(8,128)S(1)}, f32[32,128]{1,0:T(8,128)S(1)}, u32[]{:S(2)}, u32[]{:S(2)}) collective-permute-start(f32[32,128]{1,0:T(8,128)S(1)} %add.16), channel_id=1, source_target_pairs={{0,4},{4,0},{8,12},{12,8},{1,5},{5,1},{9,13},{13,9},{2,6},{6,2},{1... | collective-permute-start | bytes 49160 | tf_op jit(solution)/shard_map/ppermute | solution.py:475
  28.5 1.5 %collective-permute-start.13 = (f32[32,128]{1,0:T(8,128)S(1)}, f32[32,128]{1,0:T(8,128)S(1)}, u32[]{:S(2)}, u32[]{:S(2)}) collective-permute-start(f32[32,128]{1,0:T(8,128)S(1)} %add.17), channel_id=1, source_target_pairs={{0,5},{1,4},{2,7},{3,6},{4,0},{5,1},{6,2},{7,3},{8,13},{9,12},{10,... | collective-permute-start | bytes 49160 | tf_op jit(solution)/shard_map/ppermute | solution.py:582
  28.6 1.4 %collective-permute-start.12 = (f32[32,128]{1,0:T(8,128)S(1)}, f32[32,128]{1,0:T(8,128)S(1)}, u32[]{:S(2)}, u32[]{:S(2)}) collective-permute-start(f32[32,128]{1,0:T(8,128)S(1)} %add.17), channel_id=1, source_target_pairs={{0,4},{4,0},{8,12},{12,8},{1,5},{5,1},{9,13},{13,9},{2,6},{6,2},{1... | collective-permute-start | bytes 49160 | tf_op jit(solution)/shard_map/ppermute | solution.py:475
  30.0 4.1 %collective-permute-start.15 = (f32[32,128]{1,0:T(8,128)S(1)}, f32[32,128]{1,0:T(8,128)S(1)}, u32[]{:S(2)}, u32[]{:S(2)}) collective-permute-start(f32[32,128]{1,0:T(8,128)S(1)} %add.18), channel_id=1, source_target_pairs={{0,4},{1,5},{2,6},{3,7},{4,2},{5,3},{6,0},{7,1},{8,12},{9,13},{10,... | collective-permute-start | bytes 49160 | tf_op jit(solution)/shard_map/ppermute | solution.py:582
  31.0 3.1 %collective-permute-start.14 = (f32[32,128]{1,0:T(8,128)S(1)}, f32[32,128]{1,0:T(8,128)S(1)}, u32[]{:S(2)}, u32[]{:S(2)}) collective-permute-start(f32[32,128]{1,0:T(8,128)S(1)} %add.18), channel_id=1, source_target_pairs={{0,4},{4,0},{8,12},{12,8},{1,5},{5,1},{9,13},{13,9},{2,6},{6,2},{1... | collective-permute-start | bytes 49160 | tf_op jit(solution)/shard_map/ppermute | solution.py:475
  34.1 1.2 %collective-permute-start.16 = (f32[32,128]{1,0:T(8,128)S(1)}, f32[32,128]{1,0:T(8,128)S(1)}, u32[]{:S(2)}, u32[]{:S(2)}) collective-permute-start(f32[32,128]{1,0:T(8,128)S(1)} %add.19.gram_ref), channel_id=1, source_target_pairs={{0,4},{4,0},{8,12},{12,8},{1,5},{5,1},{9,13},{13,9},{2,6},{6,2},{1... | collective-permute-start | bytes 49160 | tf_op jit(solution)/shard_map/ppermute | solution.py:475

commit v11 on v10

--- a/solution.py
+++ b/solution.py
@@ -54,6 +54,7 @@
     start_ref,
     levels_ref,
     edges_ref,
+    half_ref,
     outer_ref,
     *refs,
 ):
@@ -96,6 +97,16 @@
                 for row in range(part_rows)
             )
             edges_ref[group] = packed if chunk == 0 else edges_ref[group] + packed
+    even_place = lax.axis_index("ly") % 2 == 0
+    lower = iota((tile, lanes), 1) % 4 < 2
+    for pair in range(parts // 2):
+        left, right = edges_ref[2 * pair], edges_ref[2 * pair + 1]
+        half_ref[pair] = jnp.where(
+            even_place,
+            jnp.where(lower, pltpu.roll(right, lanes - 2, 1), left),
+            jnp.where(lower, left, pltpu.roll(right, 2, 1)),
+        )
+    half_ref[parts // 2] = edges_ref[parts]
     for copy in copies[1 + chunks :]:
         copy.wait()
 
@@ -104,7 +115,9 @@
     from_left = iota((tile, lanes), 1) % 4 < 2
     even_place = lax.axis_index("ly") % 2 == 0
     for group in range(parts + 1):
-        near, far = near_ref[group], far_ref[group]
+        near, far = near_ref[group], far_ref[group // 2]
+        if group % 2:
+            far = jnp.where(even_place, pltpu.roll(far, lanes - 2, 1), pltpu.roll(far, 2, 1))
         beside_ref[group] = jnp.where(
             even_place, jnp.where(from_left, far, near), jnp.where(from_left, near, far)
         )
@@ -510,9 +523,9 @@
     order = (*sorted(range(1, parts), key=lambda k: (k in early, -k)), 0)
     flat = start.reshape(cols * rows, lanes)
     piece = (part_rows, cols, lanes)
-    start_here, levels_here, edges, outer, *raws = call(
+    start_here, levels_here, edges, half, outer, *raws = call(
         functools.partial(pack_kernel, *sizes, early),
-        [flat.shape, jax.ShapeDtypeStruct(levels.shape, levels.dtype), (parts + 1, tile, lanes), (2 * chunks + 1, tile, lanes)]
+        [flat.shape, jax.ShapeDtypeStruct(levels.shape, levels.dtype), (parts + 1, tile, lanes), (parts // 2 + 1, tile, lanes), (2 * chunks + 1, tile, lanes)]
         + [(cols, part_rows, lanes)] * len(early),
         pltpu.with_memory_space_constraint(flat, pltpu.HBM),
         pltpu.with_memory_space_constraint(levels, pltpu.HBM),
@@ -524,7 +537,7 @@
     count = lax.axis_size("ly")
     near = exchange(edges, "ly", 1)
     far_pairs = [(i, (i + 1) % count if i % 2 else (i - 1) % count) for i in range(count)]
-    far = lax.ppermute(edges, "ly", far_pairs)
+    far = lax.ppermute(half, "ly", far_pairs)
     raws = [exchange(values, "col", k) for k, values in zip(early, raws)]
     beside, outer = call(
         functools.partial(outer_kernel, parts),

time: 38 us -> 38.2 us (level)
  transfers between devices with their start and end apart: 17 -> 17, of which waited for: 9 -> 10; matrix products, arithmetic and copies ran while one was open for 0% -> 0% of each run, Pallas kernels for 5% -> 5%
where the time goes in v11:
time: 38.2 us; the launch traced here: 38.1 us
  starting transfers between devices  17.9 us (47%)
  waiting for transfers between devices  13.6 us (36%)
  Pallas kernels  6.39 us (17%)
    ppermute x11, starting transfers between devices, exchange(): return lax.ppermute(values, axis, [(i, i ^ distance) for i in range(count)])  10.8 us
    pallas_call x8, Pallas kernels, call(): pl.pallas_call(kernel, out_shape=[jax.ShapeDtypeStruct(shape, jnp.float32...  6.39 us
    ppermute x4, waiting for transfers between devices, shards(): gram = near + lax.ppermute(gram, axes, handover(holder, axis, bit))  6.33 us
    ppermute x11, waiting for transfers between devices, exchange(): return lax.ppermute(values, axis, [(i, i ^ distance) for i in range(count)])  6.13 us
    ppermute x4, starting transfers between devices, shards(): gram = near + lax.ppermute(gram, axes, handover(holder, axis, bit))  2.98 us
    ppermute x1, starting transfers between devices, shards(): far = lax.ppermute(half, 'ly', far_pairs)  2.64 us
    ppermute x1, starting transfers between devices, shards(): lax.ppermute(outer, 'lx', [(i, (i + 1) % count) for i in range(count)])  1.51 us
    ppermute x1, waiting for transfers between devices, shards(): lax.ppermute(outer, 'lx', [(i, (i + 1) % count) for i in range(count)])  1.16 us
  transfers between devices with their start and end apart: 17, of which 10 were waited for; matrix products, arithmetic and copies ran while one was open for 0% of the time, Pallas kernels for 5%

profile of v11, /device:TPU:0, one launch (start us, length us, event | category | flops | bytes accessed | tf_op | source)
XLA Modules:
  0.0 38.1 jit_solution(612650351132696113)
XLA Ops:
  0.0 1.4 %shard_map.28 = (f32[1024,128]{1,0:T(8,128)S(1)}, s32[64,128]{1,0:T(8,128)S(1)}, f32[5,8,128]{2,1,0:T(8,128)S(1)}, f32[3,8,128]{2,1,0:T(8,128)S(1)}, f32[5,8,128...) custom-call(f32[1024,128]{1,0:T(8,128)} %bitcast.4, s32[64,128]{1,0:T(8,128)} %levels_hbm.1, f32[16,64,128]{2,1,0:T(8,128)} %whole_hbm.1), custom_call_target="tpu_custom_call" | custom-call | tf_op jit(solution)/shard_map/pallas_call | solution.py:471
  1.4 0.5 %collective-permute-start = (f32[5,8,128]{2,1,0:T(8,128)S(1)}, f32[5,8,128]{2,1,0:T(8,128)S(1)}, u32[]{:S(2)}, u32[]{:S(2)}) collective-permute-start(f32[5,8,128]{2,1,0:T(8,128)S(1)} %get-tuple-element.27), channel_id=1, source_target_pairs={{0,4},{4,0},{8,12},{12,8},{1,5},{5,1},{9,13},{13,9},{2,6},{6,2},{1... | collective-permute-start | bytes 61448 | tf_op jit(solution)/shard_map/ppermute | solution.py:488
  2.0 2.6 %collective-permute-start.1 = (f32[3,8,128]{2,1,0:T(8,128)S(1)}, f32[3,8,128]{2,1,0:T(8,128)S(1)}, u32[]{:S(2)}, u32[]{:S(2)}) collective-permute-start(f32[3,8,128]{2,1,0:T(8,128)S(1)} %get-tuple-element.28), channel_id=1, source_target_pairs={{0,12},{4,8},{8,4},{12,0},{1,13},{5,9},{9,5},{13,1},{2,14},{6,10},... | collective-permute-start | bytes 36872 | tf_op jit(solution)/shard_map/ppermute | solution.py:540
  4.6 3.6 %collective-permute-start.6 = (f32[16,16,128]{2,1,0:T(8,128)S(1)}, f32[16,16,128]{2,1,0:T(8,128)S(1)}, u32[]{:S(2)}, u32[]{:S(2)}) collective-permute-start(f32[16,16,128]{2,1,0:T(8,128)S(1)} %get-tuple-element.38), channel_id=1, source_target_pairs={{0,3},{1,2},{2,1},{3,0},{4,7},{5,6},{6,5},{7,4},{8,11},{9,10},{10,... | collective-permute-start | bytes 393224 | tf_op jit(solution)/shard_map/ppermute | solution.py:488
  8.2 0.1 shard_map.29
  8.3 1.5 %collective-permute-start.2 = (f32[6,8,128]{2,1,0:T(8,128)S(1)}, f32[6,8,128]{2,1,0:T(8,128)S(1)}, u32[]{:S(2)}, u32[]{:S(2)}) collective-permute-start(f32[6,8,128]{2,1,0:T(8,128)S(1)} %get-tuple-element.33), channel_id=1, source_target_pairs={{0,16},{16,0},{1,17},{17,1},{2,18},{18,2},{3,19},{19,3},{4,20},{20... | collective-permute-start | bytes 73736 | tf_op jit(solution)/shard_map/ppermute | solution.py:550
  9.8 1.2 %shard_map.30 = (f32[64,16,128]{2,1,0:T(8,128)S(1)}, f32[2,16,128]{2,1,0:T(8,128)S(1)}, f32[1,8,128]{2,1,0:T(8,128)S(1)}) custom-call(f32[1024,128]{1,0:T(8,128)S(1)} %get-tuple-element.24.start_ref, s32[64,128]{1,0:T(8,128)S(1)} %get-tuple-element.25.levels_ref, f32[5,8,128]{2,1,0:T(8,128)S(1)} %get-tuple-element.29.beside_ref), custom_call_target="tpu_custom_call" | custom-call | flops 99999997952 | bytes 1000000000 | tf_op jit(solution)/shard_map/pallas_call | solution.py:471
  11.0 1.2 %collective-permute-done.2.before_ref.after_ref = f32[6,8,128]{2,1,0:T(8,128)S(1)} collective-permute-done((f32[6,8,128]{2,1,0:T(8,128)S(1)}, f32[6,8,128]{2,1,0:T(8,128)S(1)}, u32[]{:S(2)}, u32[]{:S(2)}) %collective-permute-start.2) | collective-permute-done | bytes 24608 | tf_op jit(solution)/shard_map/ppermute | solution.py:550
  12.1 0.2 shard_map.31
  12.4 0.6 %collective-permute-start.3 = (f32[16,16,128]{2,1,0:T(8,128)S(1)}, f32[16,16,128]{2,1,0:T(8,128)S(1)}, u32[]{:S(2)}, u32[]{:S(2)}) collective-permute-start(f32[16,16,128]{2,1,0:T(8,128)S(1)} %get-tuple-element.34), channel_id=1, source_target_pairs={{0,2},{1,3},{2,0},{3,1},{4,6},{5,7},{6,4},{7,5},{8,10},{9,11},{10,... | collective-permute-start | bytes 393224 | tf_op jit(solution)/shard_map/ppermute | solution.py:488
  13.0 1.6 %collective-permute-start.4 = (f32[16,16,128]{2,1,0:T(8,128)S(1)}, f32[16,16,128]{2,1,0:T(8,128)S(1)}, u32[]{:S(2)}, u32[]{:S(2)}) collective-permute-start(f32[16,16,128]{2,1,0:T(8,128)S(1)} %get-tuple-element.35), channel_id=1, source_target_pairs={{0,1},{1,0},{2,3},{3,2},{4,5},{5,4},{6,7},{7,6},{8,9},{9,8},{10,11... | collective-permute-start | bytes 393224 | tf_op jit(solution)/shard_map/ppermute | solution.py:488
  14.5 2.3 %collective-permute-start.5 = (f32[5,8,128]{2,1,0:T(8,128)S(1)}, f32[5,8,128]{2,1,0:T(8,128)S(1)}, u32[]{:S(2)}, u32[]{:S(2)}) collective-permute-start(f32[5,8,128]{2,1,0:T(8,128)S(1)} %get-tuple-element.36), channel_id=1, source_target_pairs={{0,3},{1,2},{2,1},{3,0},{4,7},{5,6},{6,5},{7,4},{8,11},{9,10},{10,... | collective-permute-start | bytes 61448 | tf_op jit(solution)/shard_map/ppermute | solution.py:488
  16.8 0.2 shard_map.32.refs_4_
  17.0 3.6 %collective-permute-done.5.refs_2_ = f32[5,8,128]{2,1,0:T(8,128)S(1)} collective-permute-done((f32[5,8,128]{2,1,0:T(8,128)S(1)}, f32[5,8,128]{2,1,0:T(8,128)S(1)}, u32[]{:S(2)}, u32[]{:S(2)}) %collective-permute-start.5) | collective-permute-done | bytes 20512 | tf_op jit(solution)/shard_map/ppermute | solution.py:488
  20.7 0.2 collective-permute-done.3.refs_0_
  20.9 0.1 collective-permute-done.4.refs_1_
  20.9 0.6 %shard_map.33 = (f32[16,64,128]{2,1,0:T(8,128)S(1)}, f32[32,128]{1,0:T(8,128)S(1)}) custom-call(f32[16,16,128]{2,1,0:T(8,128)S(1)} %collective-permute-done.3.refs_0_, f32[16,16,128]{2,1,0:T(8,128)S(1)} %collective-permute-done.4.refs_1_, f32[5,8,128]{2,1,0:T(8,128)S(1)} %collective-permute-done.5.refs_2_, f32[16,16,128]{2,1,0:T(8,128)S(1)} %get-tuple-element.37.refs_3_, ...), custom_call_target="tpu_custom_call" | custom-call | tf_op jit(solution)/shard_map/pallas_call | solution.py:471
  21.6 1.2 %collective-permute-done.7 = f32[32,128]{1,0:T(8,128)S(1)} collective-permute-done((f32[32,128]{1,0:T(8,128)S(1)}, f32[32,128]{1,0:T(8,128)S(1)}, u32[]{:S(2)}, u32[]{:S(2)}) %collective-permute-start.7) | collective-permute-done | bytes 16416 | tf_op jit(solution)/shard_map/ppermute | solution.py:488
  22.8 0.9 %collective-permute-start.9 = (f32[32,128]{1,0:T(8,128)S(1)}, f32[32,128]{1,0:T(8,128)S(1)}, u32[]{:S(2)}, u32[]{:S(2)}) collective-permute-start(f32[32,128]{1,0:T(8,128)S(1)} %add.15), channel_id=1, source_target_pairs={{0,12},{1,13},{2,14},{3,15},{4,0},{5,1},{6,2},{7,3},{8,4},{9,5},{1... | collective-permute-start | bytes 49160 | tf_op jit(solution)/shard_map/ppermute | solution.py:595
  23.7 1.4 %collective-permute-done.9 = f32[32,128]{1,0:T(8,128)S(1)} collective-permute-done((f32[32,128]{1,0:T(8,128)S(1)}, f32[32,128]{1,0:T(8,128)S(1)}, u32[]{:S(2)}, u32[]{:S(2)}) %collective-permute-start.9) | collective-permute-done | bytes 16416 | tf_op jit(solution)/shard_map/ppermute | solution.py:595
  25.2 1.0 %collective-permute-start.11 = (f32[32,128]{1,0:T(8,128)S(1)}, f32[32,128]{1,0:T(8,128)S(1)}, u32[]{:S(2)}, u32[]{:S(2)}) collective-permute-start(f32[32,128]{1,0:T(8,128)S(1)} %add.16), channel_id=1, source_target_pairs={{0,4},{1,5},{2,6},{3,7},{4,16},{5,17},{6,18},{7,19},{8,12},{9,13},... | collective-permute-start | bytes 49160 | tf_op jit(solution)/shard_map/ppermute | solution.py:595
  26.2 0.6 %collective-permute-start.10 = (f32[32,128]{1,0:T(8,128)S(1)}, f32[32,128]{1,0:T(8,128)S(1)}, u32[]{:S(2)}, u32[]{:S(2)}) collective-permute-start(f32[32,128]{1,0:T(8,128)S(1)} %add.16), channel_id=1, source_target_pairs={{0,4},{4,0},{8,12},{12,8},{1,5},{5,1},{9,13},{13,9},{2,6},{6,2},{1... | collective-permute-start | bytes 49160 | tf_op jit(solution)/shard_map/ppermute | solution.py:488
  26.8 1.9 %collective-permute-done.11 = f32[32,128]{1,0:T(8,128)S(1)} collective-permute-done((f32[32,128]{1,0:T(8,128)S(1)}, f32[32,128]{1,0:T(8,128)S(1)}, u32[]{:S(2)}, u32[]{:S(2)}) %collective-permute-start.11) | collective-permute-done | bytes 16416 | tf_op jit(solution)/shard_map/ppermute | solution.py:595
  28.8 0.5 %collective-permute-start.12 = (f32[32,128]{1,0:T(8,128)S(1)}, f32[32,128]{1,0:T(8,128)S(1)}, u32[]{:S(2)}, u32[]{:S(2)}) collective-permute-start(f32[32,128]{1,0:T(8,128)S(1)} %add.17), channel_id=1, source_target_pairs={{0,4},{4,0},{8,12},{12,8},{1,5},{5,1},{9,13},{13,9},{2,6},{6,2},{1... | collective-permute-start | bytes 49160 | tf_op jit(solution)/shard_map/ppermute | solution.py:488
  29.3 0.9 %collective-permute-done.13 = f32[32,128]{1,0:T(8,128)S(1)} collective-permute-done((f32[32,128]{1,0:T(8,128)S(1)}, f32[32,128]{1,0:T(8,128)S(1)}, u32[]{:S(2)}, u32[]{:S(2)}) %collective-permute-start.13) | collective-permute-done | bytes 16416 | tf_op jit(solution)/shard_map/ppermute | solution.py:595
  30.2 1.0 %collective-permute-start.15 = (f32[32,128]{1,0:T(8,128)S(1)}, f32[32,128]{1,0:T(8,128)S(1)}, u32[]{:S(2)}, u32[]{:S(2)}) collective-permute-start(f32[32,128]{1,0:T(8,128)S(1)} %add.18), channel_id=1, source_target_pairs={{0,4},{1,5},{2,6},{3,7},{4,2},{5,3},{6,0},{7,1},{8,12},{9,13},{10,... | collective-permute-start | bytes 49160 | tf_op jit(solution)/shard_map/ppermute | solution.py:595
  31.2 1.0 %collective-permute-start.14 = (f32[32,128]{1,0:T(8,128)S(1)}, f32[32,128]{1,0:T(8,128)S(1)}, u32[]{:S(2)}, u32[]{:S(2)}) collective-permute-start(f32[32,128]{1,0:T(8,128)S(1)} %add.18), channel_id=1, source_target_pairs={{0,4},{4,0},{8,12},{12,8},{1,5},{5,1},{9,13},{13,9},{2,6},{6,2},{1... | collective-permute-start | bytes 49160 | tf_op jit(solution)/shard_map/ppermute | solution.py:488
  32.2 2.0 %collective-permute-done.15 = f32[32,128]{1,0:T(8,128)S(1)} collective-permute-done((f32[32,128]{1,0:T(8,128)S(1)}, f32[32,128]{1,0:T(8,128)S(1)}, u32[]{:S(2)}, u32[]{:S(2)}) %collective-permute-start.15) | collective-permute-done | bytes 16416 | tf_op jit(solution)/shard_map/ppermute | solution.py:595
  34.3 0.1 collective-permute-start.16
  34.4 0.1 shard_map.34
  34.5 1.0 %collective-permute-done.16.other_ref = f32[32,128]{1,0:T(8,128)S(1)} collective-permute-done((f32[32,128]{1,0:T(8,128)S(1)}, f32[32,128]{1,0:T(8,128)S(1)}, u32[]{:S(2)}, u32[]{:S(2)}) %collective-permute-start.16) | collective-permute-done | bytes 16416 | tf_op jit(solution)/shard_map/ppermute | solution.py:488
  35.5 2.5 %shard_map.35 = f32[1024,128]{1,0:T(8,128)} custom-call(bf16[8,128,256]{2,1,0:T(8,128)(2,1)S(1)} %get-tuple-element.40.main_ref, bf16[8,128,256]{2,1,0:T(8,128)(2,1)S(1)} %get-tuple-element.41.rest_ref, f32[32,128]{1,0:T(8,128)S(1)} %add.19.gram_ref, f32[32,128]{1,0:T(8,128)S(1)} %collective-permute-done.16.other_ref), custom_call_target="tpu_custom_call" | custom-call | tf_op jit(solution)/shard_map/pallas_call | solution.py:471
  (15 shorter events, 0.1 us)
Async XLA Ops:
  1.4 6.8 %collective-permute-start = (f32[5,8,128]{2,1,0:T(8,128)S(1)}, f32[5,8,128]{2,1,0:T(8,128)S(1)}, u32[]{:S(2)}, u32[]{:S(2)}) collective-permute-start(f32[5,8,128]{2,1,0:T(8,128)S(1)} %get-tuple-element.27), channel_id=1, source_target_pairs={{0,4},{4,0},{8,12},{12,8},{1,5},{5,1},{9,13},{13,9},{2,6},{6,2},{1... | collective-permute-start | bytes 61448 | tf_op jit(solution)/shard_map/ppermute | solution.py:488
  2.0 6.2 %collective-permute-start.1 = (f32[3,8,128]{2,1,0:T(8,128)S(1)}, f32[3,8,128]{2,1,0:T(8,128)S(1)}, u32[]{:S(2)}, u32[]{:S(2)}) collective-permute-start(f32[3,8,128]{2,1,0:T(8,128)S(1)} %get-tuple-element.28), channel_id=1, source_target_pairs={{0,12},{4,8},{8,4},{12,0},{1,13},{5,9},{9,5},{13,1},{2,14},{6,10},... | collective-permute-start | bytes 36872 | tf_op jit(solution)/shard_map/ppermute | solution.py:540
  4.6 12.2 %collective-permute-start.6 = (f32[16,16,128]{2,1,0:T(8,128)S(1)}, f32[16,16,128]{2,1,0:T(8,128)S(1)}, u32[]{:S(2)}, u32[]{:S(2)}) collective-permute-start(f32[16,16,128]{2,1,0:T(8,128)S(1)} %get-tuple-element.38), channel_id=1, source_target_pairs={{0,3},{1,2},{2,1},{3,0},{4,7},{5,6},{6,5},{7,4},{8,11},{9,10},{10,... | collective-permute-start | bytes 393224 | tf_op jit(solution)/shard_map/ppermute | solution.py:488
  8.3 3.8 %collective-permute-start.2 = (f32[6,8,128]{2,1,0:T(8,128)S(1)}, f32[6,8,128]{2,1,0:T(8,128)S(1)}, u32[]{:S(2)}, u32[]{:S(2)}) collective-permute-start(f32[6,8,128]{2,1,0:T(8,128)S(1)} %get-tuple-element.33), channel_id=1, source_target_pairs={{0,16},{16,0},{1,17},{17,1},{2,18},{18,2},{3,19},{19,3},{4,20},{20... | collective-permute-start | bytes 73736 | tf_op jit(solution)/shard_map/ppermute | solution.py:550
  12.4 8.5 %collective-permute-start.3 = (f32[16,16,128]{2,1,0:T(8,128)S(1)}, f32[16,16,128]{2,1,0:T(8,128)S(1)}, u32[]{:S(2)}, u32[]{:S(2)}) collective-permute-start(f32[16,16,128]{2,1,0:T(8,128)S(1)} %get-tuple-element.34), channel_id=1, source_target_pairs={{0,2},{1,3},{2,0},{3,1},{4,6},{5,7},{6,4},{7,5},{8,10},{9,11},{10,... | collective-permute-start | bytes 393224 | tf_op jit(solution)/shard_map/ppermute | solution.py:488
  13.0 8.0 %collective-permute-start.4 = (f32[16,16,128]{2,1,0:T(8,128)S(1)}, f32[16,16,128]{2,1,0:T(8,128)S(1)}, u32[]{:S(2)}, u32[]{:S(2)}) collective-permute-start(f32[16,16,128]{2,1,0:T(8,128)S(1)} %get-tuple-element.35), channel_id=1, source_target_pairs={{0,1},{1,0},{2,3},{3,2},{4,5},{5,4},{6,7},{7,6},{8,9},{9,8},{10,11... | collective-permute-start | bytes 393224 | tf_op jit(solution)/shard_map/ppermute | solution.py:488
  14.5 6.1 %collective-permute-start.5 = (f32[5,8,128]{2,1,0:T(8,128)S(1)}, f32[5,8,128]{2,1,0:T(8,128)S(1)}, u32[]{:S(2)}, u32[]{:S(2)}) collective-permute-start(f32[5,8,128]{2,1,0:T(8,128)S(1)} %get-tuple-element.36), channel_id=1, source_target_pairs={{0,3},{1,2},{2,1},{3,0},{4,7},{5,6},{6,5},{7,4},{8,11},{9,10},{10,... | collective-permute-start | bytes 61448 | tf_op jit(solution)/shard_map/ppermute | solution.py:488
  21.6 1.2 %collective-permute-start.7 = (f32[32,128]{1,0:T(8,128)S(1)}, f32[32,128]{1,0:T(8,128)S(1)}, u32[]{:S(2)}, u32[]{:S(2)}) collective-permute-start(f32[32,128]{1,0:T(8,128)S(1)} %get-tuple-element.42), channel_id=1, source_target_pairs={{0,4},{4,0},{8,12},{12,8},{1,5},{5,1},{9,13},{13,9},{2,6},{6,2},{1... | collective-permute-start | bytes 49160 | tf_op jit(solution)/shard_map/ppermute | solution.py:488
  22.8 2.4 %collective-permute-start.9 = (f32[32,128]{1,0:T(8,128)S(1)}, f32[32,128]{1,0:T(8,128)S(1)}, u32[]{:S(2)}, u32[]{:S(2)}) collective-permute-start(f32[32,128]{1,0:T(8,128)S(1)} %add.15), channel_id=1, source_target_pairs={{0,12},{1,13},{2,14},{3,15},{4,0},{5,1},{6,2},{7,3},{8,4},{9,5},{1... | collective-permute-start | bytes 49160 | tf_op jit(solution)/shard_map/ppermute | solution.py:595
  23.7 1.4 %collective-permute-start.8 = (f32[32,128]{1,0:T(8,128)S(1)}, f32[32,128]{1,0:T(8,128)S(1)}, u32[]{:S(2)}, u32[]{:S(2)}) collective-permute-start(f32[32,128]{1,0:T(8,128)S(1)} %add.15), channel_id=1, source_target_pairs={{0,4},{4,0},{8,12},{12,8},{1,5},{5,1},{9,13},{13,9},{2,6},{6,2},{1... | collective-permute-start | bytes 49160 | tf_op jit(solution)/shard_map/ppermute | solution.py:488
  25.2 3.5 %collective-permute-start.11 = (f32[32,128]{1,0:T(8,128)S(1)}, f32[32,128]{1,0:T(8,128)S(1)}, u32[]{:S(2)}, u32[]{:S(2)}) collective-permute-start(f32[32,128]{1,0:T(8,128)S(1)} %add.16), channel_id=1, source_target_pairs={{0,4},{1,5},{2,6},{3,7},{4,16},{5,17},{6,18},{7,19},{8,12},{9,13},... | collective-permute-start | bytes 49160 | tf_op jit(solution)/shard_map/ppermute | solution.py:595
  26.2 2.5 %collective-permute-start.10 = (f32[32,128]{1,0:T(8,128)S(1)}, f32[32,128]{1,0:T(8,128)S(1)}, u32[]{:S(2)}, u32[]{:S(2)}) collective-permute-start(f32[32,128]{1,0:T(8,128)S(1)} %add.16), channel_id=1, source_target_pairs={{0,4},{4,0},{8,12},{12,8},{1,5},{5,1},{9,13},{13,9},{2,6},{6,2},{1... | collective-permute-start | bytes 49160 | tf_op jit(solution)/shard_map/ppermute | solution.py:488
  28.7 1.5 %collective-permute-start.13 = (f32[32,128]{1,0:T(8,128)S(1)}, f32[32,128]{1,0:T(8,128)S(1)}, u32[]{:S(2)}, u32[]{:S(2)}) collective-permute-start(f32[32,128]{1,0:T(8,128)S(1)} %add.17), channel_id=1, source_target_pairs={{0,5},{1,4},{2,7},{3,6},{4,0},{5,1},{6,2},{7,3},{8,13},{9,12},{10,... | collective-permute-start | bytes 49160 | tf_op jit(solution)/shard_map/ppermute | solution.py:595
  28.8 1.4 %collective-permute-start.12 = (f32[32,128]{1,0:T(8,128)S(1)}, f32[32,128]{1,0:T(8,128)S(1)}, u32[]{:S(2)}, u32[]{:S(2)}) collective-permute-start(f32[32,128]{1,0:T(8,128)S(1)} %add.17), channel_id=1, source_target_pairs={{0,4},{4,0},{8,12},{12,8},{1,5},{5,1},{9,13},{13,9},{2,6},{6,2},{1... | collective-permute-start | bytes 49160 | tf_op jit(solution)/shard_map/ppermute | solution.py:488
  30.2 4.1 %collective-permute-start.15 = (f32[32,128]{1,0:T(8,128)S(1)}, f32[32,128]{1,0:T(8,128)S(1)}, u32[]{:S(2)}, u32[]{:S(2)}) collective-permute-start(f32[32,128]{1,0:T(8,128)S(1)} %add.18), channel_id=1, source_target_pairs={{0,4},{1,5},{2,6},{3,7},{4,2},{5,3},{6,0},{7,1},{8,12},{9,13},{10,... | collective-permute-start | bytes 49160 | tf_op jit(solution)/shard_map/ppermute | solution.py:595
  31.2 3.1 %collective-permute-start.14 = (f32[32,128]{1,0:T(8,128)S(1)}, f32[32,128]{1,0:T(8,128)S(1)}, u32[]{:S(2)}, u32[]{:S(2)}) collective-permute-start(f32[32,128]{1,0:T(8,128)S(1)} %add.18), channel_id=1, source_target_pairs={{0,4},{4,0},{8,12},{12,8},{1,5},{5,1},{9,13},{13,9},{2,6},{6,2},{1... | collective-permute-start | bytes 49160 | tf_op jit(solution)/shard_map/ppermute | solution.py:488
  34.3 1.2 %collective-permute-start.16 = (f32[32,128]{1,0:T(8,128)S(1)}, f32[32,128]{1,0:T(8,128)S(1)}, u32[]{:S(2)}, u32[]{:S(2)}) collective-permute-start(f32[32,128]{1,0:T(8,128)S(1)} %add.19.gram_ref), channel_id=1, source_target_pairs={{0,4},{4,0},{8,12},{12,8},{1,5},{5,1},{9,13},{13,9},{2,6},{6,2},{1... | collective-permute-start | bytes 49160 | tf_op jit(solution)/shard_map/ppermute | solution.py:488
